TPU v7x, 768 devices: a whole 4x8x12 slice. The times are simulated.
768 devices in a mesh: section: 8 (over y), expert: 24 (over x_lo, z), dp: 4 (over x_hi, core).
Axes of the slice: x: 4 (x_hi: 2, x_lo: 2; x = x_hi * 2 + x_lo), y: 8, z: 12, core: 2. Of those that a mesh axis runs over, the one named last changes fastest.
Arguments:
- tokens_fwd: bfloat16 [8, 3072, 7168], P('section', 'expert', 'dp'), may hold values from -6 to 6
- routes_fwd: int32 [8, 3072, 1], P('section', 'expert'), may hold values from 0 to 5; in each aligned block of 128 rows (0 to 127, 128 to 255, ..., all dimensions but the last counted through in order) at most 22 rows name the same one
- gates_fwd: float32 [8, 3072, 1], P('section', 'expert'), may hold values from 0.2 to 1
- cotangent: bfloat16 [8, 3072, 7168], P('section', 'expert', 'dp'), may hold values from -6 to 6
- routes_bwd: int32 [8, 3072, 1], P('section', 'expert'), may hold values from 0 to 5; in each aligned block of 128 rows (0 to 127, 128 to 255, ..., all dimensions but the last counted through in order) at most 22 rows name the same one
- gates_bwd: float32 [8, 3072, 1], P('section', 'expert'), may hold values from 0.2 to 1
- saved_pre: bfloat16 [8, 528, 2, 6144], P('section', None, None, 'expert'), may hold values from -6 to 6
- w_gate: bfloat16 [8, 7168, 6144], P('section', 'dp', 'expert'), may hold values from -0.0625 to 0.0625
- w_up: bfloat16 [8, 7168, 6144], P('section', 'dp', 'expert'), may hold values from -0.0625 to 0.0625
- w_down: bfloat16 [8, 6144, 7168], P('section', 'expert', 'dp'), may hold values from -0.1875 to 0.1875
Outputs:
- forwarded: bfloat16 [8, 3072, 7168], P('section', 'expert', 'dp')
- returned: bfloat16 [8, 3072, 7168], P('section', 'expert', 'dp')
Inputs may be any that keep to these rules, and one draw needn't show every extreme that they name: `routes_fwd`: each token names 1 different experts; in each aligned block of 128 tokens (the tokens of one index of expert) no expert is named more than 22 times. `routes_bwd`: each token names 1 different experts; in each aligned block of 128 tokens (the tokens of one index of expert) no expert is named more than 22 times.
All inputs are finite; a program needn't handle non-finite values.
Results may differ from a plain program's by a relative error of at most 0.0065.
Values may be sent and summed in bfloat16 or wider, within the bound.
No kernel may reach another device: no remote copies, remote signals or barrier semaphores. Data moves between devices by JAX's collectives and lax.ppermute only.
A program may use at most 32 MiB of HBM per device.

v0:
```python
import jax
import jax.numpy as jnp
from jax import lax
from jax.sharding import PartitionSpec as P

GROUP = 4


def with_halo(cells, sides, width):
    for axis, dim in sides:
        count = lax.axis_size(axis)
        ends = count - 1
        head = lax.slice_in_dim(cells, 0, width, axis=dim)
        tail = lax.slice_in_dim(cells, cells.shape[dim] - width, cells.shape[dim], axis=dim)
        cells = jnp.concatenate(
            [
                lax.ppermute(tail, axis, [(i, (i + 1) % count) for i in range(ends)]),
                cells,
                lax.ppermute(head, axis, [((i + 1) % count, i) for i in range(ends)]),
            ],
            axis=dim,
        )
    return cells


def route_tables(routes, gate_values, experts, capacity):
    expert_ids = jnp.arange(experts, dtype=jnp.int32)
    matches = routes[:, :, None] == expert_ids[None, None, :]
    member = jnp.sum(matches.astype(jnp.int32), axis=1).T
    weighting = jnp.sum(
        jnp.where(matches, gate_values[:, :, None], jnp.zeros_like(gate_values[:, :, None])), axis=1
    ).T
    before = jnp.cumsum(member, axis=1) - member
    slot_ids = jnp.arange(capacity, dtype=jnp.int32)
    hit = (before[:, None, :] == slot_ids[None, :, None]).astype(jnp.int32)
    placing = (member[:, None, :] * hit).astype(jnp.float32)
    return (placing, weighting)


def contract_last(left_side, right_side):
    return lax.dot_general(
        left_side, right_side, (((1,), (1,)), ((), ())), preferred_element_type=jnp.float32
    )


def combine(arrived, placing, experts, capacity):
    per_expert = jnp.sum(
        arrived.reshape(experts, GROUP, capacity, arrived.shape[-1]).astype(jnp.float32), axis=1
    )
    return jnp.einsum("ecr,ecd->rd", placing, per_expert, precision=lax.Precision.HIGHEST)


def shards(
    tokens_fwd,
    routes_fwd,
    gates_fwd,
    cotangent,
    routes_bwd,
    gates_bwd,
    saved_pre,
    w_gate,
    w_up,
    w_down,
):
    expert_devices = lax.axis_size("expert")
    experts = expert_devices // GROUP
    slot_total = saved_pre.shape[1]
    capacity = slot_total // expert_devices
    tokens_here = tokens_fwd[0]
    quarter = tokens_here.shape[1]
    placing_fwd, weight_fwd = route_tables(routes_fwd[0], gates_fwd[0], experts, capacity)
    placing_bwd, weight_bwd = route_tables(routes_bwd[0], gates_bwd[0], experts, capacity)
    send_tokens = jnp.einsum(
        "ecr,rd->ecd",
        placing_fwd.astype(jnp.bfloat16),
        tokens_here,
        preferred_element_type=jnp.float32,
    ).astype(jnp.bfloat16)
    send_grads = jnp.einsum(
        "ecr,rd->ecd",
        placing_bwd * weight_bwd[:, None, :],
        cotangent[0].astype(jnp.float32),
        precision=lax.Precision.HIGHEST,
    ).astype(jnp.bfloat16)
    got_tokens, got_grads = (
        lax.all_to_all(
            jnp.repeat(send_tokens, GROUP, axis=0),
            "expert",
            split_axis=0,
            concat_axis=0,
            tiled=True,
        ),
        lax.all_to_all(
            jnp.repeat(send_grads, GROUP, axis=0), "expert", split_axis=0, concat_axis=0, tiled=True
        ),
    )
    flat_tokens = got_tokens.reshape(slot_total, quarter)
    gate_part = jnp.dot(flat_tokens, w_gate[0], preferred_element_type=jnp.float32)
    up_part = jnp.dot(flat_tokens, w_up[0], preferred_element_type=jnp.float32)
    gate_pre, up_pre = lax.psum((gate_part, up_part), "dp")
    hidden = (gate_pre * jax.nn.sigmoid(gate_pre) * up_pre).astype(jnp.bfloat16)
    out_part = (
        jnp.dot(hidden, w_down[0], preferred_element_type=jnp.float32)
        .astype(jnp.bfloat16)
        .reshape(expert_devices, capacity, quarter)
    )
    back_out = lax.all_to_all(out_part, "expert", split_axis=0, concat_axis=0, tiled=True)
    flat_grads = got_grads.reshape(slot_total, quarter)
    grad_hidden = lax.psum(contract_last(flat_grads, w_down[0]), "dp")
    pre_gate = saved_pre[0][:, 0, :].astype(jnp.float32)
    pre_up = saved_pre[0][:, 1, :].astype(jnp.float32)
    sigmoid_gate = jax.nn.sigmoid(pre_gate)
    grad_gate = (
        grad_hidden * pre_up * sigmoid_gate * (1.0 + pre_gate * (1.0 - sigmoid_gate))
    ).astype(jnp.bfloat16)
    grad_up = (grad_hidden * pre_gate * sigmoid_gate).astype(jnp.bfloat16)
    grad_out = (
        (contract_last(grad_gate, w_gate[0]) + contract_last(grad_up, w_up[0]))
        .astype(jnp.bfloat16)
        .reshape(expert_devices, capacity, quarter)
    )
    back_grad = lax.all_to_all(grad_out, "expert", split_axis=0, concat_axis=0, tiled=True)
    layer_out = combine(back_out, placing_fwd * weight_fwd[:, None, :], experts, capacity).astype(
        jnp.bfloat16
    )
    layer_grad = combine(back_grad, placing_bwd, experts, capacity).astype(jnp.bfloat16)
    stacked = jnp.stack([layer_grad, layer_out])
    extended = with_halo(stacked, (("section", 0),), 1)
    forwarded = extended[0][None]
    returned = extended[3][None]
    return (forwarded, returned)


def solution(mesh):
    return jax.shard_map(
        shards,
        mesh=mesh,
        in_specs=(
            P("section", "expert", "dp"),
            P("section", "expert", None),
            P("section", "expert", None),
            P("section", "expert", "dp"),
            P("section", "expert", None),
            P("section", "expert", None),
            P("section", None, None, "expert"),
            P("section", "dp", "expert"),
            P("section", "dp", "expert"),
            P("section", "expert", "dp"),
        ),
        out_specs=(P("section", "expert", "dp"), P("section", "expert", "dp")),
        check_vma=False,
    )
```

profile of v0, /device:TPU:26, one launch (start us, length us, event | category | flops | bytes accessed | tf_op | source)
XLA Modules:
  0.0 437.2 jit_solution(3774729596833952143)
XLA Ops:
  7.2 0.0 copy-start
  7.2 0.7 fusion.55
  7.9 0.3 reduce_window_sum.17
  8.2 0.7 fusion.56
  8.9 1.3 convolution_convert_fusion.2
  10.2 1.5 broadcast_in_dim.47
  11.7 0.0 copy-start.5
  11.7 0.0 copy-start.7
  11.7 16.8 %all-to-all-start = ((bf16[24,22,1792]{2,1,0:T(8,128)(2,1)}), bf16[24,22,1792]{2,1,0:T(8,128)(2,1)S(1)}, u32[]{:S(2)}, u32[]{:S(2)}) async-start(bf16[24,22,1792]{2,1,0:T(8,128)(2,1)} %bitcast.73), calls=%async_computation | async-start | bytes 4128768 | tf_op jit(solution)/shard_map/all_to_all | solution.py:86
  28.4 0.0 copy-done.5
  28.5 0.3 reduce_window_sum.18
  28.8 0.0 copy-done.7
  28.8 1.6 convolution_convert_fusion.1
  30.4 69.4 %all-to-all-done = bf16[24,22,1792]{2,1,0:T(8,128)(2,1)S(1)} async-done(((bf16[24,22,1792]{2,1,0:T(8,128)(2,1)}), bf16[24,22,1792]{2,1,0:T(8,128)(2,1)S(1)}, u32[]{:S(2)}, u32[]{:S(2)}) %all-to-all-start) | async-done | bytes 1892384 | tf_op jit(solution)/shard_map/all_to_all | solution.py:86
  99.8 1.4 broadcast_in_dim.50
  101.2 7.1 %all-to-all-start.2 = ((bf16[24,22,1792]{2,1,0:T(8,128)(2,1)}), bf16[24,22,1792]{2,1,0:T(8,128)(2,1)}, u32[]{:S(2)}, u32[]{:S(2)}) async-start(bf16[24,22,1792]{2,1,0:T(8,128)(2,1)} %bitcast.74), calls=%async_computation.2 | async-start | bytes 4128768 | tf_op jit(solution)/shard_map/all_to_all | solution.py:93
  108.4 0.0 all-reduce.3.cloned.1.call-start
  108.4 2.1 reshape.125
  110.5 0.0 copy-start.2
  110.5 0.0 copy-start.3
  110.5 3.4 fusion.8
  113.8 0.0 copy-done.2
  113.9 0.0 copy-done.3
  113.9 1.5 fusion.12
  115.3 62.2 %all-to-all-done.2 = bf16[24,22,1792]{2,1,0:T(8,128)(2,1)} async-done(((bf16[24,22,1792]{2,1,0:T(8,128)(2,1)}), bf16[24,22,1792]{2,1,0:T(8,128)(2,1)}, u32[]{:S(2)}, u32[]{:S(2)}) %all-to-all-start.2) | async-done | bytes 1892384 | tf_op jit(solution)/shard_map/all_to_all | solution.py:93
  177.6 2.6 reshape.128
  180.1 0.0 copy-done
  180.1 1.5 fusion.4
  181.6 0.0 all-reduce.3.cloned.1.call-update
  181.7 66.7 %all-reduce.3.cloned.1.call-done = (f32[528,256]{1,0:T(8,128)}, f32[528,256]{1,0:T(8,128)}, f32[528,256]{1,0:T(8,128)}) async-done(((f32[528,256]{1,0:T(8,128)}, f32[528,256]{1,0:T(8,128)}, f32[528,256]{1,0:T(8,128)}), (f32[528,256]{1,0:T(8,128)}, f32[528,256]{1,0:T(8,128)}, f32[528,256]{1,0:T(8,128)})) %all-reduce.3.cloned.1.call-update) | async-done | bytes 1622032 | tf_op jit(solution)/shard_map/psum | solution.py:100
  248.4 1.9 convolution_convert_fusion
  250.3 2.1 reshape.126
  252.4 0.0 copy-start.1
  252.4 11.8 %all-to-all-start.1 = ((bf16[24,22,1792]{2,1,0:T(8,128)(2,1)}), bf16[24,22,1792]{2,1,0:T(8,128)(2,1)S(1)}, u32[]{:S(2)}, u32[]{:S(2)}) async-start(bf16[24,22,1792]{2,1,0:T(8,128)(2,1)} %reshape.126), calls=%async_computation.1 | async-start | bytes 4128768 | tf_op jit(solution)/shard_map/all_to_all | solution.py:107
  264.2 1.1 copy.15
  265.4 0.0 copy-done.1
  265.4 0.0 copy-start.4
  265.4 2.1 fusion.10
  267.5 0.0 copy-done.4
  267.5 2.0 add_convert_fusion
  269.5 3.8 reshape.129
  273.3 0.0 copy-start.6
  273.3 0.0 copy-start.8
  273.3 62.7 %all-to-all-done.1 = bf16[24,22,1792]{2,1,0:T(8,128)(2,1)S(1)} async-done(((bf16[24,22,1792]{2,1,0:T(8,128)(2,1)}), bf16[24,22,1792]{2,1,0:T(8,128)(2,1)S(1)}, u32[]{:S(2)}, u32[]{:S(2)}) %all-to-all-start.1) | async-done | bytes 1892384 | tf_op jit(solution)/shard_map/all_to_all | solution.py:107
  336.1 7.1 %all-to-all-start.3 = ((bf16[24,22,1792]{2,1,0:T(8,128)(2,1)}), bf16[24,22,1792]{2,1,0:T(8,128)(2,1)}, u32[]{:S(2)}, u32[]{:S(2)}) async-start(bf16[24,22,1792]{2,1,0:T(8,128)(2,1)} %reshape.129), calls=%async_computation.3 | async-start | bytes 4128768 | tf_op jit(solution)/shard_map/all_to_all | solution.py:122
  343.2 0.0 copy-done.6
  343.2 0.0 copy-done.8
  343.2 0.3 convert_reduce_fusion.1
  343.5 1.0 fusion.3
  344.5 4.6 %collective-permute-start = (bf16[1,128,1792]{2,1,0:T(8,128)(2,1)S(1)}, bf16[1,128,1792]{2,1,0:T(8,128)(2,1)S(1)}, u32[]{:S(2)}, u32[]{:S(2)}) collective-permute-start(bf16[1,128,1792]{2,1,0:T(8,128)(2,1)S(1)} %fusion.3), channel_id=1, source_target_pairs={{0,96},{96,192},{192,288},{288,384},{384,480},{480,576},{576,672},... | collective-permute-start | bytes 1376264 | tf_op jit(solution)/shard_map/ppermute | solution.py:17
  349.1 63.5 %all-to-all-done.3 = bf16[24,22,1792]{2,1,0:T(8,128)(2,1)} async-done(((bf16[24,22,1792]{2,1,0:T(8,128)(2,1)}), bf16[24,22,1792]{2,1,0:T(8,128)(2,1)}, u32[]{:S(2)}, u32[]{:S(2)}) %all-to-all-start.3) | async-done | bytes 1892384 | tf_op jit(solution)/shard_map/all_to_all | solution.py:122
  412.6 2.1 convert_reduce_fusion
  414.7 1.0 fusion.2
  415.7 2.4 collective-permute-start.1
  418.1 0.0 collective-permute-done
  418.1 10.7 %collective-permute-done.1 = bf16[1,128,1792]{2,1,0:T(8,128)(2,1)S(1)} collective-permute-done((bf16[1,128,1792]{2,1,0:T(8,128)(2,1)S(1)}, bf16[1,128,1792]{2,1,0:T(8,128)(2,1)S(1)}, u32[]{:S(2)}, u32[]{:S(2)}) %collective-permute-start.1) | collective-permute-done | bytes 458784 | tf_op jit(solution)/shard_map/ppermute | solution.py:19
  428.8 0.8 copy.21
  429.6 0.8 copy.22
  (4 shorter events, 0.0 us)
Async XLA Ops:
  7.2 173.0 %copy-start = (bf16[1,256,1792]{2,1,0:T(8,128)(2,1)S(1)}, bf16[1,256,1792]{2,1,0:T(8,128)(2,1)}, u32[]{:S(2)}) copy-start(bf16[1,256,1792]{2,1,0:T(8,128)(2,1)} %param.19) | copy-start | bytes 2752516
  11.7 16.8 %copy-start.5 = (s32[1,128,1]{1,2,0:T(1,128)S(1)}, s32[1,128,1]{1,2,0:T(1,128)}, u32[]{:S(2)}) copy-start(s32[1,128,1]{1,2,0:T(1,128)} %param.14) | copy-start | bytes 1540
  11.7 17.1 %copy-start.7 = (f32[1,128,1]{1,2,0:T(1,128)S(1)}, f32[1,128,1]{1,2,0:T(1,128)}, u32[]{:S(2)}) copy-start(f32[1,128,1]{1,2,0:T(1,128)} %param.15) | copy-start | bytes 1540
  11.7 88.1 %all-to-all-start = ((bf16[24,22,1792]{2,1,0:T(8,128)(2,1)}), bf16[24,22,1792]{2,1,0:T(8,128)(2,1)S(1)}, u32[]{:S(2)}, u32[]{:S(2)}) async-start(bf16[24,22,1792]{2,1,0:T(8,128)(2,1)} %bitcast.73), calls=%async_computation | async-start | bytes 4128768 | tf_op jit(solution)/shard_map/all_to_all | solution.py:86
  101.2 76.3 %all-to-all-start.2 = ((bf16[24,22,1792]{2,1,0:T(8,128)(2,1)}), bf16[24,22,1792]{2,1,0:T(8,128)(2,1)}, u32[]{:S(2)}, u32[]{:S(2)}) async-start(bf16[24,22,1792]{2,1,0:T(8,128)(2,1)} %bitcast.74), calls=%async_computation.2 | async-start | bytes 4128768 | tf_op jit(solution)/shard_map/all_to_all | solution.py:93
  108.4 140.0 %all-reduce.3.cloned.1.call-start = ((), (), s32[]{:S(2)}) async-start(), calls=%async_computation.4 | async-start | bytes 3244032 | tf_op jit(solution)/shard_map/psum | solution.py:100
  110.5 3.4 copy-start.2
  110.5 3.4 copy-start.3
  252.4 13.0 %copy-start.1 = (f32[528,256]{1,0:T(8,128)S(1)}, f32[528,256]{1,0:T(8,128)}, u32[]{:S(2)}) copy-start(f32[528,256]{1,0:T(8,128)} %get-tuple-element.4) | copy-start | bytes 1622020
  252.4 83.6 %all-to-all-start.1 = ((bf16[24,22,1792]{2,1,0:T(8,128)(2,1)}), bf16[24,22,1792]{2,1,0:T(8,128)(2,1)S(1)}, u32[]{:S(2)}, u32[]{:S(2)}) async-start(bf16[24,22,1792]{2,1,0:T(8,128)(2,1)} %reshape.126), calls=%async_computation.1 | async-start | bytes 4128768 | tf_op jit(solution)/shard_map/all_to_all | solution.py:107
  265.4 2.1 copy-start.4
  273.3 69.9 %copy-start.6 = (s32[1,128,1]{1,2,0:T(1,128)S(1)}, s32[1,128,1]{1,2,0:T(1,128)}, u32[]{:S(2)}) copy-start(s32[1,128,1]{1,2,0:T(1,128)} %param.11) | copy-start | bytes 1540
  273.3 69.9 %copy-start.8 = (f32[1,128,1]{1,2,0:T(1,128)S(1)}, f32[1,128,1]{1,2,0:T(1,128)}, u32[]{:S(2)}) copy-start(f32[1,128,1]{1,2,0:T(1,128)} %param.12) | copy-start | bytes 1540
  336.1 76.6 %all-to-all-start.3 = ((bf16[24,22,1792]{2,1,0:T(8,128)(2,1)}), bf16[24,22,1792]{2,1,0:T(8,128)(2,1)}, u32[]{:S(2)}, u32[]{:S(2)}) async-start(bf16[24,22,1792]{2,1,0:T(8,128)(2,1)} %reshape.129), calls=%async_computation.3 | async-start | bytes 4128768 | tf_op jit(solution)/shard_map/all_to_all | solution.py:122
  344.5 73.6 %collective-permute-start = (bf16[1,128,1792]{2,1,0:T(8,128)(2,1)S(1)}, bf16[1,128,1792]{2,1,0:T(8,128)(2,1)S(1)}, u32[]{:S(2)}, u32[]{:S(2)}) collective-permute-start(bf16[1,128,1792]{2,1,0:T(8,128)(2,1)S(1)} %fusion.3), channel_id=1, source_target_pairs={{0,96},{96,192},{192,288},{288,384},{384,480},{480,576},{576,672},... | collective-permute-start | bytes 1376264 | tf_op jit(solution)/shard_map/ppermute | solution.py:17
  415.7 13.2 %collective-permute-start.1 = (bf16[1,128,1792]{2,1,0:T(8,128)(2,1)S(1)}, bf16[1,128,1792]{2,1,0:T(8,128)(2,1)S(1)}, u32[]{:S(2)}, u32[]{:S(2)}) collective-permute-start(bf16[1,128,1792]{2,1,0:T(8,128)(2,1)S(1)} %fusion.2), channel_id=1, source_target_pairs={{96,0},{192,96},{288,192},{384,288},{480,384},{576,480},{672,576},... | collective-permute-start | bytes 1376264 | tf_op jit(solution)/shard_map/ppermute | solution.py:19
Sparse Core Ops, SparseCore 0:
  181.8 66.5 all-reduce.2
where the time goes:
time: 438 us; the launch traced here: 437 us
  waiting for transfers between devices  335 us (76%)
  starting transfers between devices  49.9 us (11%)
  matrix products  17.2 us (4%)
  local copies, waits for them, and re-layouts  16.1 us (4%)
  between operations  14.2 us (3%)
    all_to_all x1, waiting for transfers between devices, shards(): lax.all_to_all(jnp.repeat(send_tokens, GROUP, axis=0), 'expert', split_ax...  69.4 us
    psum x1, waiting for transfers between devices, shards(): gate_pre, up_pre = lax.psum((gate_part, up_part), 'dp')  66.7 us
    all_to_all x1, waiting for transfers between devices, shards(): lax.all_to_all(grad_out, 'expert', split_axis=0, concat_axis=0, tiled=True)  63.5 us
    all_to_all x1, waiting for transfers between devices, shards(): lax.all_to_all(out_part, 'expert', split_axis=0, concat_axis=0, tiled=True)  62.7 us
    all_to_all x1, waiting for transfers between devices, shards(): lax.all_to_all(jnp.repeat(send_grads, GROUP, axis=0), 'expert', split_axi...  62.2 us
    all_to_all x1, starting transfers between devices, shards(): lax.all_to_all(jnp.repeat(send_tokens, GROUP, axis=0), 'expert', split_ax...  16.8 us
    all_to_all x1, starting transfers between devices, shards(): lax.all_to_all(out_part, 'expert', split_axis=0, concat_axis=0, tiled=True)  11.8 us
    ppermute x1, waiting for transfers between devices, with_halo(): lax.ppermute(head, axis, [((i + 1) % count, i) for i in range(ends)])  10.7 us
  transfers between devices with their start and end apart: 7, of which 6 were waited for; matrix products, arithmetic and copies ran while one was open for 5% of the time, Pallas kernels for 0%

commit v1 on v0

v1 whole, which is shorter than its diff:
```python
import jax
import jax.numpy as jnp
from jax import lax
from jax.sharding import Mesh
from jax.sharding import PartitionSpec as P

GROUP = 4
PAD = 8
RING = ("group", "member")
BF16 = jnp.bfloat16
F32 = jnp.float32


def hop(values, step):
    count = lax.axis_size(RING)
    return lax.ppermute(values, RING, [(i, (i + step) % count) for i in range(count)])


def swap(values, axis):
    return lax.ppermute(values, axis, [(0, 1), (1, 0)])


def placing_of(routes, capacity, width):
    groups = lax.axis_size("group")
    half, group = lax.axis_index("half"), lax.axis_index("group")
    near = [half * groups + (group + k) % groups for k in range(groups)]
    far = [(1 - half) * groups + (group + k) % groups for k in range(groups)]
    ids = jnp.stack(near + far).astype(jnp.int32)
    member = (routes[None, :, 0] == ids[:, None]).astype(jnp.int32)
    before = jnp.cumsum(member, axis=1) - member
    slot_ids = jnp.arange(width, dtype=jnp.int32)
    hit = (before[:, None, :] == slot_ids[None, :, None]) & (slot_ids < capacity)[None, :, None]
    placing = jnp.where(hit & (member[:, None, :] > 0), 1.0, 0.0).astype(BF16)
    return placing.reshape(-1, routes.shape[0])


def dispatch(slots):
    member = lax.axis_index("member")
    other = swap(slots[1], "half")
    blocks = jnp.concatenate([slots[0], other], axis=1)
    own = blocks[0]
    right = jnp.stack([blocks[0], blocks[1]])
    left = jnp.stack([blocks[0], blocks[2]])
    rights, lefts = {}, {}
    for step in range(1, 8):
        if step == 4:
            right, left = right[1], left[1]
        right, left = hop(right, 1), hop(left, -1)
        rights[step], lefts[step] = right, left
    out = [jnp.stack([own, lefts[4], rights[4]])]
    for s in range(1, GROUP):
        out.append(
            jnp.stack(
                [
                    jnp.where(member >= s, rights[s][0], lefts[4 - s][0]),
                    jnp.where(member >= s, lefts[4 - s][1], lefts[8 - s]),
                    jnp.where(member < s, rights[s][1], rights[s + 4]),
                ]
            )
        )
    return jnp.stack(out)


def collect(parts):
    member = lax.axis_index("member")
    width = parts.shape[2] // 2
    zero = jnp.zeros_like(parts[0, 0])

    def only(mask, values):
        return jnp.where(mask, values, zero)

    right = only(member >= 3, parts[3, 2])
    left = only(member < 1, parts[1, 1])
    for s in (2, 1):
        right = hop(right, -1) + only(member >= s, parts[s, 2])
        left = hop(left, 1) + only(member < 4 - s, parts[4 - s, 1])
    right = hop(right, -1) + parts[0, 2]
    left = hop(left, 1) + parts[0, 1]
    right = jnp.stack([only(member >= 3, parts[3, 0]), hop(right, -1) + only(member < 3, parts[3, 2])])
    left = jnp.stack([only(member < 1, parts[1, 0]), hop(left, 1) + only(member >= 1, parts[1, 1])])
    for s in (2, 1):
        right = hop(right, -1) + jnp.stack(
            [only(member >= s, parts[s, 0]), only(member < s, parts[s, 2])]
        )
        left = hop(left, 1) + jnp.stack(
            [only(member < 4 - s, parts[4 - s, 0]), only(member >= 4 - s, parts[4 - s, 1])]
        )
    right = hop(right, -1)
    left = hop(left, 1)
    blocks = jnp.stack([parts[0, 0] + right[0] + left[0], right[1], left[1]])
    mine, others = blocks[:, :width], blocks[:, width:]
    return jnp.stack([mine, swap(others, "half")])


def halves(values, axis):
    place = lax.axis_index(axis)
    half = values.shape[0] // 2
    low, high = values[:half], values[half:]
    return jnp.where(place == 0, low, high), jnp.where(place == 0, high, low)


def reduce_rows(values):
    for axis in ("core", "far"):
        kept, sent = halves(values, axis)
        values = kept + swap(sent.astype(BF16), axis).astype(F32)
    return values


def gather_rows(values):
    for axis in ("far", "core"):
        place = lax.axis_index(axis)
        other = swap(values, axis)
        values = jnp.concatenate(
            [jnp.where(place == 0, values, other), jnp.where(place == 0, other, values)]
        )
    return values


def contract_last(left_side, right_side):
    return lax.dot_general(
        left_side, right_side, (((1,), (1,)), ((), ())), preferred_element_type=F32
    )


def saved_quarter(saved, capacity, width):
    groups = lax.axis_size("group")
    half, group, member = (lax.axis_index(name) for name in ("half", "group", "member"))
    quarter = lax.axis_index("core") * 2 + lax.axis_index("far")
    source = (member - quarter) % GROUP
    blocks = saved.reshape(2, groups, GROUP, capacity, *saved.shape[1:])
    blocks = lax.dynamic_index_in_dim(blocks, source, axis=2, keepdims=False)
    rolled = [
        lax.dynamic_index_in_dim(blocks, (group + k) % groups, axis=1, keepdims=False)
        for k in range(groups)
    ]
    out = jnp.stack(rolled)
    out = jnp.where(half == 0, out, out[:, ::-1])
    out = jnp.pad(out, ((0, 0), (0, 0), (0, width - capacity), (0, 0), (0, 0)))
    return out.reshape(groups * 2 * width, *saved.shape[1:])


def shards(
    tokens_fwd,
    routes_fwd,
    gates_fwd,
    cotangent,
    routes_bwd,
    gates_bwd,
    saved_pre,
    w_gate,
    w_up,
    w_down,
):
    groups = lax.axis_size("group")
    devices = 2 * groups * GROUP
    capacity = saved_pre.shape[1] // devices
    width = -(-capacity // PAD) * PAD
    columns = tokens_fwd.shape[2]

    place_fwd = placing_of(routes_fwd[0], capacity, width)
    place_bwd = placing_of(routes_bwd[0], capacity, width)
    send_fwd = jnp.dot(place_fwd, tokens_fwd[0], preferred_element_type=F32).astype(BF16)
    scaled = (cotangent[0].astype(F32) * gates_bwd[0]).astype(BF16)
    send_bwd = jnp.dot(place_bwd, scaled, preferred_element_type=F32).astype(BF16)

    got_fwd = dispatch(send_fwd.reshape(2, groups, width, columns)).reshape(-1, columns)
    part = jnp.concatenate(
        [
            jnp.dot(got_fwd, w_gate[0], preferred_element_type=F32),
            jnp.dot(got_fwd, w_up[0], preferred_element_type=F32),
        ],
        axis=1,
    )
    got_bwd = dispatch(send_bwd.reshape(2, groups, width, columns)).reshape(-1, columns)
    summed = reduce_rows(part)
    hidden_width = w_gate.shape[2]
    gate_pre, up_pre = summed[:, :hidden_width], summed[:, hidden_width:]
    hidden = gather_rows((gate_pre * jax.nn.sigmoid(gate_pre) * up_pre).astype(BF16))
    out = jnp.dot(hidden, w_down[0], preferred_element_type=F32).astype(BF16)
    back_fwd = collect(out.reshape(GROUP, groups, 2 * width, columns)).reshape(-1, columns)

    grad_hidden = reduce_rows(contract_last(got_bwd, w_down[0]))
    saved = saved_quarter(saved_pre[0], capacity, width)
    pre_gate = saved[:, 0].astype(F32)
    pre_up = saved[:, 1].astype(F32)
    sigmoid_gate = jax.nn.sigmoid(pre_gate)
    grad_gate = grad_hidden * pre_up * sigmoid_gate * (1.0 + pre_gate * (1.0 - sigmoid_gate))
    grad_up = grad_hidden * pre_gate * sigmoid_gate
    grads = gather_rows(jnp.concatenate([grad_gate, grad_up], axis=1).astype(BF16))
    grad_out = (
        contract_last(grads[:, :hidden_width], w_gate[0])
        + contract_last(grads[:, hidden_width:], w_up[0])
    ).astype(BF16)
    back_bwd = collect(grad_out.reshape(GROUP, groups, 2 * width, columns)).reshape(-1, columns)

    def rows_of(placing, values):
        return lax.dot_general(
            placing, values, (((0,), (0,)), ((), ())), preferred_element_type=F32
        )

    layer_out = (rows_of(place_fwd, back_fwd) * gates_fwd[0]).astype(BF16)
    layer_grad = rows_of(place_bwd, back_bwd).astype(BF16)
    ends = lax.axis_size("section") - 1
    forwarded = lax.ppermute(layer_out, "section", [(i, i + 1) for i in range(ends)])
    returned = lax.ppermute(layer_grad, "section", [(i + 1, i) for i in range(ends)])
    return (forwarded[None], returned[None])


def solution(mesh):
    sections, expert_devices, quarters = (mesh.shape[name] for name in ("section", "expert", "dp"))
    fine = Mesh(
        mesh.devices.reshape(sections, 2, expert_devices // 2 // GROUP, GROUP, 2, quarters // 2),
        ("section", "half", "group", "member", "far", "core"),
    )
    expert, dp = ("half", "group", "member"), ("far", "core")
    return jax.shard_map(
        shards,
        mesh=fine,
        in_specs=(
            P("section", expert, dp),
            P("section", expert, None),
            P("section", expert, None),
            P("section", expert, dp),
            P("section", expert, None),
            P("section", expert, None),
            P("section", None, None, expert),
            P("section", dp, expert),
            P("section", dp, expert),
            P("section", expert, dp),
        ),
        out_specs=(P("section", expert, dp), P("section", expert, dp)),
        check_vma=False,
    )
```

time: 438 us -> 305 us (0.70)
  the two profiles are of different devices: /device:TPU:26 before, /device:TPU:32 now
where the time goes in v1:
time: 305 us; the launch traced here: 303 us
  starting transfers between devices  242 us (79%)
  waiting for transfers between devices  39.2 us (13%)
  other arithmetic  7.82 us (3%)
  matrix products  6.61 us (2%)
  local copies, waits for them, and re-layouts  4.84 us (2%)
    ppermute x56, starting transfers between devices, hop(): lax.ppermute(values, RING, [(i, (i + step) % count) for i in range(count)])  202 us
    ppermute x12, starting transfers between devices, swap(): return lax.ppermute(values, axis, [(0, 1), (1, 0)])  34.3 us
    ppermute x12, waiting for transfers between devices, swap(): return lax.ppermute(values, axis, [(0, 1), (1, 0)])  16.8 us
    ppermute x56, waiting for transfers between devices, hop(): lax.ppermute(values, RING, [(i, (i + step) % count) for i in range(count)])  13.3 us
  transfers between devices with their start and end apart: 70, of which 14 were waited for; matrix products, arithmetic and copies ran while one was open for 4% of the time, Pallas kernels for 0%

profile of v1, /device:TPU:32, one launch (start us, length us, event | category | flops | bytes accessed | tf_op | source)
XLA Modules:
  0.0 302.7 jit_solution(13250546238353846718)
XLA Ops:
  4.5 3.4 %collective-permute-start.35 = (bf16[3,24,1792]{2,1,0:T(8,128)(2,1)S(1)}, bf16[3,24,1792]{2,1,0:T(8,128)(2,1)S(1)}, u32[]{:S(2)}, u32[]{:S(2)}) collective-permute-start(bf16[3,24,1792]{2,1,0:T(8,128)(2,1)S(1)} %bitcast.329), channel_id=1, source_target_pairs={{0,48},{48,0},{1,49},{49,1},{2,50},{50,2},{3,51},{51,3},{4,52},{52... | collective-permute-start | bytes 774152 | tf_op jit(solution)/shard_map/ppermute | solution.py:20
  8.9 2.4 collective-permute-start
  12.4 3.1 %collective-permute-done.35 = bf16[3,24,1792]{2,1,0:T(8,128)(2,1)S(1)} collective-permute-done((bf16[3,24,1792]{2,1,0:T(8,128)(2,1)S(1)}, bf16[3,24,1792]{2,1,0:T(8,128)(2,1)S(1)}, u32[]{:S(2)}, u32[]{:S(2)}) %collective-permute-start.35) | collective-permute-done | bytes 258080 | tf_op jit(solution)/shard_map/ppermute | solution.py:20
  16.3 14.5 %collective-permute-start.36 = (bf16[2,48,1792]{2,1,0:T(8,128)(2,1)}, bf16[2,48,1792]{2,1,0:T(8,128)(2,1)S(1)}, u32[]{:S(2)}, u32[]{:S(2)}) collective-permute-start(bf16[2,48,1792]{2,1,0:T(8,128)(2,1)} %pad_maximum_fusion.12), channel_id=1, source_target_pairs={{0,44},{4,0},{8,4},{12,8},{16,12},{20,16},{24,20},{28,24},{32,28},... | collective-permute-start | bytes 1032200 | tf_op jit(solution)/shard_map/ppermute | solution.py:16
  30.8 1.9 collective-permute-start.40
  33.6 5.1 %collective-permute-start.1 = (bf16[2,48,1792]{2,1,0:T(8,128)(2,1)}, bf16[2,48,1792]{2,1,0:T(8,128)(2,1)S(1)}, u32[]{:S(2)}, u32[]{:S(2)}) collective-permute-start(bf16[2,48,1792]{2,1,0:T(8,128)(2,1)} %pad_maximum_fusion.9), channel_id=1, source_target_pairs={{0,44},{4,0},{8,4},{12,8},{16,12},{20,16},{24,20},{28,24},{32,28},... | collective-permute-start | bytes 1032200 | tf_op jit(solution)/shard_map/ppermute | solution.py:16
  38.8 1.9 collective-permute-start.5
  40.7 5.1 %collective-permute-start.37 = (bf16[2,48,1792]{2,1,0:T(8,128)(2,1)S(1)}, bf16[2,48,1792]{2,1,0:T(8,128)(2,1)S(1)}, u32[]{:S(2)}, u32[]{:S(2)}) collective-permute-start(bf16[2,48,1792]{2,1,0:T(8,128)(2,1)S(1)} %collective-permute-done.36), channel_id=1, source_target_pairs={{0,44},{4,0},{8,4},{12,8},{16,12},{20,16},{24,20},{28,24},{32,28},... | collective-permute-start | bytes 1032200 | tf_op jit(solution)/shard_map/ppermute | solution.py:16
  45.9 1.9 collective-permute-start.41
  47.8 5.1 %collective-permute-start.2 = (bf16[2,48,1792]{2,1,0:T(8,128)(2,1)S(1)}, bf16[2,48,1792]{2,1,0:T(8,128)(2,1)S(1)}, u32[]{:S(2)}, u32[]{:S(2)}) collective-permute-start(bf16[2,48,1792]{2,1,0:T(8,128)(2,1)S(1)} %collective-permute-done.1), channel_id=1, source_target_pairs={{0,44},{4,0},{8,4},{12,8},{16,12},{20,16},{24,20},{28,24},{32,28},... | collective-permute-start | bytes 1032200 | tf_op jit(solution)/shard_map/ppermute | solution.py:16
  53.1 1.9 collective-permute-start.6
  55.0 5.1 %collective-permute-start.38 = (bf16[2,48,1792]{2,1,0:T(8,128)(2,1)S(1)}, bf16[2,48,1792]{2,1,0:T(8,128)(2,1)S(1)}, u32[]{:S(2)}, u32[]{:S(2)}) collective-permute-start(bf16[2,48,1792]{2,1,0:T(8,128)(2,1)S(1)} %collective-permute-done.37), channel_id=1, source_target_pairs={{0,44},{4,0},{8,4},{12,8},{16,12},{20,16},{24,20},{28,24},{32,28},... | collective-permute-start | bytes 1032200 | tf_op jit(solution)/shard_map/ppermute | solution.py:16
  60.1 1.9 collective-permute-start.42
  62.1 5.1 %collective-permute-start.3 = (bf16[2,48,1792]{2,1,0:T(8,128)(2,1)S(1)}, bf16[2,48,1792]{2,1,0:T(8,128)(2,1)S(1)}, u32[]{:S(2)}, u32[]{:S(2)}) collective-permute-start(bf16[2,48,1792]{2,1,0:T(8,128)(2,1)S(1)} %collective-permute-done.2), channel_id=1, source_target_pairs={{0,44},{4,0},{8,4},{12,8},{16,12},{20,16},{24,20},{28,24},{32,28},... | collective-permute-start | bytes 1032200 | tf_op jit(solution)/shard_map/ppermute | solution.py:16
  67.3 1.9 collective-permute-start.7
  69.3 5.1 %collective-permute-start.39 = (bf16[48,1792]{1,0:T(8,128)(2,1)S(1)}, bf16[48,1792]{1,0:T(8,128)(2,1)S(1)}, u32[]{:S(2)}, u32[]{:S(2)}) collective-permute-start(bf16[48,1792]{1,0:T(8,128)(2,1)S(1)} %get-tuple-element.65), channel_id=1, source_target_pairs={{0,44},{4,0},{8,4},{12,8},{16,12},{20,16},{24,20},{28,24},{32,28},... | collective-permute-start | bytes 516104 | tf_op jit(solution)/shard_map/ppermute | solution.py:16
  74.5 1.9 collective-permute-start.43
  76.4 5.1 %collective-permute-start.4 = (bf16[48,1792]{1,0:T(8,128)(2,1)S(1)}, bf16[48,1792]{1,0:T(8,128)(2,1)S(1)}, u32[]{:S(2)}, u32[]{:S(2)}) collective-permute-start(bf16[48,1792]{1,0:T(8,128)(2,1)S(1)} %get-tuple-element.72), channel_id=1, source_target_pairs={{0,44},{4,0},{8,4},{12,8},{16,12},{20,16},{24,20},{28,24},{32,28},... | collective-permute-start | bytes 516104 | tf_op jit(solution)/shard_map/ppermute | solution.py:16
  83.6 5.1 %collective-permute-start.44 = (bf16[48,1792]{1,0:T(8,128)(2,1)S(1)}, bf16[48,1792]{1,0:T(8,128)(2,1)S(1)}, u32[]{:S(2)}, u32[]{:S(2)}) collective-permute-start(bf16[48,1792]{1,0:T(8,128)(2,1)S(1)} %collective-permute-done.39), channel_id=1, source_target_pairs={{0,44},{4,0},{8,4},{12,8},{16,12},{20,16},{24,20},{28,24},{32,28},... | collective-permute-start | bytes 516104 | tf_op jit(solution)/shard_map/ppermute | solution.py:16
  88.7 1.9 collective-permute-start.47
  90.7 5.1 %collective-permute-start.9 = (bf16[48,1792]{1,0:T(8,128)(2,1)S(1)}, bf16[48,1792]{1,0:T(8,128)(2,1)S(1)}, u32[]{:S(2)}, u32[]{:S(2)}) collective-permute-start(bf16[48,1792]{1,0:T(8,128)(2,1)S(1)} %collective-permute-done.4), channel_id=1, source_target_pairs={{0,44},{4,0},{8,4},{12,8},{16,12},{20,16},{24,20},{28,24},{32,28},... | collective-permute-start | bytes 516104 | tf_op jit(solution)/shard_map/ppermute | solution.py:16
  95.9 1.9 collective-permute-start.12
  97.9 5.1 %collective-permute-start.45 = (bf16[48,1792]{1,0:T(8,128)(2,1)S(1)}, bf16[48,1792]{1,0:T(8,128)(2,1)S(1)}, u32[]{:S(2)}, u32[]{:S(2)}) collective-permute-start(bf16[48,1792]{1,0:T(8,128)(2,1)S(1)} %collective-permute-done.44), channel_id=1, source_target_pairs={{0,44},{4,0},{8,4},{12,8},{16,12},{20,16},{24,20},{28,24},{32,28},... | collective-permute-start | bytes 516104 | tf_op jit(solution)/shard_map/ppermute | solution.py:16
  103.1 1.9 collective-permute-start.48
  106.3 1.9 collective-permute-start.13
  108.2 5.1 %collective-permute-start.10 = (bf16[48,1792]{1,0:T(8,128)(2,1)S(1)}, bf16[48,1792]{1,0:T(8,128)(2,1)S(1)}, u32[]{:S(2)}, u32[]{:S(2)}) collective-permute-start(bf16[48,1792]{1,0:T(8,128)(2,1)S(1)} %collective-permute-done.9), channel_id=1, source_target_pairs={{0,44},{4,0},{8,4},{12,8},{16,12},{20,16},{24,20},{28,24},{32,28},... | collective-permute-start | bytes 516104 | tf_op jit(solution)/shard_map/ppermute | solution.py:16
  113.4 2.7 collective-permute-start.46
  117.0 5.6 %collective-permute-start.11 = (bf16[48,1792]{1,0:T(8,128)(2,1)S(1)}, bf16[48,1792]{1,0:T(8,128)(2,1)S(1)}, u32[]{:S(2)}, u32[]{:S(2)}) collective-permute-start(bf16[48,1792]{1,0:T(8,128)(2,1)S(1)} %collective-permute-done.10), channel_id=1, source_target_pairs={{0,44},{4,0},{8,4},{12,8},{16,12},{20,16},{24,20},{28,24},{32,28},... | collective-permute-start | bytes 516104 | tf_op jit(solution)/shard_map/ppermute | solution.py:16
  126.8 4.3 %collective-permute-done.49 = bf16[48,1792]{1,0:T(8,128)(2,1)S(1)} collective-permute-done((bf16[48,1792]{1,0:T(8,128)(2,1)S(1)}, bf16[48,1792]{1,0:T(8,128)(2,1)S(1)}, u32[]{:S(2)}, u32[]{:S(2)}) %collective-permute-start.49) | collective-permute-done | bytes 172064 | tf_op jit(solution)/shard_map/ppermute | solution.py:16
  133.2 1.9 collective-permute-start.50
  137.6 5.0 %collective-permute-start.51 = (bf16[144,256]{1,0:T(8,128)(2,1)S(1)}, bf16[144,256]{1,0:T(8,128)(2,1)S(1)}, u32[]{:S(2)}, u32[]{:S(2)}) collective-permute-start(bf16[144,256]{1,0:T(8,128)(2,1)S(1)} %select_convert_fusion.3), channel_id=1, source_target_pairs={{0,2},{2,0},{1,3},{3,1},{4,6},{6,4},{5,7},{7,5},{8,10},{10,8},{9,1... | collective-permute-start | bytes 221192 | tf_op jit(solution)/shard_map/ppermute | solution.py:20
  142.7 2.1 collective-permute-start.15
  145.8 5.0 %collective-permute-start.52 = (bf16[144,512]{1,0:T(8,128)(2,1)S(1)}, bf16[144,512]{1,0:T(8,128)(2,1)S(1)}, u32[]{:S(2)}, u32[]{:S(2)}) collective-permute-start(bf16[144,512]{1,0:T(8,128)(2,1)S(1)} %pad_maximum_fusion.20), channel_id=1, source_target_pairs={{0,2},{2,0},{1,3},{3,1},{4,6},{6,4},{5,7},{7,5},{8,10},{10,8},{9,1... | collective-permute-start | bytes 442376 | tf_op jit(solution)/shard_map/ppermute | solution.py:20
  150.9 2.4 collective-permute-start.16
  154.7 4.8 %collective-permute-done.16 = bf16[144,512]{1,0:T(8,128)(2,1)S(1)} collective-permute-done((bf16[144,512]{1,0:T(8,128)(2,1)S(1)}, bf16[144,512]{1,0:T(8,128)(2,1)S(1)}, u32[]{:S(2)}, u32[]{:S(2)}) %collective-permute-start.16) | collective-permute-done | bytes 147488 | tf_op jit(solution)/shard_map/ppermute | solution.py:20
  159.6 3.3 %collective-permute-start.17 = (bf16[144,256]{1,0:T(8,128)(2,1)S(1)}, bf16[144,256]{1,0:T(8,128)(2,1)S(1)}, u32[]{:S(2)}, u32[]{:S(2)}) collective-permute-start(bf16[144,256]{1,0:T(8,128)(2,1)S(1)} %fusion.58), channel_id=1, source_target_pairs={{0,2},{2,0},{1,3},{3,1},{4,6},{6,4},{5,7},{7,5},{8,10},{10,8},{9,1... | collective-permute-start | bytes 221192 | tf_op jit(solution)/shard_map/ppermute | solution.py:20
  164.9 2.5 collective-permute-done.17
  173.1 3.9 %collective-permute-start.61 = (bf16[48,1792]{1,0:T(8,128)(2,1)S(1)}, bf16[48,1792]{1,0:T(8,128)(2,1)S(1)}, u32[]{:S(2)}, u32[]{:S(2)}) collective-permute-start(bf16[48,1792]{1,0:T(8,128)(2,1)S(1)} %get-tuple-element.10), channel_id=1, source_target_pairs={{0,4},{4,8},{8,12},{12,16},{16,20},{20,24},{24,28},{28,32},{32,36}... | collective-permute-start | bytes 516104 | tf_op jit(solution)/shard_map/ppermute | solution.py:16
  177.9 3.1 %collective-permute-start.19 = (bf16[48,1792]{1,0:T(8,128)(2,1)S(1)}, bf16[48,1792]{1,0:T(8,128)(2,1)S(1)}, u32[]{:S(2)}, u32[]{:S(2)}) collective-permute-start(bf16[48,1792]{1,0:T(8,128)(2,1)S(1)} %get-tuple-element.32), channel_id=1, source_target_pairs={{0,44},{4,0},{8,4},{12,8},{16,12},{20,16},{24,20},{28,24},{32,28},... | collective-permute-start | bytes 516104 | tf_op jit(solution)/shard_map/ppermute | solution.py:16
  181.1 2.7 collective-permute-start.26
  183.9 4.3 %collective-permute-start.55 = (bf16[48,1792]{1,0:T(8,128)(2,1)S(1)}, bf16[48,1792]{1,0:T(8,128)(2,1)S(1)}, u32[]{:S(2)}, u32[]{:S(2)}) collective-permute-start(bf16[48,1792]{1,0:T(8,128)(2,1)S(1)} %get-tuple-element.20), channel_id=1, source_target_pairs={{0,44},{4,0},{8,4},{12,8},{16,12},{20,16},{24,20},{28,24},{32,28},... | collective-permute-start | bytes 516104 | tf_op jit(solution)/shard_map/ppermute | solution.py:16
  190.4 4.9 %collective-permute-start.20 = (bf16[48,1792]{1,0:T(8,128)(2,1)S(1)}, bf16[48,1792]{1,0:T(8,128)(2,1)S(1)}, u32[]{:S(2)}, u32[]{:S(2)}) collective-permute-start(bf16[48,1792]{1,0:T(8,128)(2,1)S(1)} %get-tuple-element.40), channel_id=1, source_target_pairs={{0,44},{4,0},{8,4},{12,8},{16,12},{20,16},{24,20},{28,24},{32,28},... | collective-permute-start | bytes 516104 | tf_op jit(solution)/shard_map/ppermute | solution.py:16
  197.3 5.1 %collective-permute-start.56 = (bf16[48,1792]{1,0:T(8,128)(2,1)S(1)}, bf16[48,1792]{1,0:T(8,128)(2,1)S(1)}, u32[]{:S(2)}, u32[]{:S(2)}) collective-permute-start(bf16[48,1792]{1,0:T(8,128)(2,1)S(1)} %get-tuple-element.18), channel_id=1, source_target_pairs={{0,44},{4,0},{8,4},{12,8},{16,12},{20,16},{24,20},{28,24},{32,28},... | collective-permute-start | bytes 516104 | tf_op jit(solution)/shard_map/ppermute | solution.py:16
  202.5 2.1 collective-permute-start.63
  204.7 5.1 %collective-permute-start.21 = (bf16[48,1792]{1,0:T(8,128)(2,1)S(1)}, bf16[48,1792]{1,0:T(8,128)(2,1)S(1)}, u32[]{:S(2)}, u32[]{:S(2)}) collective-permute-start(bf16[48,1792]{1,0:T(8,128)(2,1)S(1)} %get-tuple-element.38), channel_id=1, source_target_pairs={{0,44},{4,0},{8,4},{12,8},{16,12},{20,16},{24,20},{28,24},{32,28},... | collective-permute-start | bytes 516104 | tf_op jit(solution)/shard_map/ppermute | solution.py:16
  211.8 5.1 %collective-permute-start.57 = (bf16[48,1792]{1,0:T(8,128)(2,1)S(1)}, bf16[48,1792]{1,0:T(8,128)(2,1)S(1)}, u32[]{:S(2)}, u32[]{:S(2)}) collective-permute-start(bf16[48,1792]{1,0:T(8,128)(2,1)S(1)} %get-tuple-element.16), channel_id=1, source_target_pairs={{0,44},{4,0},{8,4},{12,8},{16,12},{20,16},{24,20},{28,24},{32,28},... | collective-permute-start | bytes 516104 | tf_op jit(solution)/shard_map/ppermute | solution.py:16
  216.9 1.9 collective-permute-start.64
  218.9 5.1 %collective-permute-start.22 = (bf16[48,1792]{1,0:T(8,128)(2,1)S(1)}, bf16[48,1792]{1,0:T(8,128)(2,1)S(1)}, u32[]{:S(2)}, u32[]{:S(2)}) collective-permute-start(bf16[48,1792]{1,0:T(8,128)(2,1)S(1)} %get-tuple-element.36), channel_id=1, source_target_pairs={{0,44},{4,0},{8,4},{12,8},{16,12},{20,16},{24,20},{28,24},{32,28},... | collective-permute-start | bytes 516104 | tf_op jit(solution)/shard_map/ppermute | solution.py:16
  226.1 5.1 %collective-permute-start.58 = (bf16[2,48,1792]{2,1,0:T(8,128)(2,1)S(1)}, bf16[2,48,1792]{2,1,0:T(8,128)(2,1)S(1)}, u32[]{:S(2)}, u32[]{:S(2)}) collective-permute-start(bf16[2,48,1792]{2,1,0:T(8,128)(2,1)S(1)} %pad_maximum_fusion.13), channel_id=1, source_target_pairs={{0,44},{4,0},{8,4},{12,8},{16,12},{20,16},{24,20},{28,24},{32,28},... | collective-permute-start | bytes 1032200 | tf_op jit(solution)/shard_map/ppermute | solution.py:16
  233.3 5.1 %collective-permute-start.23 = (bf16[2,48,1792]{2,1,0:T(8,128)(2,1)S(1)}, bf16[2,48,1792]{2,1,0:T(8,128)(2,1)S(1)}, u32[]{:S(2)}, u32[]{:S(2)}) collective-permute-start(bf16[2,48,1792]{2,1,0:T(8,128)(2,1)S(1)} %pad_maximum_fusion.10), channel_id=1, source_target_pairs={{0,44},{4,0},{8,4},{12,8},{16,12},{20,16},{24,20},{28,24},{32,28},... | collective-permute-start | bytes 1032200 | tf_op jit(solution)/shard_map/ppermute | solution.py:16
  238.5 1.9 collective-permute-start.30
  240.5 5.1 %collective-permute-start.59 = (bf16[2,48,1792]{2,1,0:T(8,128)(2,1)S(1)}, bf16[2,48,1792]{2,1,0:T(8,128)(2,1)S(1)}, u32[]{:S(2)}, u32[]{:S(2)}) collective-permute-start(bf16[2,48,1792]{2,1,0:T(8,128)(2,1)S(1)} %maximum_add_fusion.4), channel_id=1, source_target_pairs={{0,44},{4,0},{8,4},{12,8},{16,12},{20,16},{24,20},{28,24},{32,28},... | collective-permute-start | bytes 1032200 | tf_op jit(solution)/shard_map/ppermute | solution.py:16
  247.7 5.1 %collective-permute-start.24 = (bf16[2,48,1792]{2,1,0:T(8,128)(2,1)S(1)}, bf16[2,48,1792]{2,1,0:T(8,128)(2,1)S(1)}, u32[]{:S(2)}, u32[]{:S(2)}) collective-permute-start(bf16[2,48,1792]{2,1,0:T(8,128)(2,1)S(1)} %maximum_add_fusion), channel_id=1, source_target_pairs={{0,44},{4,0},{8,4},{12,8},{16,12},{20,16},{24,20},{28,24},{32,28},... | collective-permute-start | bytes 1032200 | tf_op jit(solution)/shard_map/ppermute | solution.py:16
  252.9 1.9 collective-permute-start.31
  254.9 5.1 %collective-permute-start.60 = (bf16[2,48,1792]{2,1,0:T(8,128)(2,1)S(1)}, bf16[2,48,1792]{2,1,0:T(8,128)(2,1)S(1)}, u32[]{:S(2)}, u32[]{:S(2)}) collective-permute-start(bf16[2,48,1792]{2,1,0:T(8,128)(2,1)S(1)} %maximum_add_fusion.5), channel_id=1, source_target_pairs={{0,44},{4,0},{8,4},{12,8},{16,12},{20,16},{24,20},{28,24},{32,28},... | collective-permute-start | bytes 1032200 | tf_op jit(solution)/shard_map/ppermute | solution.py:16
  262.1 5.1 %collective-permute-start.25 = (bf16[2,48,1792]{2,1,0:T(8,128)(2,1)S(1)}, bf16[2,48,1792]{2,1,0:T(8,128)(2,1)S(1)}, u32[]{:S(2)}, u32[]{:S(2)}) collective-permute-start(bf16[2,48,1792]{2,1,0:T(8,128)(2,1)S(1)} %maximum_add_fusion.1), channel_id=1, source_target_pairs={{0,44},{4,0},{8,4},{12,8},{16,12},{20,16},{24,20},{28,24},{32,28},... | collective-permute-start | bytes 1032200 | tf_op jit(solution)/shard_map/ppermute | solution.py:16
  269.3 5.3 %collective-permute-done.67 = bf16[2,48,1792]{2,1,0:T(8,128)(2,1)S(1)} collective-permute-done((bf16[2,48,1792]{2,1,0:T(8,128)(2,1)S(1)}, bf16[2,48,1792]{2,1,0:T(8,128)(2,1)S(1)}, u32[]{:S(2)}, u32[]{:S(2)}) %collective-permute-start.67) | collective-permute-done | bytes 344096 | tf_op jit(solution)/shard_map/ppermute | solution.py:16
  274.7 2.5 collective-permute-start.68
  278.7 2.5 collective-permute-start.33
  281.2 4.2 %collective-permute-done.68 = bf16[3,24,1792]{2,1,0:T(8,128)(2,1)S(1)} collective-permute-done((bf16[3,24,1792]{2,1,0:T(8,128)(2,1)S(1)}, bf16[3,24,1792]{2,1,0:T(8,128)(2,1)S(1)}, u32[]{:S(2)}, u32[]{:S(2)}) %collective-permute-start.68) | collective-permute-done | bytes 258080 | tf_op jit(solution)/shard_map/ppermute | solution.py:20
  285.8 2.4 collective-permute-start.69
  288.6 3.5 %collective-permute-start.34 = (bf16[128,1792]{1,0:T(8,128)(2,1)S(1)}, bf16[128,1792]{1,0:T(8,128)(2,1)S(1)}, u32[]{:S(2)}, u32[]{:S(2)}) collective-permute-start(bf16[128,1792]{1,0:T(8,128)(2,1)S(1)} %fusion), channel_id=1, source_target_pairs={{0,96},{96,192},{192,288},{288,384},{384,480},{480,576},{576,672},... | collective-permute-start | bytes 1376264 | tf_op jit(solution)/shard_map/ppermute | solution.py:204
  292.1 4.1 %collective-permute-done.69 = bf16[128,1792]{1,0:T(8,128)(2,1)S(1)} collective-permute-done((bf16[128,1792]{1,0:T(8,128)(2,1)S(1)}, bf16[128,1792]{1,0:T(8,128)(2,1)S(1)}, u32[]{:S(2)}, u32[]{:S(2)}) %collective-permute-start.69) | collective-permute-done | bytes 458784 | tf_op jit(solution)/shard_map/ppermute | solution.py:205
  296.2 4.9 %collective-permute-done.34 = bf16[128,1792]{1,0:T(8,128)(2,1)S(1)} collective-permute-done((bf16[128,1792]{1,0:T(8,128)(2,1)S(1)}, bf16[128,1792]{1,0:T(8,128)(2,1)S(1)}, u32[]{:S(2)}, u32[]{:S(2)}) %collective-permute-start.34) | collective-permute-done | bytes 458784 | tf_op jit(solution)/shard_map/ppermute | solution.py:204
  (195 shorter events, 52.1 us)
Async XLA Ops:
  4.5 11.0 %collective-permute-start.35 = (bf16[3,24,1792]{2,1,0:T(8,128)(2,1)S(1)}, bf16[3,24,1792]{2,1,0:T(8,128)(2,1)S(1)}, u32[]{:S(2)}, u32[]{:S(2)}) collective-permute-start(bf16[3,24,1792]{2,1,0:T(8,128)(2,1)S(1)} %bitcast.329), channel_id=1, source_target_pairs={{0,48},{48,0},{1,49},{49,1},{2,50},{50,2},{3,51},{51,3},{4,52},{52... | collective-permute-start | bytes 774152 | tf_op jit(solution)/shard_map/ppermute | solution.py:20
  8.9 23.8 %collective-permute-start = (bf16[3,24,1792]{2,1,0:T(8,128)(2,1)}, bf16[3,24,1792]{2,1,0:T(8,128)(2,1)S(1)}, u32[]{:S(2)}, u32[]{:S(2)}) collective-permute-start(bf16[3,24,1792]{2,1,0:T(8,128)(2,1)} %bitcast.10), channel_id=1, source_target_pairs={{0,48},{48,0},{1,49},{49,1},{2,50},{50,2},{3,51},{51,3},{4,52},{52... | collective-permute-start | bytes 774152 | tf_op jit(solution)/shard_map/ppermute | solution.py:20
  16.3 24.4 %collective-permute-start.36 = (bf16[2,48,1792]{2,1,0:T(8,128)(2,1)}, bf16[2,48,1792]{2,1,0:T(8,128)(2,1)S(1)}, u32[]{:S(2)}, u32[]{:S(2)}) collective-permute-start(bf16[2,48,1792]{2,1,0:T(8,128)(2,1)} %pad_maximum_fusion.12), channel_id=1, source_target_pairs={{0,44},{4,0},{8,4},{12,8},{16,12},{20,16},{24,20},{28,24},{32,28},... | collective-permute-start | bytes 1032200 | tf_op jit(solution)/shard_map/ppermute | solution.py:16
  30.8 15.0 %collective-permute-start.40 = (bf16[2,48,1792]{2,1,0:T(8,128)(2,1)S(1)}, bf16[2,48,1792]{2,1,0:T(8,128)(2,1)S(1)}, u32[]{:S(2)}, u32[]{:S(2)}) collective-permute-start(bf16[2,48,1792]{2,1,0:T(8,128)(2,1)S(1)} %pad_maximum_fusion.7), channel_id=1, source_target_pairs={{0,4},{4,8},{8,12},{12,16},{16,20},{20,24},{24,28},{28,32},{32,36}... | collective-permute-start | bytes 1032200 | tf_op jit(solution)/shard_map/ppermute | solution.py:16
  33.6 14.3 %collective-permute-start.1 = (bf16[2,48,1792]{2,1,0:T(8,128)(2,1)}, bf16[2,48,1792]{2,1,0:T(8,128)(2,1)S(1)}, u32[]{:S(2)}, u32[]{:S(2)}) collective-permute-start(bf16[2,48,1792]{2,1,0:T(8,128)(2,1)} %pad_maximum_fusion.9), channel_id=1, source_target_pairs={{0,44},{4,0},{8,4},{12,8},{16,12},{20,16},{24,20},{28,24},{32,28},... | collective-permute-start | bytes 1032200 | tf_op jit(solution)/shard_map/ppermute | solution.py:16
  38.8 14.3 %collective-permute-start.5 = (bf16[2,48,1792]{2,1,0:T(8,128)(2,1)S(1)}, bf16[2,48,1792]{2,1,0:T(8,128)(2,1)S(1)}, u32[]{:S(2)}, u32[]{:S(2)}) collective-permute-start(bf16[2,48,1792]{2,1,0:T(8,128)(2,1)S(1)} %pad_maximum_fusion.8), channel_id=1, source_target_pairs={{0,4},{4,8},{8,12},{12,16},{16,20},{20,24},{24,28},{28,32},{32,36}... | collective-permute-start | bytes 1032200 | tf_op jit(solution)/shard_map/ppermute | solution.py:16
  40.7 14.3 %collective-permute-start.37 = (bf16[2,48,1792]{2,1,0:T(8,128)(2,1)S(1)}, bf16[2,48,1792]{2,1,0:T(8,128)(2,1)S(1)}, u32[]{:S(2)}, u32[]{:S(2)}) collective-permute-start(bf16[2,48,1792]{2,1,0:T(8,128)(2,1)S(1)} %collective-permute-done.36), channel_id=1, source_target_pairs={{0,44},{4,0},{8,4},{12,8},{16,12},{20,16},{24,20},{28,24},{32,28},... | collective-permute-start | bytes 1032200 | tf_op jit(solution)/shard_map/ppermute | solution.py:16
  45.9 14.3 %collective-permute-start.41 = (bf16[2,48,1792]{2,1,0:T(8,128)(2,1)S(1)}, bf16[2,48,1792]{2,1,0:T(8,128)(2,1)S(1)}, u32[]{:S(2)}, u32[]{:S(2)}) collective-permute-start(bf16[2,48,1792]{2,1,0:T(8,128)(2,1)S(1)} %collective-permute-done.40), channel_id=1, source_target_pairs={{0,4},{4,8},{8,12},{12,16},{16,20},{20,24},{24,28},{28,32},{32,36}... | collective-permute-start | bytes 1032200 | tf_op jit(solution)/shard_map/ppermute | solution.py:16
  47.8 14.3 %collective-permute-start.2 = (bf16[2,48,1792]{2,1,0:T(8,128)(2,1)S(1)}, bf16[2,48,1792]{2,1,0:T(8,128)(2,1)S(1)}, u32[]{:S(2)}, u32[]{:S(2)}) collective-permute-start(bf16[2,48,1792]{2,1,0:T(8,128)(2,1)S(1)} %collective-permute-done.1), channel_id=1, source_target_pairs={{0,44},{4,0},{8,4},{12,8},{16,12},{20,16},{24,20},{28,24},{32,28},... | collective-permute-start | bytes 1032200 | tf_op jit(solution)/shard_map/ppermute | solution.py:16
  53.1 14.2 %collective-permute-start.6 = (bf16[2,48,1792]{2,1,0:T(8,128)(2,1)S(1)}, bf16[2,48,1792]{2,1,0:T(8,128)(2,1)S(1)}, u32[]{:S(2)}, u32[]{:S(2)}) collective-permute-start(bf16[2,48,1792]{2,1,0:T(8,128)(2,1)S(1)} %collective-permute-done.5), channel_id=1, source_target_pairs={{0,4},{4,8},{8,12},{12,16},{16,20},{20,24},{24,28},{28,32},{32,36}... | collective-permute-start | bytes 1032200 | tf_op jit(solution)/shard_map/ppermute | solution.py:16
  55.0 14.2 %collective-permute-start.38 = (bf16[2,48,1792]{2,1,0:T(8,128)(2,1)S(1)}, bf16[2,48,1792]{2,1,0:T(8,128)(2,1)S(1)}, u32[]{:S(2)}, u32[]{:S(2)}) collective-permute-start(bf16[2,48,1792]{2,1,0:T(8,128)(2,1)S(1)} %collective-permute-done.37), channel_id=1, source_target_pairs={{0,44},{4,0},{8,4},{12,8},{16,12},{20,16},{24,20},{28,24},{32,28},... | collective-permute-start | bytes 1032200 | tf_op jit(solution)/shard_map/ppermute | solution.py:16
  60.1 14.3 %collective-permute-start.42 = (bf16[2,48,1792]{2,1,0:T(8,128)(2,1)S(1)}, bf16[2,48,1792]{2,1,0:T(8,128)(2,1)S(1)}, u32[]{:S(2)}, u32[]{:S(2)}) collective-permute-start(bf16[2,48,1792]{2,1,0:T(8,128)(2,1)S(1)} %collective-permute-done.41), channel_id=1, source_target_pairs={{0,4},{4,8},{8,12},{12,16},{16,20},{20,24},{24,28},{28,32},{32,36}... | collective-permute-start | bytes 1032200 | tf_op jit(solution)/shard_map/ppermute | solution.py:16
  62.1 14.3 %collective-permute-start.3 = (bf16[2,48,1792]{2,1,0:T(8,128)(2,1)S(1)}, bf16[2,48,1792]{2,1,0:T(8,128)(2,1)S(1)}, u32[]{:S(2)}, u32[]{:S(2)}) collective-permute-start(bf16[2,48,1792]{2,1,0:T(8,128)(2,1)S(1)} %collective-permute-done.2), channel_id=1, source_target_pairs={{0,44},{4,0},{8,4},{12,8},{16,12},{20,16},{24,20},{28,24},{32,28},... | collective-permute-start | bytes 1032200 | tf_op jit(solution)/shard_map/ppermute | solution.py:16
  67.3 14.3 %collective-permute-start.7 = (bf16[2,48,1792]{2,1,0:T(8,128)(2,1)S(1)}, bf16[2,48,1792]{2,1,0:T(8,128)(2,1)S(1)}, u32[]{:S(2)}, u32[]{:S(2)}) collective-permute-start(bf16[2,48,1792]{2,1,0:T(8,128)(2,1)S(1)} %collective-permute-done.6), channel_id=1, source_target_pairs={{0,4},{4,8},{8,12},{12,16},{16,20},{20,24},{24,28},{28,32},{32,36}... | collective-permute-start | bytes 1032200 | tf_op jit(solution)/shard_map/ppermute | solution.py:16
  69.3 14.3 %collective-permute-start.39 = (bf16[48,1792]{1,0:T(8,128)(2,1)S(1)}, bf16[48,1792]{1,0:T(8,128)(2,1)S(1)}, u32[]{:S(2)}, u32[]{:S(2)}) collective-permute-start(bf16[48,1792]{1,0:T(8,128)(2,1)S(1)} %get-tuple-element.65), channel_id=1, source_target_pairs={{0,44},{4,0},{8,4},{12,8},{16,12},{20,16},{24,20},{28,24},{32,28},... | collective-permute-start | bytes 516104 | tf_op jit(solution)/shard_map/ppermute | solution.py:16
  74.5 14.3 %collective-permute-start.43 = (bf16[48,1792]{1,0:T(8,128)(2,1)S(1)}, bf16[48,1792]{1,0:T(8,128)(2,1)S(1)}, u32[]{:S(2)}, u32[]{:S(2)}) collective-permute-start(bf16[48,1792]{1,0:T(8,128)(2,1)S(1)} %get-tuple-element.67), channel_id=1, source_target_pairs={{0,4},{4,8},{8,12},{12,16},{16,20},{20,24},{24,28},{28,32},{32,36}... | collective-permute-start | bytes 516104 | tf_op jit(solution)/shard_map/ppermute | solution.py:16
  76.4 14.2 %collective-permute-start.4 = (bf16[48,1792]{1,0:T(8,128)(2,1)S(1)}, bf16[48,1792]{1,0:T(8,128)(2,1)S(1)}, u32[]{:S(2)}, u32[]{:S(2)}) collective-permute-start(bf16[48,1792]{1,0:T(8,128)(2,1)S(1)} %get-tuple-element.72), channel_id=1, source_target_pairs={{0,44},{4,0},{8,4},{12,8},{16,12},{20,16},{24,20},{28,24},{32,28},... | collective-permute-start | bytes 516104 | tf_op jit(solution)/shard_map/ppermute | solution.py:16
  81.6 14.2 %collective-permute-start.8 = (bf16[48,1792]{1,0:T(8,128)(2,1)S(1)}, bf16[48,1792]{1,0:T(8,128)(2,1)S(1)}, u32[]{:S(2)}, u32[]{:S(2)}) collective-permute-start(bf16[48,1792]{1,0:T(8,128)(2,1)S(1)} %get-tuple-element.74), channel_id=1, source_target_pairs={{0,4},{4,8},{8,12},{12,16},{16,20},{20,24},{24,28},{28,32},{32,36}... | collective-permute-start | bytes 516104 | tf_op jit(solution)/shard_map/ppermute | solution.py:16
  83.6 14.3 %collective-permute-start.44 = (bf16[48,1792]{1,0:T(8,128)(2,1)S(1)}, bf16[48,1792]{1,0:T(8,128)(2,1)S(1)}, u32[]{:S(2)}, u32[]{:S(2)}) collective-permute-start(bf16[48,1792]{1,0:T(8,128)(2,1)S(1)} %collective-permute-done.39), channel_id=1, source_target_pairs={{0,44},{4,0},{8,4},{12,8},{16,12},{20,16},{24,20},{28,24},{32,28},... | collective-permute-start | bytes 516104 | tf_op jit(solution)/shard_map/ppermute | solution.py:16
  88.7 14.3 %collective-permute-start.47 = (bf16[48,1792]{1,0:T(8,128)(2,1)S(1)}, bf16[48,1792]{1,0:T(8,128)(2,1)S(1)}, u32[]{:S(2)}, u32[]{:S(2)}) collective-permute-start(bf16[48,1792]{1,0:T(8,128)(2,1)S(1)} %collective-permute-done.43), channel_id=1, source_target_pairs={{0,4},{4,8},{8,12},{12,16},{16,20},{20,24},{24,28},{28,32},{32,36}... | collective-permute-start | bytes 516104 | tf_op jit(solution)/shard_map/ppermute | solution.py:16
  90.7 17.5 %collective-permute-start.9 = (bf16[48,1792]{1,0:T(8,128)(2,1)S(1)}, bf16[48,1792]{1,0:T(8,128)(2,1)S(1)}, u32[]{:S(2)}, u32[]{:S(2)}) collective-permute-start(bf16[48,1792]{1,0:T(8,128)(2,1)S(1)} %collective-permute-done.4), channel_id=1, source_target_pairs={{0,44},{4,0},{8,4},{12,8},{16,12},{20,16},{24,20},{28,24},{32,28},... | collective-permute-start | bytes 516104 | tf_op jit(solution)/shard_map/ppermute | solution.py:16
  95.9 10.4 %collective-permute-start.12 = (bf16[48,1792]{1,0:T(8,128)(2,1)S(1)}, bf16[48,1792]{1,0:T(8,128)(2,1)S(1)}, u32[]{:S(2)}, u32[]{:S(2)}) collective-permute-start(bf16[48,1792]{1,0:T(8,128)(2,1)S(1)} %collective-permute-done.8), channel_id=1, source_target_pairs={{0,4},{4,8},{8,12},{12,16},{16,20},{20,24},{24,28},{28,32},{32,36}... | collective-permute-start | bytes 516104 | tf_op jit(solution)/shard_map/ppermute | solution.py:16
  97.9 15.5 %collective-permute-start.45 = (bf16[48,1792]{1,0:T(8,128)(2,1)S(1)}, bf16[48,1792]{1,0:T(8,128)(2,1)S(1)}, u32[]{:S(2)}, u32[]{:S(2)}) collective-permute-start(bf16[48,1792]{1,0:T(8,128)(2,1)S(1)} %collective-permute-done.44), channel_id=1, source_target_pairs={{0,44},{4,0},{8,4},{12,8},{16,12},{20,16},{24,20},{28,24},{32,28},... | collective-permute-start | bytes 516104 | tf_op jit(solution)/shard_map/ppermute | solution.py:16
  103.1 19.5 %collective-permute-start.48 = (bf16[48,1792]{1,0:T(8,128)(2,1)S(1)}, bf16[48,1792]{1,0:T(8,128)(2,1)S(1)}, u32[]{:S(2)}, u32[]{:S(2)}) collective-permute-start(bf16[48,1792]{1,0:T(8,128)(2,1)S(1)} %collective-permute-done.47), channel_id=1, source_target_pairs={{0,4},{4,8},{8,12},{12,16},{16,20},{20,24},{24,28},{28,32},{32,36}... | collective-permute-start | bytes 516104 | tf_op jit(solution)/shard_map/ppermute | solution.py:16
  106.3 18.4 %collective-permute-start.13 = (bf16[48,1792]{1,0:T(8,128)(2,1)S(1)}, bf16[48,1792]{1,0:T(8,128)(2,1)S(1)}, u32[]{:S(2)}, u32[]{:S(2)}) collective-permute-start(bf16[48,1792]{1,0:T(8,128)(2,1)S(1)} %collective-permute-done.12), channel_id=1, source_target_pairs={{0,4},{4,8},{8,12},{12,16},{16,20},{20,24},{24,28},{28,32},{32,36}... | collective-permute-start | bytes 516104 | tf_op jit(solution)/shard_map/ppermute | solution.py:16
  108.2 8.8 %collective-permute-start.10 = (bf16[48,1792]{1,0:T(8,128)(2,1)S(1)}, bf16[48,1792]{1,0:T(8,128)(2,1)S(1)}, u32[]{:S(2)}, u32[]{:S(2)}) collective-permute-start(bf16[48,1792]{1,0:T(8,128)(2,1)S(1)} %collective-permute-done.9), channel_id=1, source_target_pairs={{0,44},{4,0},{8,4},{12,8},{16,12},{20,16},{24,20},{28,24},{32,28},... | collective-permute-start | bytes 516104 | tf_op jit(solution)/shard_map/ppermute | solution.py:16
  113.4 13.3 %collective-permute-start.46 = (bf16[48,1792]{1,0:T(8,128)(2,1)S(1)}, bf16[48,1792]{1,0:T(8,128)(2,1)S(1)}, u32[]{:S(2)}, u32[]{:S(2)}) collective-permute-start(bf16[48,1792]{1,0:T(8,128)(2,1)S(1)} %collective-permute-done.45), channel_id=1, source_target_pairs={{0,44},{4,0},{8,4},{12,8},{16,12},{20,16},{24,20},{28,24},{32,28},... | collective-permute-start | bytes 516104 | tf_op jit(solution)/shard_map/ppermute | solution.py:16
  117.0 18.1 %collective-permute-start.11 = (bf16[48,1792]{1,0:T(8,128)(2,1)S(1)}, bf16[48,1792]{1,0:T(8,128)(2,1)S(1)}, u32[]{:S(2)}, u32[]{:S(2)}) collective-permute-start(bf16[48,1792]{1,0:T(8,128)(2,1)S(1)} %collective-permute-done.10), channel_id=1, source_target_pairs={{0,44},{4,0},{8,4},{12,8},{16,12},{20,16},{24,20},{28,24},{32,28},... | collective-permute-start | bytes 516104 | tf_op jit(solution)/shard_map/ppermute | solution.py:16
  124.7 10.5 %collective-permute-start.14 = (bf16[48,1792]{1,0:T(8,128)(2,1)S(1)}, bf16[48,1792]{1,0:T(8,128)(2,1)S(1)}, u32[]{:S(2)}, u32[]{:S(2)}) collective-permute-start(bf16[48,1792]{1,0:T(8,128)(2,1)S(1)} %collective-permute-done.13), channel_id=1, source_target_pairs={{0,4},{4,8},{8,12},{12,16},{16,20},{20,24},{24,28},{28,32},{32,36}... | collective-permute-start | bytes 516104 | tf_op jit(solution)/shard_map/ppermute | solution.py:16
  145.8 8.9 %collective-permute-start.52 = (bf16[144,512]{1,0:T(8,128)(2,1)S(1)}, bf16[144,512]{1,0:T(8,128)(2,1)S(1)}, u32[]{:S(2)}, u32[]{:S(2)}) collective-permute-start(bf16[144,512]{1,0:T(8,128)(2,1)S(1)} %pad_maximum_fusion.20), channel_id=1, source_target_pairs={{0,2},{2,0},{1,3},{3,1},{4,6},{6,4},{5,7},{7,5},{8,10},{10,8},{9,1... | collective-permute-start | bytes 442376 | tf_op jit(solution)/shard_map/ppermute | solution.py:20
  150.9 8.6 %collective-permute-start.16 = (bf16[144,512]{1,0:T(8,128)(2,1)S(1)}, bf16[144,512]{1,0:T(8,128)(2,1)S(1)}, u32[]{:S(2)}, u32[]{:S(2)}) collective-permute-start(bf16[144,512]{1,0:T(8,128)(2,1)S(1)} %select_convert_fusion.2), channel_id=1, source_target_pairs={{0,2},{2,0},{1,3},{3,1},{4,6},{6,4},{5,7},{7,5},{8,10},{10,8},{9,1... | collective-permute-start | bytes 442376 | tf_op jit(solution)/shard_map/ppermute | solution.py:20
  167.5 9.5 %collective-permute-start.18 = (bf16[288,256]{1,0:T(8,128)(2,1)S(1)}, bf16[288,256]{1,0:T(8,128)(2,1)S(1)}, u32[]{:S(2)}, u32[]{:S(2)}) collective-permute-start(bf16[288,256]{1,0:T(8,128)(2,1)S(1)} %pad_maximum_fusion.18), channel_id=1, source_target_pairs={{0,1},{1,0},{2,3},{3,2},{4,5},{5,4},{6,7},{7,6},{8,9},{9,8},{10,11... | collective-permute-start | bytes 442376 | tf_op jit(solution)/shard_map/ppermute | solution.py:20
  171.1 12.7 %collective-permute-start.54 = (bf16[48,1792]{1,0:T(8,128)(2,1)S(1)}, bf16[48,1792]{1,0:T(8,128)(2,1)S(1)}, u32[]{:S(2)}, u32[]{:S(2)}) collective-permute-start(bf16[48,1792]{1,0:T(8,128)(2,1)S(1)} %get-tuple-element.12), channel_id=1, source_target_pairs={{0,44},{4,0},{8,4},{12,8},{16,12},{20,16},{24,20},{28,24},{32,28},... | collective-permute-start | bytes 516104 | tf_op jit(solution)/shard_map/ppermute | solution.py:16
  173.1 10.7 %collective-permute-start.61 = (bf16[48,1792]{1,0:T(8,128)(2,1)S(1)}, bf16[48,1792]{1,0:T(8,128)(2,1)S(1)}, u32[]{:S(2)}, u32[]{:S(2)}) collective-permute-start(bf16[48,1792]{1,0:T(8,128)(2,1)S(1)} %get-tuple-element.10), channel_id=1, source_target_pairs={{0,4},{4,8},{8,12},{12,16},{16,20},{20,24},{24,28},{28,32},{32,36}... | collective-permute-start | bytes 516104 | tf_op jit(solution)/shard_map/ppermute | solution.py:16
  177.9 12.2 %collective-permute-start.19 = (bf16[48,1792]{1,0:T(8,128)(2,1)S(1)}, bf16[48,1792]{1,0:T(8,128)(2,1)S(1)}, u32[]{:S(2)}, u32[]{:S(2)}) collective-permute-start(bf16[48,1792]{1,0:T(8,128)(2,1)S(1)} %get-tuple-element.32), channel_id=1, source_target_pairs={{0,44},{4,0},{8,4},{12,8},{16,12},{20,16},{24,20},{28,24},{32,28},... | collective-permute-start | bytes 516104 | tf_op jit(solution)/shard_map/ppermute | solution.py:16
  181.1 9.3 %collective-permute-start.26 = (bf16[48,1792]{1,0:T(8,128)(2,1)S(1)}, bf16[48,1792]{1,0:T(8,128)(2,1)S(1)}, u32[]{:S(2)}, u32[]{:S(2)}) collective-permute-start(bf16[48,1792]{1,0:T(8,128)(2,1)S(1)} %get-tuple-element.30), channel_id=1, source_target_pairs={{0,4},{4,8},{8,12},{12,16},{16,20},{20,24},{24,28},{28,32},{32,36}... | collective-permute-start | bytes 516104 | tf_op jit(solution)/shard_map/ppermute | solution.py:16
  183.9 13.4 %collective-permute-start.55 = (bf16[48,1792]{1,0:T(8,128)(2,1)S(1)}, bf16[48,1792]{1,0:T(8,128)(2,1)S(1)}, u32[]{:S(2)}, u32[]{:S(2)}) collective-permute-start(bf16[48,1792]{1,0:T(8,128)(2,1)S(1)} %get-tuple-element.20), channel_id=1, source_target_pairs={{0,44},{4,0},{8,4},{12,8},{16,12},{20,16},{24,20},{28,24},{32,28},... | collective-permute-start | bytes 516104 | tf_op jit(solution)/shard_map/ppermute | solution.py:16
  188.2 9.1 %collective-permute-start.62 = (bf16[48,1792]{1,0:T(8,128)(2,1)S(1)}, bf16[48,1792]{1,0:T(8,128)(2,1)S(1)}, u32[]{:S(2)}, u32[]{:S(2)}) collective-permute-start(bf16[48,1792]{1,0:T(8,128)(2,1)S(1)} %get-tuple-element.21), channel_id=1, source_target_pairs={{0,4},{4,8},{8,12},{12,16},{16,20},{20,24},{24,28},{28,32},{32,36}... | collective-permute-start | bytes 516104 | tf_op jit(solution)/shard_map/ppermute | solution.py:16
  190.4 14.2 %collective-permute-start.20 = (bf16[48,1792]{1,0:T(8,128)(2,1)S(1)}, bf16[48,1792]{1,0:T(8,128)(2,1)S(1)}, u32[]{:S(2)}, u32[]{:S(2)}) collective-permute-start(bf16[48,1792]{1,0:T(8,128)(2,1)S(1)} %get-tuple-element.40), channel_id=1, source_target_pairs={{0,44},{4,0},{8,4},{12,8},{16,12},{20,16},{24,20},{28,24},{32,28},... | collective-permute-start | bytes 516104 | tf_op jit(solution)/shard_map/ppermute | solution.py:16
  195.4 9.3 %collective-permute-start.27 = (bf16[48,1792]{1,0:T(8,128)(2,1)S(1)}, bf16[48,1792]{1,0:T(8,128)(2,1)S(1)}, u32[]{:S(2)}, u32[]{:S(2)}) collective-permute-start(bf16[48,1792]{1,0:T(8,128)(2,1)S(1)} %get-tuple-element.41), channel_id=1, source_target_pairs={{0,4},{4,8},{8,12},{12,16},{16,20},{20,24},{24,28},{28,32},{32,36}... | collective-permute-start | bytes 516104 | tf_op jit(solution)/shard_map/ppermute | solution.py:16
  197.3 14.4 %collective-permute-start.56 = (bf16[48,1792]{1,0:T(8,128)(2,1)S(1)}, bf16[48,1792]{1,0:T(8,128)(2,1)S(1)}, u32[]{:S(2)}, u32[]{:S(2)}) collective-permute-start(bf16[48,1792]{1,0:T(8,128)(2,1)S(1)} %get-tuple-element.18), channel_id=1, source_target_pairs={{0,44},{4,0},{8,4},{12,8},{16,12},{20,16},{24,20},{28,24},{32,28},... | collective-permute-start | bytes 516104 | tf_op jit(solution)/shard_map/ppermute | solution.py:16
  202.5 9.3 %collective-permute-start.63 = (bf16[48,1792]{1,0:T(8,128)(2,1)S(1)}, bf16[48,1792]{1,0:T(8,128)(2,1)S(1)}, u32[]{:S(2)}, u32[]{:S(2)}) collective-permute-start(bf16[48,1792]{1,0:T(8,128)(2,1)S(1)} %get-tuple-element.19), channel_id=1, source_target_pairs={{0,4},{4,8},{8,12},{12,16},{16,20},{20,24},{24,28},{28,32},{32,36}... | collective-permute-start | bytes 516104 | tf_op jit(solution)/shard_map/ppermute | solution.py:16
  204.7 14.2 %collective-permute-start.21 = (bf16[48,1792]{1,0:T(8,128)(2,1)S(1)}, bf16[48,1792]{1,0:T(8,128)(2,1)S(1)}, u32[]{:S(2)}, u32[]{:S(2)}) collective-permute-start(bf16[48,1792]{1,0:T(8,128)(2,1)S(1)} %get-tuple-element.38), channel_id=1, source_target_pairs={{0,44},{4,0},{8,4},{12,8},{16,12},{20,16},{24,20},{28,24},{32,28},... | collective-permute-start | bytes 516104 | tf_op jit(solution)/shard_map/ppermute | solution.py:16
  209.8 9.1 %collective-permute-start.28 = (bf16[48,1792]{1,0:T(8,128)(2,1)S(1)}, bf16[48,1792]{1,0:T(8,128)(2,1)S(1)}, u32[]{:S(2)}, u32[]{:S(2)}) collective-permute-start(bf16[48,1792]{1,0:T(8,128)(2,1)S(1)} %get-tuple-element.39), channel_id=1, source_target_pairs={{0,4},{4,8},{8,12},{12,16},{16,20},{20,24},{24,28},{28,32},{32,36}... | collective-permute-start | bytes 516104 | tf_op jit(solution)/shard_map/ppermute | solution.py:16
  211.8 14.2 %collective-permute-start.57 = (bf16[48,1792]{1,0:T(8,128)(2,1)S(1)}, bf16[48,1792]{1,0:T(8,128)(2,1)S(1)}, u32[]{:S(2)}, u32[]{:S(2)}) collective-permute-start(bf16[48,1792]{1,0:T(8,128)(2,1)S(1)} %get-tuple-element.16), channel_id=1, source_target_pairs={{0,44},{4,0},{8,4},{12,8},{16,12},{20,16},{24,20},{28,24},{32,28},... | collective-permute-start | bytes 516104 | tf_op jit(solution)/shard_map/ppermute | solution.py:16
  216.9 9.1 %collective-permute-start.64 = (bf16[48,1792]{1,0:T(8,128)(2,1)S(1)}, bf16[48,1792]{1,0:T(8,128)(2,1)S(1)}, u32[]{:S(2)}, u32[]{:S(2)}) collective-permute-start(bf16[48,1792]{1,0:T(8,128)(2,1)S(1)} %get-tuple-element.17), channel_id=1, source_target_pairs={{0,4},{4,8},{8,12},{12,16},{16,20},{20,24},{24,28},{28,32},{32,36}... | collective-permute-start | bytes 516104 | tf_op jit(solution)/shard_map/ppermute | solution.py:16
  218.9 14.3 %collective-permute-start.22 = (bf16[48,1792]{1,0:T(8,128)(2,1)S(1)}, bf16[48,1792]{1,0:T(8,128)(2,1)S(1)}, u32[]{:S(2)}, u32[]{:S(2)}) collective-permute-start(bf16[48,1792]{1,0:T(8,128)(2,1)S(1)} %get-tuple-element.36), channel_id=1, source_target_pairs={{0,44},{4,0},{8,4},{12,8},{16,12},{20,16},{24,20},{28,24},{32,28},... | collective-permute-start | bytes 516104 | tf_op jit(solution)/shard_map/ppermute | solution.py:16
  224.1 9.2 %collective-permute-start.29 = (bf16[48,1792]{1,0:T(8,128)(2,1)S(1)}, bf16[48,1792]{1,0:T(8,128)(2,1)S(1)}, u32[]{:S(2)}, u32[]{:S(2)}) collective-permute-start(bf16[48,1792]{1,0:T(8,128)(2,1)S(1)} %get-tuple-element.37), channel_id=1, source_target_pairs={{0,4},{4,8},{8,12},{12,16},{16,20},{20,24},{24,28},{28,32},{32,36}... | collective-permute-start | bytes 516104 | tf_op jit(solution)/shard_map/ppermute | solution.py:16
  226.1 14.3 %collective-permute-start.58 = (bf16[2,48,1792]{2,1,0:T(8,128)(2,1)S(1)}, bf16[2,48,1792]{2,1,0:T(8,128)(2,1)S(1)}, u32[]{:S(2)}, u32[]{:S(2)}) collective-permute-start(bf16[2,48,1792]{2,1,0:T(8,128)(2,1)S(1)} %pad_maximum_fusion.13), channel_id=1, source_target_pairs={{0,44},{4,0},{8,4},{12,8},{16,12},{20,16},{24,20},{28,24},{32,28},... | collective-permute-start | bytes 1032200 | tf_op jit(solution)/shard_map/ppermute | solution.py:16
  231.3 14.4 %collective-permute-start.65 = (bf16[2,48,1792]{2,1,0:T(8,128)(2,1)S(1)}, bf16[2,48,1792]{2,1,0:T(8,128)(2,1)S(1)}, u32[]{:S(2)}, u32[]{:S(2)}) collective-permute-start(bf16[2,48,1792]{2,1,0:T(8,128)(2,1)S(1)} %pad_maximum_fusion.14), channel_id=1, source_target_pairs={{0,4},{4,8},{8,12},{12,16},{16,20},{20,24},{24,28},{28,32},{32,36}... | collective-permute-start | bytes 1032200 | tf_op jit(solution)/shard_map/ppermute | solution.py:16
  233.3 14.3 %collective-permute-start.23 = (bf16[2,48,1792]{2,1,0:T(8,128)(2,1)S(1)}, bf16[2,48,1792]{2,1,0:T(8,128)(2,1)S(1)}, u32[]{:S(2)}, u32[]{:S(2)}) collective-permute-start(bf16[2,48,1792]{2,1,0:T(8,128)(2,1)S(1)} %pad_maximum_fusion.10), channel_id=1, source_target_pairs={{0,44},{4,0},{8,4},{12,8},{16,12},{20,16},{24,20},{28,24},{32,28},... | collective-permute-start | bytes 1032200 | tf_op jit(solution)/shard_map/ppermute | solution.py:16
  238.5 14.3 %collective-permute-start.30 = (bf16[2,48,1792]{2,1,0:T(8,128)(2,1)S(1)}, bf16[2,48,1792]{2,1,0:T(8,128)(2,1)S(1)}, u32[]{:S(2)}, u32[]{:S(2)}) collective-permute-start(bf16[2,48,1792]{2,1,0:T(8,128)(2,1)S(1)} %pad_maximum_fusion.11), channel_id=1, source_target_pairs={{0,4},{4,8},{8,12},{12,16},{16,20},{20,24},{24,28},{28,32},{32,36}... | collective-permute-start | bytes 1032200 | tf_op jit(solution)/shard_map/ppermute | solution.py:16
  240.5 14.3 %collective-permute-start.59 = (bf16[2,48,1792]{2,1,0:T(8,128)(2,1)S(1)}, bf16[2,48,1792]{2,1,0:T(8,128)(2,1)S(1)}, u32[]{:S(2)}, u32[]{:S(2)}) collective-permute-start(bf16[2,48,1792]{2,1,0:T(8,128)(2,1)S(1)} %maximum_add_fusion.4), channel_id=1, source_target_pairs={{0,44},{4,0},{8,4},{12,8},{16,12},{20,16},{24,20},{28,24},{32,28},... | collective-permute-start | bytes 1032200 | tf_op jit(solution)/shard_map/ppermute | solution.py:16
  245.7 14.3 %collective-permute-start.66 = (bf16[2,48,1792]{2,1,0:T(8,128)(2,1)S(1)}, bf16[2,48,1792]{2,1,0:T(8,128)(2,1)S(1)}, u32[]{:S(2)}, u32[]{:S(2)}) collective-permute-start(bf16[2,48,1792]{2,1,0:T(8,128)(2,1)S(1)} %maximum_add_fusion.6), channel_id=1, source_target_pairs={{0,4},{4,8},{8,12},{12,16},{16,20},{20,24},{24,28},{28,32},{32,36}... | collective-permute-start | bytes 1032200 | tf_op jit(solution)/shard_map/ppermute | solution.py:16
  247.7 14.3 %collective-permute-start.24 = (bf16[2,48,1792]{2,1,0:T(8,128)(2,1)S(1)}, bf16[2,48,1792]{2,1,0:T(8,128)(2,1)S(1)}, u32[]{:S(2)}, u32[]{:S(2)}) collective-permute-start(bf16[2,48,1792]{2,1,0:T(8,128)(2,1)S(1)} %maximum_add_fusion), channel_id=1, source_target_pairs={{0,44},{4,0},{8,4},{12,8},{16,12},{20,16},{24,20},{28,24},{32,28},... | collective-permute-start | bytes 1032200 | tf_op jit(solution)/shard_map/ppermute | solution.py:16
  252.9 14.3 %collective-permute-start.31 = (bf16[2,48,1792]{2,1,0:T(8,128)(2,1)S(1)}, bf16[2,48,1792]{2,1,0:T(8,128)(2,1)S(1)}, u32[]{:S(2)}, u32[]{:S(2)}) collective-permute-start(bf16[2,48,1792]{2,1,0:T(8,128)(2,1)S(1)} %maximum_add_fusion.2), channel_id=1, source_target_pairs={{0,4},{4,8},{8,12},{12,16},{16,20},{20,24},{24,28},{28,32},{32,36}... | collective-permute-start | bytes 1032200 | tf_op jit(solution)/shard_map/ppermute | solution.py:16
  254.9 14.4 %collective-permute-start.60 = (bf16[2,48,1792]{2,1,0:T(8,128)(2,1)S(1)}, bf16[2,48,1792]{2,1,0:T(8,128)(2,1)S(1)}, u32[]{:S(2)}, u32[]{:S(2)}) collective-permute-start(bf16[2,48,1792]{2,1,0:T(8,128)(2,1)S(1)} %maximum_add_fusion.5), channel_id=1, source_target_pairs={{0,44},{4,0},{8,4},{12,8},{16,12},{20,16},{24,20},{28,24},{32,28},... | collective-permute-start | bytes 1032200 | tf_op jit(solution)/shard_map/ppermute | solution.py:16
  260.1 14.4 %collective-permute-start.67 = (bf16[2,48,1792]{2,1,0:T(8,128)(2,1)S(1)}, bf16[2,48,1792]{2,1,0:T(8,128)(2,1)S(1)}, u32[]{:S(2)}, u32[]{:S(2)}) collective-permute-start(bf16[2,48,1792]{2,1,0:T(8,128)(2,1)S(1)} %maximum_add_fusion.7), channel_id=1, source_target_pairs={{0,4},{4,8},{8,12},{12,16},{16,20},{20,24},{24,28},{28,32},{32,36}... | collective-permute-start | bytes 1032200 | tf_op jit(solution)/shard_map/ppermute | solution.py:16
  262.1 15.1 %collective-permute-start.25 = (bf16[2,48,1792]{2,1,0:T(8,128)(2,1)S(1)}, bf16[2,48,1792]{2,1,0:T(8,128)(2,1)S(1)}, u32[]{:S(2)}, u32[]{:S(2)}) collective-permute-start(bf16[2,48,1792]{2,1,0:T(8,128)(2,1)S(1)} %maximum_add_fusion.1), channel_id=1, source_target_pairs={{0,44},{4,0},{8,4},{12,8},{16,12},{20,16},{24,20},{28,24},{32,28},... | collective-permute-start | bytes 1032200 | tf_op jit(solution)/shard_map/ppermute | solution.py:16
  267.3 11.2 %collective-permute-start.32 = (bf16[2,48,1792]{2,1,0:T(8,128)(2,1)S(1)}, bf16[2,48,1792]{2,1,0:T(8,128)(2,1)S(1)}, u32[]{:S(2)}, u32[]{:S(2)}) collective-permute-start(bf16[2,48,1792]{2,1,0:T(8,128)(2,1)S(1)} %maximum_add_fusion.3), channel_id=1, source_target_pairs={{0,4},{4,8},{8,12},{12,16},{16,20},{20,24},{24,28},{28,32},{32,36}... | collective-permute-start | bytes 1032200 | tf_op jit(solution)/shard_map/ppermute | solution.py:16
  274.7 10.7 %collective-permute-start.68 = (bf16[3,24,1792]{2,1,0:T(8,128)(2,1)S(1)}, bf16[3,24,1792]{2,1,0:T(8,128)(2,1)S(1)}, u32[]{:S(2)}, u32[]{:S(2)}) collective-permute-start(bf16[3,24,1792]{2,1,0:T(8,128)(2,1)S(1)} %get-tuple-element.48), channel_id=1, source_target_pairs={{0,48},{48,0},{1,49},{49,1},{2,50},{50,2},{3,51},{51,3},{4,52},{52... | collective-permute-start | bytes 774152 | tf_op jit(solution)/shard_map/ppermute | solution.py:20
  278.7 9.5 %collective-permute-start.33 = (bf16[3,24,1792]{2,1,0:T(8,128)(2,1)S(1)}, bf16[3,24,1792]{2,1,0:T(8,128)(2,1)S(1)}, u32[]{:S(2)}, u32[]{:S(2)}) collective-permute-start(bf16[3,24,1792]{2,1,0:T(8,128)(2,1)S(1)} %get-tuple-element.56), channel_id=1, source_target_pairs={{0,48},{48,0},{1,49},{49,1},{2,50},{50,2},{3,51},{51,3},{4,52},{52... | collective-permute-start | bytes 774152 | tf_op jit(solution)/shard_map/ppermute | solution.py:20
  285.8 10.4 %collective-permute-start.69 = (bf16[128,1792]{1,0:T(8,128)(2,1)S(1)}, bf16[128,1792]{1,0:T(8,128)(2,1)S(1)}, u32[]{:S(2)}, u32[]{:S(2)}) collective-permute-start(bf16[128,1792]{1,0:T(8,128)(2,1)S(1)} %convolution_convert_fusion.3), channel_id=1, source_target_pairs={{96,0},{192,96},{288,192},{384,288},{480,384},{576,480},{672,576},... | collective-permute-start | bytes 1376264 | tf_op jit(solution)/shard_map/ppermute | solution.py:205
  288.6 12.5 %collective-permute-start.34 = (bf16[128,1792]{1,0:T(8,128)(2,1)S(1)}, bf16[128,1792]{1,0:T(8,128)(2,1)S(1)}, u32[]{:S(2)}, u32[]{:S(2)}) collective-permute-start(bf16[128,1792]{1,0:T(8,128)(2,1)S(1)} %fusion), channel_id=1, source_target_pairs={{0,96},{96,192},{192,288},{288,384},{384,480},{480,576},{576,672},... | collective-permute-start | bytes 1376264 | tf_op jit(solution)/shard_map/ppermute | solution.py:204
  (12 other events, 214.6 us)

commit v2 on v1

v2 whole, which is shorter than its diff:
```python
import jax
import jax.numpy as jnp
from jax import lax
from jax.sharding import Mesh
from jax.sharding import PartitionSpec as P

GROUP = 4
PAD = 8
RING = ("group", "member")
BF16 = jnp.bfloat16
F32 = jnp.float32


def hop(values, step):
    count = lax.axis_size(RING)
    return lax.ppermute(values, RING, [(i, (i + step) % count) for i in range(count)])


def swap(values, axis):
    return lax.ppermute(values, axis, [(0, 1), (1, 0)])


def placing_of(routes, capacity, width):
    groups = lax.axis_size("group")
    half, group = lax.axis_index("half"), lax.axis_index("group")
    near = [half * groups + (group + k) % groups for k in range(groups)]
    far = [(1 - half) * groups + (group + k) % groups for k in range(groups)]
    ids = jnp.stack(near + far).astype(jnp.int32)
    member = (routes[None, :, 0] == ids[:, None]).astype(jnp.int32)
    before = jnp.cumsum(member, axis=1) - member
    slot_ids = jnp.arange(width, dtype=jnp.int32)
    hit = (before[:, None, :] == slot_ids[None, :, None]) & (slot_ids < capacity)[None, :, None]
    placing = jnp.where(hit & (member[:, None, :] > 0), 1.0, 0.0).astype(BF16)
    return placing.reshape(-1, routes.shape[0])


def around(values, step):
    return lax.ppermute(values, "member", [(i, (i + step) % GROUP) for i in range(GROUP)])


def dispatch(slots, step):
    blocks = jnp.concatenate([slots[0], swap(slots[1], "half")], axis=1)
    part = jnp.stack([blocks[0], hop(blocks[2], -GROUP), hop(blocks[1], GROUP)])
    part = part.reshape(-1, slots.shape[-1])
    parts = [part]
    for _ in range(1, GROUP):
        part = around(part, step)
        parts.append(part)
    return parts


def collect(parts, step, groups):
    total = parts[GROUP - 1]
    for k in range(GROUP - 2, -1, -1):
        total = around(total, -step) + parts[k]
    total = total.reshape(groups, 2, -1, total.shape[-1])
    blocks = jnp.stack([total[0], hop(total[2], -GROUP), hop(total[1], GROUP)])
    return jnp.stack([blocks[:, 0], swap(blocks[:, 1], "half")])


def reduce_rows(parts):
    place = lax.axis_index("core")
    low = jnp.concatenate(parts[: GROUP // 2])
    high = jnp.concatenate(parts[GROUP // 2 :])
    kept, sent = jnp.where(place == 0, low, high), jnp.where(place == 0, high, low)
    kept = kept + swap(sent, "core")
    return kept + swap(kept.astype(BF16), "far").astype(F32)


def gather_rows(values):
    place = lax.axis_index("core")
    other = swap(values, "core")
    low, high = jnp.where(place == 0, values, other), jnp.where(place == 0, other, values)
    rows = values.shape[0] // 2
    return [low[:rows], low[rows:], high[:rows], high[rows:]]


def contract_last(left_side, right_side):
    return lax.dot_general(
        left_side, right_side, (((1,), (1,)), ((), ())), preferred_element_type=F32
    )


def saved_half(saved, capacity, width, step):
    groups = lax.axis_size("group")
    half, group, member, core = (lax.axis_index(n) for n in ("half", "group", "member", "core"))
    blocks = saved.reshape(2, groups, GROUP, capacity, *saved.shape[1:])
    out = []
    for k in range(GROUP // 2):
        source = (member - step * (core * (GROUP // 2) + k)) % GROUP
        own = lax.dynamic_index_in_dim(blocks, source, axis=2, keepdims=False)
        for g in range(groups):
            at = (group + g) % groups
            pair = lax.dynamic_index_in_dim(own, at, axis=1, keepdims=False)
            out.append(jnp.where(half == 0, pair, pair[::-1]))
    out = jnp.pad(jnp.stack(out), ((0, 0), (0, 0), (0, width - capacity), (0, 0), (0, 0)))
    return out.reshape(-1, *saved.shape[1:])


def shards(
    tokens_fwd,
    routes_fwd,
    gates_fwd,
    cotangent,
    routes_bwd,
    gates_bwd,
    saved_pre,
    w_gate,
    w_up,
    w_down,
):
    groups = lax.axis_size("group")
    devices = 2 * groups * GROUP
    capacity = saved_pre.shape[1] // devices
    width = -(-capacity // PAD) * PAD
    columns = tokens_fwd.shape[2]
    hidden_width = w_gate.shape[2]

    place_fwd = placing_of(routes_fwd[0], capacity, width)
    place_bwd = placing_of(routes_bwd[0], capacity, width)
    send_fwd = jnp.dot(place_fwd, tokens_fwd[0], preferred_element_type=F32).astype(BF16)
    scaled = (cotangent[0].astype(F32) * gates_bwd[0]).astype(BF16)
    send_bwd = jnp.dot(place_bwd, scaled, preferred_element_type=F32).astype(BF16)

    got_fwd = dispatch(send_fwd.reshape(2, groups, width, columns), 1)
    got_bwd = dispatch(send_bwd.reshape(2, groups, width, columns), -1)
    partial_fwd = [
        jnp.concatenate(
            [
                jnp.dot(rows, w_gate[0], preferred_element_type=F32),
                jnp.dot(rows, w_up[0], preferred_element_type=F32),
            ],
            axis=1,
        )
        for rows in got_fwd
    ]
    summed = reduce_rows(partial_fwd)
    gate_pre, up_pre = summed[:, :hidden_width], summed[:, hidden_width:]
    hidden = gather_rows((gate_pre * jax.nn.sigmoid(gate_pre) * up_pre).astype(BF16))
    out = [jnp.dot(rows, w_down[0], preferred_element_type=F32).astype(BF16) for rows in hidden]
    back_fwd = collect(out, 1, groups).reshape(-1, columns)

    grad_hidden = reduce_rows([contract_last(rows, w_down[0]) for rows in got_bwd])
    saved = saved_half(saved_pre[0], capacity, width, -1)
    pre_gate = saved[:, 0].astype(F32)
    pre_up = saved[:, 1].astype(F32)
    sigmoid_gate = jax.nn.sigmoid(pre_gate)
    grad_gate = grad_hidden * pre_up * sigmoid_gate * (1.0 + pre_gate * (1.0 - sigmoid_gate))
    grad_up = grad_hidden * pre_gate * sigmoid_gate
    grads = gather_rows(jnp.concatenate([grad_gate, grad_up], axis=1).astype(BF16))
    grad_out = [
        (
            contract_last(rows[:, :hidden_width], w_gate[0])
            + contract_last(rows[:, hidden_width:], w_up[0])
        ).astype(BF16)
        for rows in grads
    ]
    back_bwd = collect(grad_out, -1, groups).reshape(-1, columns)

    def rows_of(placing, values):
        return lax.dot_general(
            placing, values, (((0,), (0,)), ((), ())), preferred_element_type=F32
        )

    layer_out = (rows_of(place_fwd, back_fwd) * gates_fwd[0]).astype(BF16)
    layer_grad = rows_of(place_bwd, back_bwd).astype(BF16)
    ends = lax.axis_size("section") - 1
    forwarded = lax.ppermute(layer_out, "section", [(i, i + 1) for i in range(ends)])
    returned = lax.ppermute(layer_grad, "section", [(i + 1, i) for i in range(ends)])
    return (forwarded[None], returned[None])


def solution(mesh):
    sections, expert_devices, quarters = (mesh.shape[name] for name in ("section", "expert", "dp"))
    fine = Mesh(
        mesh.devices.reshape(sections, 2, expert_devices // 2 // GROUP, GROUP, 2, quarters // 2),
        ("section", "half", "group", "member", "far", "core"),
    )
    expert, dp = ("half", "group", "member"), ("far", "core")
    return jax.shard_map(
        shards,
        mesh=fine,
        in_specs=(
            P("section", expert, dp),
            P("section", expert, None),
            P("section", expert, None),
            P("section", expert, dp),
            P("section", expert, None),
            P("section", expert, None),
            P("section", None, None, expert),
            P("section", dp, expert),
            P("section", dp, expert),
            P("section", expert, dp),
        ),
        out_specs=(P("section", expert, dp), P("section", expert, dp)),
        check_vma=False,
    )
```

time: 305 us -> 297 us (0.974)
  the two profiles are of different devices: /device:TPU:32 before, /device:TPU:102 now
where the time goes in v2:
time: 297 us; the launch traced here: 296 us
  starting transfers between devices  143 us (48%)
  waiting for transfers between devices  132 us (44%)
  matrix products  11.6 us (4%)
  local copies, waits for them, and re-layouts  4.2 us (1%)
  other arithmetic  3.06 us (1%)
    ppermute x12, starting transfers between devices, around(): lax.ppermute(values, 'member', [(i, (i + step) % GROUP) for i in range(GR...  68.3 us
    ppermute x12, waiting for transfers between devices, around(): lax.ppermute(values, 'member', [(i, (i + step) % GROUP) for i in range(GR...  65.7 us
    ppermute x8, starting transfers between devices, hop(): lax.ppermute(values, RING, [(i, (i + step) % count) for i in range(count)])  44.8 us
    ppermute x8, waiting for transfers between devices, hop(): lax.ppermute(values, RING, [(i, (i + step) % count) for i in range(count)])  33.9 us
    ppermute x10, starting transfers between devices, swap(): return lax.ppermute(values, axis, [(0, 1), (1, 0)])  24.9 us
    ppermute x10, waiting for transfers between devices, swap(): return lax.ppermute(values, axis, [(0, 1), (1, 0)])  20.3 us
    ppermute x1, waiting for transfers between devices, shards(): lax.ppermute(layer_out, 'section', [(i, i + 1) for i in range(ends)])  9.12 us
  transfers between devices with their start and end apart: 32, of which 23 were waited for; matrix products, arithmetic and copies ran while one was open for 4% of the time, Pallas kernels for 0%

profile of v2, /device:TPU:102, one launch (start us, length us, event | category | flops | bytes accessed | tf_op | source)
XLA Modules:
  0.0 295.5 jit_solution(5722517819429833385)
XLA Ops:
  0.8 0.7 copy-done.5
  2.4 1.3 convolution_convert_fusion.5
  3.8 2.9 collective-permute-start
  6.7 0.6 copy-done.7
  7.7 3.2 %collective-permute-start.16 = (bf16[3,24,1792]{2,1,0:T(8,128)(2,1)S(1)}, bf16[3,24,1792]{2,1,0:T(8,128)(2,1)S(1)}, u32[]{:S(2)}, u32[]{:S(2)}) collective-permute-start(bf16[3,24,1792]{2,1,0:T(8,128)(2,1)S(1)} %bitcast.211), channel_id=1, source_target_pairs={{0,48},{48,0},{1,49},{49,1},{2,50},{50,2},{3,51},{51,3},{4,52},{52... | collective-permute-start | bytes 774152 | tf_op jit(solution)/shard_map/ppermute | solution.py:20
  11.4 3.5 %collective-permute-done = bf16[3,24,1792]{2,1,0:T(8,128)(2,1)S(1)} collective-permute-done((bf16[3,24,1792]{2,1,0:T(8,128)(2,1)S(1)}, bf16[3,24,1792]{2,1,0:T(8,128)(2,1)S(1)}, u32[]{:S(2)}, u32[]{:S(2)}) %collective-permute-start) | collective-permute-done | bytes 258080 | tf_op jit(solution)/shard_map/ppermute | solution.py:20
  14.9 10.9 %collective-permute-start.2 = (bf16[48,1792]{1,0:T(8,128)(2,1)S(1)}, bf16[48,1792]{1,0:T(8,128)(2,1)S(1)}, u32[]{:S(2)}, u32[]{:S(2)}) collective-permute-start(bf16[48,1792]{1,0:T(8,128)(2,1)S(1)} %get-tuple-element.32), channel_id=1, source_target_pairs={{0,16},{4,20},{8,24},{12,28},{16,32},{20,36},{24,40},{28,44},{32,0... | collective-permute-start | bytes 516104 | tf_op jit(solution)/shard_map/ppermute | solution.py:16
  25.8 4.7 %collective-permute-start.1 = (bf16[48,1792]{1,0:T(8,128)(2,1)S(1)}, bf16[48,1792]{1,0:T(8,128)(2,1)S(1)}, u32[]{:S(2)}, u32[]{:S(2)}) collective-permute-start(bf16[48,1792]{1,0:T(8,128)(2,1)S(1)} %get-tuple-element.33), channel_id=1, source_target_pairs={{0,32},{4,36},{8,40},{12,44},{16,0},{20,4},{24,8},{28,12},{32,16},... | collective-permute-start | bytes 516104 | tf_op jit(solution)/shard_map/ppermute | solution.py:16
  30.6 5.1 %collective-permute-start.18 = (bf16[48,1792]{1,0:T(8,128)(2,1)S(1)}, bf16[48,1792]{1,0:T(8,128)(2,1)S(1)}, u32[]{:S(2)}, u32[]{:S(2)}) collective-permute-start(bf16[48,1792]{1,0:T(8,128)(2,1)S(1)} %get-tuple-element.22), channel_id=1, source_target_pairs={{0,16},{4,20},{8,24},{12,28},{16,32},{20,36},{24,40},{28,44},{32,0... | collective-permute-start | bytes 516104 | tf_op jit(solution)/shard_map/ppermute | solution.py:16
  35.7 4.7 %collective-permute-start.17 = (bf16[48,1792]{1,0:T(8,128)(2,1)S(1)}, bf16[48,1792]{1,0:T(8,128)(2,1)S(1)}, u32[]{:S(2)}, u32[]{:S(2)}) collective-permute-start(bf16[48,1792]{1,0:T(8,128)(2,1)S(1)} %get-tuple-element.23), channel_id=1, source_target_pairs={{0,32},{4,36},{8,40},{12,44},{16,0},{20,4},{24,8},{28,12},{32,16},... | collective-permute-start | bytes 516104 | tf_op jit(solution)/shard_map/ppermute | solution.py:16
  40.3 0.6 collective-permute-done.1
  41.0 8.2 %collective-permute-start.3 = (bf16[144,1792]{1,0:T(8,128)(2,1)S(1)}, bf16[144,1792]{1,0:T(8,128)(2,1)S(1)}, u32[]{:S(2)}, u32[]{:S(2)}) collective-permute-start(bf16[144,1792]{1,0:T(8,128)(2,1)S(1)} %bitcast.193), channel_id=1, source_target_pairs={{0,4},{4,8},{8,12},{12,0},{1,5},{5,9},{9,13},{13,1},{2,6},{6,10},{... | collective-permute-start | bytes 1548296 | tf_op jit(solution)/shard_map/ppermute | solution.py:38
  49.5 3.5 %collective-permute-done.17 = bf16[48,1792]{1,0:T(8,128)(2,1)S(1)} collective-permute-done((bf16[48,1792]{1,0:T(8,128)(2,1)S(1)}, bf16[48,1792]{1,0:T(8,128)(2,1)S(1)}, u32[]{:S(2)}, u32[]{:S(2)}) %collective-permute-start.17) | collective-permute-done | bytes 172064 | tf_op jit(solution)/shard_map/ppermute | solution.py:16
  53.1 10.5 %collective-permute-start.19 = (bf16[144,1792]{1,0:T(8,128)(2,1)S(1)}, bf16[144,1792]{1,0:T(8,128)(2,1)S(1)}, u32[]{:S(2)}, u32[]{:S(2)}) collective-permute-start(bf16[144,1792]{1,0:T(8,128)(2,1)S(1)} %bitcast.196), channel_id=1, source_target_pairs={{0,12},{4,0},{8,4},{12,8},{1,13},{5,1},{9,5},{13,9},{2,14},{6,2},{... | collective-permute-start | bytes 1548296 | tf_op jit(solution)/shard_map/ppermute | solution.py:38
  64.4 3.7 %collective-permute-done.3 = bf16[144,1792]{1,0:T(8,128)(2,1)S(1)} collective-permute-done((bf16[144,1792]{1,0:T(8,128)(2,1)S(1)}, bf16[144,1792]{1,0:T(8,128)(2,1)S(1)}, u32[]{:S(2)}, u32[]{:S(2)}) %collective-permute-start.3) | collective-permute-done | bytes 516128 | tf_op jit(solution)/shard_map/ppermute | solution.py:38
  68.0 18.7 %collective-permute-start.4 = (bf16[144,1792]{1,0:T(8,128)(2,1)S(1)}, bf16[144,1792]{1,0:T(8,128)(2,1)S(1)}, u32[]{:S(2)}, u32[]{:S(2)}) collective-permute-start(bf16[144,1792]{1,0:T(8,128)(2,1)S(1)} %collective-permute-done.3), channel_id=1, source_target_pairs={{0,4},{4,8},{8,12},{12,0},{1,5},{5,9},{9,13},{13,1},{2,6},{6,10},{... | collective-permute-start | bytes 1548296 | tf_op jit(solution)/shard_map/ppermute | solution.py:38
  87.0 0.6 collective-permute-done.19
  87.6 3.5 %collective-permute-start.20 = (bf16[144,1792]{1,0:T(8,128)(2,1)S(1)}, bf16[144,1792]{1,0:T(8,128)(2,1)S(1)}, u32[]{:S(2)}, u32[]{:S(2)}) collective-permute-start(bf16[144,1792]{1,0:T(8,128)(2,1)S(1)} %collective-permute-done.19), channel_id=1, source_target_pairs={{0,12},{4,0},{8,4},{12,8},{1,13},{5,1},{9,5},{13,9},{2,14},{6,2},{... | collective-permute-start | bytes 1548296 | tf_op jit(solution)/shard_map/ppermute | solution.py:38
  91.9 14.7 %collective-permute-done.4 = bf16[144,1792]{1,0:T(8,128)(2,1)S(1)} collective-permute-done((bf16[144,1792]{1,0:T(8,128)(2,1)S(1)}, bf16[144,1792]{1,0:T(8,128)(2,1)S(1)}, u32[]{:S(2)}, u32[]{:S(2)}) %collective-permute-start.4) | collective-permute-done | bytes 516128 | tf_op jit(solution)/shard_map/ppermute | solution.py:38
  106.6 5.3 %collective-permute-start.5 = (bf16[144,1792]{1,0:T(8,128)(2,1)S(1)}, bf16[144,1792]{1,0:T(8,128)(2,1)S(1)}, u32[]{:S(2)}, u32[]{:S(2)}) collective-permute-start(bf16[144,1792]{1,0:T(8,128)(2,1)S(1)} %collective-permute-done.4), channel_id=1, source_target_pairs={{0,4},{4,8},{8,12},{12,0},{1,5},{5,9},{9,13},{13,1},{2,6},{6,10},{... | collective-permute-start | bytes 1548296 | tf_op jit(solution)/shard_map/ppermute | solution.py:38
  112.6 4.1 %collective-permute-start.21 = (bf16[144,1792]{1,0:T(8,128)(2,1)S(1)}, bf16[144,1792]{1,0:T(8,128)(2,1)S(1)}, u32[]{:S(2)}, u32[]{:S(2)}) collective-permute-start(bf16[144,1792]{1,0:T(8,128)(2,1)S(1)} %collective-permute-done.20), channel_id=1, source_target_pairs={{0,12},{4,0},{8,4},{12,8},{1,13},{5,1},{9,5},{13,9},{2,14},{6,2},{... | collective-permute-start | bytes 1548296 | tf_op jit(solution)/shard_map/ppermute | solution.py:38
  117.5 15.0 %collective-permute-done.21 = bf16[144,1792]{1,0:T(8,128)(2,1)S(1)} collective-permute-done((bf16[144,1792]{1,0:T(8,128)(2,1)S(1)}, bf16[144,1792]{1,0:T(8,128)(2,1)S(1)}, u32[]{:S(2)}, u32[]{:S(2)}) %collective-permute-start.21) | collective-permute-done | bytes 516128 | tf_op jit(solution)/shard_map/ppermute | solution.py:38
  133.0 1.9 collective-permute-start.22
  135.6 2.4 collective-permute-start.6
  138.1 3.4 %collective-permute-start.23 = (bf16[288,256]{1,0:T(8,128)(2,1)S(1)}, bf16[288,256]{1,0:T(8,128)(2,1)S(1)}, u32[]{:S(2)}, u32[]{:S(2)}) collective-permute-start(bf16[288,256]{1,0:T(8,128)(2,1)S(1)} %get-tuple-element.2), channel_id=1, source_target_pairs={{0,2},{2,0},{1,3},{3,1},{4,6},{6,4},{5,7},{7,5},{8,10},{10,8},{9,1... | collective-permute-start | bytes 442376 | tf_op jit(solution)/shard_map/ppermute | solution.py:20
  141.6 5.7 %collective-permute-done.23 = bf16[288,256]{1,0:T(8,128)(2,1)S(1)} collective-permute-done((bf16[288,256]{1,0:T(8,128)(2,1)S(1)}, bf16[288,256]{1,0:T(8,128)(2,1)S(1)}, u32[]{:S(2)}, u32[]{:S(2)}) %collective-permute-start.23) | collective-permute-done | bytes 147488 | tf_op jit(solution)/shard_map/ppermute | solution.py:20
  147.5 1.9 collective-permute-start.24
  149.6 3.4 %collective-permute-start.7 = (bf16[288,512]{1,0:T(8,128)(2,1)S(1)}, bf16[288,512]{1,0:T(8,128)(2,1)S(1)}, u32[]{:S(2)}, u32[]{:S(2)}) collective-permute-start(bf16[288,512]{1,0:T(8,128)(2,1)S(1)} %get-tuple-element.4), channel_id=1, source_target_pairs={{0,2},{2,0},{1,3},{3,1},{4,6},{6,4},{5,7},{7,5},{8,10},{10,8},{9,1... | collective-permute-start | bytes 884744 | tf_op jit(solution)/shard_map/ppermute | solution.py:20
  154.1 0.5 fusion
  154.5 1.9 collective-permute-start.25
  156.9 0.5 fusion.1
  157.4 5.0 %collective-permute-done.7 = bf16[288,512]{1,0:T(8,128)(2,1)S(1)} collective-permute-done((bf16[288,512]{1,0:T(8,128)(2,1)S(1)}, bf16[288,512]{1,0:T(8,128)(2,1)S(1)}, u32[]{:S(2)}, u32[]{:S(2)}) %collective-permute-start.7) | collective-permute-done | bytes 294944 | tf_op jit(solution)/shard_map/ppermute | solution.py:20
  162.6 1.9 collective-permute-start.8
  164.5 0.5 fusion.2
  165.0 0.9 collective-permute-done.8
  166.3 3.9 %collective-permute-start.9 = (bf16[144,1792]{1,0:T(8,128)(2,1)S(1)}, bf16[144,1792]{1,0:T(8,128)(2,1)S(1)}, u32[]{:S(2)}, u32[]{:S(2)}) collective-permute-start(bf16[144,1792]{1,0:T(8,128)(2,1)S(1)} %convolution_convert_fusion.4), channel_id=1, source_target_pairs={{0,12},{4,0},{8,4},{12,8},{1,13},{5,1},{9,5},{13,9},{2,14},{6,2},{... | collective-permute-start | bytes 1548296 | tf_op jit(solution)/shard_map/ppermute | solution.py:38
  170.7 2.0 collective-permute-start.26
  172.7 0.5 fusion.17
  173.4 10.9 %collective-permute-done.9 = bf16[144,1792]{1,0:T(8,128)(2,1)S(1)} collective-permute-done((bf16[144,1792]{1,0:T(8,128)(2,1)S(1)}, bf16[144,1792]{1,0:T(8,128)(2,1)S(1)}, u32[]{:S(2)}, u32[]{:S(2)}) %collective-permute-start.9) | collective-permute-done | bytes 516128 | tf_op jit(solution)/shard_map/ppermute | solution.py:38
  184.5 3.4 %collective-permute-start.10 = (bf16[144,1792]{1,0:T(8,128)(2,1)S(1)}, bf16[144,1792]{1,0:T(8,128)(2,1)S(1)}, u32[]{:S(2)}, u32[]{:S(2)}) collective-permute-start(bf16[144,1792]{1,0:T(8,128)(2,1)S(1)} %add.197), channel_id=1, source_target_pairs={{0,12},{4,0},{8,4},{12,8},{1,13},{5,1},{9,5},{13,9},{2,14},{6,2},{... | collective-permute-start | bytes 1548296 | tf_op jit(solution)/shard_map/ppermute | solution.py:38
  187.9 5.9 %collective-permute-done.26 = bf16[144,1792]{1,0:T(8,128)(2,1)S(1)} collective-permute-done((bf16[144,1792]{1,0:T(8,128)(2,1)S(1)}, bf16[144,1792]{1,0:T(8,128)(2,1)S(1)}, u32[]{:S(2)}, u32[]{:S(2)}) %collective-permute-start.26) | collective-permute-done | bytes 516128 | tf_op jit(solution)/shard_map/ppermute | solution.py:38
  193.9 3.3 %collective-permute-start.27 = (bf16[144,1792]{1,0:T(8,128)(2,1)S(1)}, bf16[144,1792]{1,0:T(8,128)(2,1)S(1)}, u32[]{:S(2)}, u32[]{:S(2)}) collective-permute-start(bf16[144,1792]{1,0:T(8,128)(2,1)S(1)} %add.216), channel_id=1, source_target_pairs={{0,4},{4,8},{8,12},{12,0},{1,5},{5,9},{9,13},{13,1},{2,6},{6,10},{... | collective-permute-start | bytes 1548296 | tf_op jit(solution)/shard_map/ppermute | solution.py:38
  197.2 0.5 fusion.3
  198.0 8.4 %collective-permute-done.10 = bf16[144,1792]{1,0:T(8,128)(2,1)S(1)} collective-permute-done((bf16[144,1792]{1,0:T(8,128)(2,1)S(1)}, bf16[144,1792]{1,0:T(8,128)(2,1)S(1)}, u32[]{:S(2)}, u32[]{:S(2)}) %collective-permute-start.10) | collective-permute-done | bytes 516128 | tf_op jit(solution)/shard_map/ppermute | solution.py:38
  206.6 3.5 %collective-permute-start.11 = (bf16[144,1792]{1,0:T(8,128)(2,1)S(1)}, bf16[144,1792]{1,0:T(8,128)(2,1)S(1)}, u32[]{:S(2)}, u32[]{:S(2)}) collective-permute-start(bf16[144,1792]{1,0:T(8,128)(2,1)S(1)} %add.198), channel_id=1, source_target_pairs={{0,12},{4,0},{8,4},{12,8},{1,13},{5,1},{9,5},{13,9},{2,14},{6,2},{... | collective-permute-start | bytes 1548296 | tf_op jit(solution)/shard_map/ppermute | solution.py:38
  210.1 5.9 %collective-permute-done.27 = bf16[144,1792]{1,0:T(8,128)(2,1)S(1)} collective-permute-done((bf16[144,1792]{1,0:T(8,128)(2,1)S(1)}, bf16[144,1792]{1,0:T(8,128)(2,1)S(1)}, u32[]{:S(2)}, u32[]{:S(2)}) %collective-permute-start.27) | collective-permute-done | bytes 516128 | tf_op jit(solution)/shard_map/ppermute | solution.py:38
  216.2 5.1 %collective-permute-start.29 = (bf16[2,24,1792]{2,1,0:T(8,128)(2,1)S(1)}, bf16[2,24,1792]{2,1,0:T(8,128)(2,1)S(1)}, u32[]{:S(2)}, u32[]{:S(2)}) collective-permute-start(bf16[2,24,1792]{2,1,0:T(8,128)(2,1)S(1)} %bitcast.225), channel_id=1, source_target_pairs={{0,16},{4,20},{8,24},{12,28},{16,32},{20,36},{24,40},{28,44},{32,0... | collective-permute-start | bytes 516104 | tf_op jit(solution)/shard_map/ppermute | solution.py:16
  221.3 4.6 %collective-permute-start.28 = (bf16[2,24,1792]{2,1,0:T(8,128)(2,1)S(1)}, bf16[2,24,1792]{2,1,0:T(8,128)(2,1)S(1)}, u32[]{:S(2)}, u32[]{:S(2)}) collective-permute-start(bf16[2,24,1792]{2,1,0:T(8,128)(2,1)S(1)} %bitcast.223), channel_id=1, source_target_pairs={{0,32},{4,36},{8,40},{12,44},{16,0},{20,4},{24,8},{28,12},{32,16},... | collective-permute-start | bytes 516104 | tf_op jit(solution)/shard_map/ppermute | solution.py:16
  226.3 15.2 %collective-permute-done.29 = bf16[2,24,1792]{2,1,0:T(8,128)(2,1)S(1)} collective-permute-done((bf16[2,24,1792]{2,1,0:T(8,128)(2,1)S(1)}, bf16[2,24,1792]{2,1,0:T(8,128)(2,1)S(1)}, u32[]{:S(2)}, u32[]{:S(2)}) %collective-permute-start.29) | collective-permute-done | bytes 172064 | tf_op jit(solution)/shard_map/ppermute | solution.py:16
  241.5 3.8 %collective-permute-done.28 = bf16[2,24,1792]{2,1,0:T(8,128)(2,1)S(1)} collective-permute-done((bf16[2,24,1792]{2,1,0:T(8,128)(2,1)S(1)}, bf16[2,24,1792]{2,1,0:T(8,128)(2,1)S(1)}, u32[]{:S(2)}, u32[]{:S(2)}) %collective-permute-start.28) | collective-permute-done | bytes 172064 | tf_op jit(solution)/shard_map/ppermute | solution.py:16
  245.5 5.9 %collective-permute-start.13 = (bf16[2,24,1792]{2,1,0:T(8,128)(2,1)S(1)}, bf16[2,24,1792]{2,1,0:T(8,128)(2,1)S(1)}, u32[]{:S(2)}, u32[]{:S(2)}) collective-permute-start(bf16[2,24,1792]{2,1,0:T(8,128)(2,1)S(1)} %bitcast.221), channel_id=1, source_target_pairs={{0,16},{4,20},{8,24},{12,28},{16,32},{20,36},{24,40},{28,44},{32,0... | collective-permute-start | bytes 516104 | tf_op jit(solution)/shard_map/ppermute | solution.py:16
  251.4 3.9 %collective-permute-start.12 = (bf16[2,24,1792]{2,1,0:T(8,128)(2,1)S(1)}, bf16[2,24,1792]{2,1,0:T(8,128)(2,1)S(1)}, u32[]{:S(2)}, u32[]{:S(2)}) collective-permute-start(bf16[2,24,1792]{2,1,0:T(8,128)(2,1)S(1)} %bitcast.219), channel_id=1, source_target_pairs={{0,32},{4,36},{8,40},{12,44},{16,0},{20,4},{24,8},{28,12},{32,16},... | collective-permute-start | bytes 516104 | tf_op jit(solution)/shard_map/ppermute | solution.py:16
  255.3 1.9 collective-permute-start.30
  257.2 1.6 collective-permute-done.13
  258.8 9.3 %collective-permute-done.12 = bf16[2,24,1792]{2,1,0:T(8,128)(2,1)S(1)} collective-permute-done((bf16[2,24,1792]{2,1,0:T(8,128)(2,1)S(1)}, bf16[2,24,1792]{2,1,0:T(8,128)(2,1)S(1)}, u32[]{:S(2)}, u32[]{:S(2)}) %collective-permute-start.12) | collective-permute-done | bytes 172064 | tf_op jit(solution)/shard_map/ppermute | solution.py:16
  268.2 1.9 collective-permute-start.14
  270.5 2.4 collective-permute-start.31
  273.0 5.3 %collective-permute-done.14 = bf16[3,24,1792]{2,1,0:T(8,128)(2,1)S(1)} collective-permute-done((bf16[3,24,1792]{2,1,0:T(8,128)(2,1)S(1)}, bf16[3,24,1792]{2,1,0:T(8,128)(2,1)S(1)}, u32[]{:S(2)}, u32[]{:S(2)}) %collective-permute-start.14) | collective-permute-done | bytes 258080 | tf_op jit(solution)/shard_map/ppermute | solution.py:20
  278.3 0.6 copy-done.8
  279.3 2.6 collective-permute-start.15
  281.9 3.0 %collective-permute-done.31 = bf16[128,1792]{1,0:T(8,128)(2,1)S(1)} collective-permute-done((bf16[128,1792]{1,0:T(8,128)(2,1)S(1)}, bf16[128,1792]{1,0:T(8,128)(2,1)S(1)}, u32[]{:S(2)}, u32[]{:S(2)}) %collective-permute-start.31) | collective-permute-done | bytes 458784 | tf_op jit(solution)/shard_map/ppermute | solution.py:169
  284.9 9.1 %collective-permute-done.15 = bf16[128,1792]{1,0:T(8,128)(2,1)S(1)} collective-permute-done((bf16[128,1792]{1,0:T(8,128)(2,1)S(1)}, bf16[128,1792]{1,0:T(8,128)(2,1)S(1)}, u32[]{:S(2)}, u32[]{:S(2)}) %collective-permute-start.15) | collective-permute-done | bytes 458784 | tf_op jit(solution)/shard_map/ppermute | solution.py:168
  294.0 0.8 copy.40
  294.7 0.8 copy.41
  (96 shorter events, 12.3 us)
Async XLA Ops:
  0.6 48.5 %copy-start = (bf16[1,1792,256]{2,1,0:T(8,128)(2,1)S(1)}, bf16[1,1792,256]{2,1,0:T(8,128)(2,1)}, u32[]{:S(2)}) copy-start(bf16[1,1792,256]{2,1,0:T(8,128)(2,1)} %param.18) | copy-start | bytes 2752516
  0.8 0.7 copy-start.5
  0.8 0.8 copy-start.6
  3.7 2.9 copy-start.3
  3.8 11.1 %collective-permute-start = (bf16[3,24,1792]{2,1,0:T(8,128)(2,1)S(1)}, bf16[3,24,1792]{2,1,0:T(8,128)(2,1)S(1)}, u32[]{:S(2)}, u32[]{:S(2)}) collective-permute-start(bf16[3,24,1792]{2,1,0:T(8,128)(2,1)S(1)} %bitcast.212), channel_id=1, source_target_pairs={{0,48},{48,0},{1,49},{49,1},{2,50},{50,2},{3,51},{51,3},{4,52},{52... | collective-permute-start | bytes 774152 | tf_op jit(solution)/shard_map/ppermute | solution.py:20
  6.6 0.7 copy-start.7
  7.7 3.4 %copy-start.4 = (bf16[1,528,2,256]{3,2,1,0:T(2,128)(2,1)S(1)}, bf16[1,528,2,256]{3,2,1,0:T(2,128)(2,1)}, u32[]{:S(2)}) copy-start(bf16[1,528,2,256]{3,2,1,0:T(2,128)(2,1)} %param.16) | copy-start | bytes 1622020
  7.7 22.8 %collective-permute-start.16 = (bf16[3,24,1792]{2,1,0:T(8,128)(2,1)S(1)}, bf16[3,24,1792]{2,1,0:T(8,128)(2,1)S(1)}, u32[]{:S(2)}, u32[]{:S(2)}) collective-permute-start(bf16[3,24,1792]{2,1,0:T(8,128)(2,1)S(1)} %bitcast.211), channel_id=1, source_target_pairs={{0,48},{48,0},{1,49},{49,1},{2,50},{50,2},{3,51},{51,3},{4,52},{52... | collective-permute-start | bytes 774152 | tf_op jit(solution)/shard_map/ppermute | solution.py:20
  14.9 25.4 %collective-permute-start.2 = (bf16[48,1792]{1,0:T(8,128)(2,1)S(1)}, bf16[48,1792]{1,0:T(8,128)(2,1)S(1)}, u32[]{:S(2)}, u32[]{:S(2)}) collective-permute-start(bf16[48,1792]{1,0:T(8,128)(2,1)S(1)} %get-tuple-element.32), channel_id=1, source_target_pairs={{0,16},{4,20},{8,24},{12,28},{16,32},{20,36},{24,40},{28,44},{32,0... | collective-permute-start | bytes 516104 | tf_op jit(solution)/shard_map/ppermute | solution.py:16
  25.8 15.1 %collective-permute-start.1 = (bf16[48,1792]{1,0:T(8,128)(2,1)S(1)}, bf16[48,1792]{1,0:T(8,128)(2,1)S(1)}, u32[]{:S(2)}, u32[]{:S(2)}) collective-permute-start(bf16[48,1792]{1,0:T(8,128)(2,1)S(1)} %get-tuple-element.33), channel_id=1, source_target_pairs={{0,32},{4,36},{8,40},{12,44},{16,0},{20,4},{24,8},{28,12},{32,16},... | collective-permute-start | bytes 516104 | tf_op jit(solution)/shard_map/ppermute | solution.py:16
  30.6 18.9 %collective-permute-start.18 = (bf16[48,1792]{1,0:T(8,128)(2,1)S(1)}, bf16[48,1792]{1,0:T(8,128)(2,1)S(1)}, u32[]{:S(2)}, u32[]{:S(2)}) collective-permute-start(bf16[48,1792]{1,0:T(8,128)(2,1)S(1)} %get-tuple-element.22), channel_id=1, source_target_pairs={{0,16},{4,20},{8,24},{12,28},{16,32},{20,36},{24,40},{28,44},{32,0... | collective-permute-start | bytes 516104 | tf_op jit(solution)/shard_map/ppermute | solution.py:16
  35.7 17.3 %collective-permute-start.17 = (bf16[48,1792]{1,0:T(8,128)(2,1)S(1)}, bf16[48,1792]{1,0:T(8,128)(2,1)S(1)}, u32[]{:S(2)}, u32[]{:S(2)}) collective-permute-start(bf16[48,1792]{1,0:T(8,128)(2,1)S(1)} %get-tuple-element.23), channel_id=1, source_target_pairs={{0,32},{4,36},{8,40},{12,44},{16,0},{20,4},{24,8},{28,12},{32,16},... | collective-permute-start | bytes 516104 | tf_op jit(solution)/shard_map/ppermute | solution.py:16
  41.0 22.6 %copy-start.1 = (bf16[1,1792,256]{2,1,0:T(8,128)(2,1)S(1)}, bf16[1,1792,256]{2,1,0:T(8,128)(2,1)}, u32[]{:S(2)}) copy-start(bf16[1,1792,256]{2,1,0:T(8,128)(2,1)} %param.17) | copy-start | bytes 2752516
  41.0 27.1 %collective-permute-start.3 = (bf16[144,1792]{1,0:T(8,128)(2,1)S(1)}, bf16[144,1792]{1,0:T(8,128)(2,1)S(1)}, u32[]{:S(2)}, u32[]{:S(2)}) collective-permute-start(bf16[144,1792]{1,0:T(8,128)(2,1)S(1)} %bitcast.193), channel_id=1, source_target_pairs={{0,4},{4,8},{8,12},{12,0},{1,5},{5,9},{9,13},{13,1},{2,6},{6,10},{... | collective-permute-start | bytes 1548296 | tf_op jit(solution)/shard_map/ppermute | solution.py:38
  53.1 10.8 %copy-start.2 = (bf16[1,256,1792]{2,1,0:T(8,128)(2,1)S(1)}, bf16[1,256,1792]{2,1,0:T(8,128)(2,1)}, u32[]{:S(2)}) copy-start(bf16[1,256,1792]{2,1,0:T(8,128)(2,1)} %param.19) | copy-start | bytes 2752516
  53.1 34.5 %collective-permute-start.19 = (bf16[144,1792]{1,0:T(8,128)(2,1)S(1)}, bf16[144,1792]{1,0:T(8,128)(2,1)S(1)}, u32[]{:S(2)}, u32[]{:S(2)}) collective-permute-start(bf16[144,1792]{1,0:T(8,128)(2,1)S(1)} %bitcast.196), channel_id=1, source_target_pairs={{0,12},{4,0},{8,4},{12,8},{1,13},{5,1},{9,5},{13,9},{2,14},{6,2},{... | collective-permute-start | bytes 1548296 | tf_op jit(solution)/shard_map/ppermute | solution.py:38
  68.0 38.6 %collective-permute-start.4 = (bf16[144,1792]{1,0:T(8,128)(2,1)S(1)}, bf16[144,1792]{1,0:T(8,128)(2,1)S(1)}, u32[]{:S(2)}, u32[]{:S(2)}) collective-permute-start(bf16[144,1792]{1,0:T(8,128)(2,1)S(1)} %collective-permute-done.3), channel_id=1, source_target_pairs={{0,4},{4,8},{8,12},{12,0},{1,5},{5,9},{9,13},{13,1},{2,6},{6,10},{... | collective-permute-start | bytes 1548296 | tf_op jit(solution)/shard_map/ppermute | solution.py:38
  87.6 25.0 %collective-permute-start.20 = (bf16[144,1792]{1,0:T(8,128)(2,1)S(1)}, bf16[144,1792]{1,0:T(8,128)(2,1)S(1)}, u32[]{:S(2)}, u32[]{:S(2)}) collective-permute-start(bf16[144,1792]{1,0:T(8,128)(2,1)S(1)} %collective-permute-done.19), channel_id=1, source_target_pairs={{0,12},{4,0},{8,4},{12,8},{1,13},{5,1},{9,5},{13,9},{2,14},{6,2},{... | collective-permute-start | bytes 1548296 | tf_op jit(solution)/shard_map/ppermute | solution.py:38
  106.6 28.3 %collective-permute-start.5 = (bf16[144,1792]{1,0:T(8,128)(2,1)S(1)}, bf16[144,1792]{1,0:T(8,128)(2,1)S(1)}, u32[]{:S(2)}, u32[]{:S(2)}) collective-permute-start(bf16[144,1792]{1,0:T(8,128)(2,1)S(1)} %collective-permute-done.4), channel_id=1, source_target_pairs={{0,4},{4,8},{8,12},{12,0},{1,5},{5,9},{9,13},{13,1},{2,6},{6,10},{... | collective-permute-start | bytes 1548296 | tf_op jit(solution)/shard_map/ppermute | solution.py:38
  112.6 19.9 %collective-permute-start.21 = (bf16[144,1792]{1,0:T(8,128)(2,1)S(1)}, bf16[144,1792]{1,0:T(8,128)(2,1)S(1)}, u32[]{:S(2)}, u32[]{:S(2)}) collective-permute-start(bf16[144,1792]{1,0:T(8,128)(2,1)S(1)} %collective-permute-done.20), channel_id=1, source_target_pairs={{0,12},{4,0},{8,4},{12,8},{1,13},{5,1},{9,5},{13,9},{2,14},{6,2},{... | collective-permute-start | bytes 1548296 | tf_op jit(solution)/shard_map/ppermute | solution.py:38
  133.0 5.1 %collective-permute-start.22 = (f32[288,256]{1,0:T(8,128)S(1)}, f32[288,256]{1,0:T(8,128)S(1)}, u32[]{:S(2)}, u32[]{:S(2)}) collective-permute-start(f32[288,256]{1,0:T(8,128)S(1)} %fusion.60), channel_id=1, source_target_pairs={{0,1},{1,0},{2,3},{3,2},{4,5},{5,4},{6,7},{7,6},{8,9},{9,8},{10,11... | collective-permute-start | bytes 884744 | tf_op jit(solution)/shard_map/ppermute | solution.py:20
  135.6 13.8 %collective-permute-start.6 = (f32[288,512]{1,0:T(8,128)S(1)}, f32[288,512]{1,0:T(8,128)S(1)}, u32[]{:S(2)}, u32[]{:S(2)}) collective-permute-start(f32[288,512]{1,0:T(8,128)S(1)} %fusion.49), channel_id=1, source_target_pairs={{0,1},{1,0},{2,3},{3,2},{4,5},{5,4},{6,7},{7,6},{8,9},{9,8},{10,11... | collective-permute-start | bytes 1769480 | tf_op jit(solution)/shard_map/ppermute | solution.py:20
  138.1 9.2 %collective-permute-start.23 = (bf16[288,256]{1,0:T(8,128)(2,1)S(1)}, bf16[288,256]{1,0:T(8,128)(2,1)S(1)}, u32[]{:S(2)}, u32[]{:S(2)}) collective-permute-start(bf16[288,256]{1,0:T(8,128)(2,1)S(1)} %get-tuple-element.2), channel_id=1, source_target_pairs={{0,2},{2,0},{1,3},{3,1},{4,6},{6,4},{5,7},{7,5},{8,10},{10,8},{9,1... | collective-permute-start | bytes 442376 | tf_op jit(solution)/shard_map/ppermute | solution.py:20
  147.5 5.5 %collective-permute-start.24 = (bf16[288,512]{1,0:T(8,128)(2,1)S(1)}, bf16[288,512]{1,0:T(8,128)(2,1)S(1)}, u32[]{:S(2)}, u32[]{:S(2)}) collective-permute-start(bf16[288,512]{1,0:T(8,128)(2,1)S(1)} %pad_maximum_fusion.8), channel_id=1, source_target_pairs={{0,1},{1,0},{2,3},{3,2},{4,5},{5,4},{6,7},{7,6},{8,9},{9,8},{10,11... | collective-permute-start | bytes 884744 | tf_op jit(solution)/shard_map/ppermute | solution.py:20
  149.6 12.8 %collective-permute-start.7 = (bf16[288,512]{1,0:T(8,128)(2,1)S(1)}, bf16[288,512]{1,0:T(8,128)(2,1)S(1)}, u32[]{:S(2)}, u32[]{:S(2)}) collective-permute-start(bf16[288,512]{1,0:T(8,128)(2,1)S(1)} %get-tuple-element.4), channel_id=1, source_target_pairs={{0,2},{2,0},{1,3},{3,1},{4,6},{6,4},{5,7},{7,5},{8,10},{10,8},{9,1... | collective-permute-start | bytes 884744 | tf_op jit(solution)/shard_map/ppermute | solution.py:20
  154.5 16.0 %collective-permute-start.25 = (bf16[144,1792]{1,0:T(8,128)(2,1)S(1)}, bf16[144,1792]{1,0:T(8,128)(2,1)S(1)}, u32[]{:S(2)}, u32[]{:S(2)}) collective-permute-start(bf16[144,1792]{1,0:T(8,128)(2,1)S(1)} %fusion), channel_id=1, source_target_pairs={{0,4},{4,8},{8,12},{12,0},{1,5},{5,9},{9,13},{13,1},{2,6},{6,10},{... | collective-permute-start | bytes 1548296 | tf_op jit(solution)/shard_map/ppermute | solution.py:38
  162.6 3.3 %collective-permute-start.8 = (bf16[288,256]{1,0:T(8,128)(2,1)S(1)}, bf16[288,256]{1,0:T(8,128)(2,1)S(1)}, u32[]{:S(2)}, u32[]{:S(2)}) collective-permute-start(bf16[288,256]{1,0:T(8,128)(2,1)S(1)} %fusion.58), channel_id=1, source_target_pairs={{0,1},{1,0},{2,3},{3,2},{4,5},{5,4},{6,7},{7,6},{8,9},{9,8},{10,11... | collective-permute-start | bytes 442376 | tf_op jit(solution)/shard_map/ppermute | solution.py:20
  166.3 18.1 %collective-permute-start.9 = (bf16[144,1792]{1,0:T(8,128)(2,1)S(1)}, bf16[144,1792]{1,0:T(8,128)(2,1)S(1)}, u32[]{:S(2)}, u32[]{:S(2)}) collective-permute-start(bf16[144,1792]{1,0:T(8,128)(2,1)S(1)} %convolution_convert_fusion.4), channel_id=1, source_target_pairs={{0,12},{4,0},{8,4},{12,8},{1,13},{5,1},{9,5},{13,9},{2,14},{6,2},{... | collective-permute-start | bytes 1548296 | tf_op jit(solution)/shard_map/ppermute | solution.py:38
  170.7 23.1 %collective-permute-start.26 = (bf16[144,1792]{1,0:T(8,128)(2,1)S(1)}, bf16[144,1792]{1,0:T(8,128)(2,1)S(1)}, u32[]{:S(2)}, u32[]{:S(2)}) collective-permute-start(bf16[144,1792]{1,0:T(8,128)(2,1)S(1)} %add.214), channel_id=1, source_target_pairs={{0,4},{4,8},{8,12},{12,0},{1,5},{5,9},{9,13},{13,1},{2,6},{6,10},{... | collective-permute-start | bytes 1548296 | tf_op jit(solution)/shard_map/ppermute | solution.py:38
  184.5 22.0 %collective-permute-start.10 = (bf16[144,1792]{1,0:T(8,128)(2,1)S(1)}, bf16[144,1792]{1,0:T(8,128)(2,1)S(1)}, u32[]{:S(2)}, u32[]{:S(2)}) collective-permute-start(bf16[144,1792]{1,0:T(8,128)(2,1)S(1)} %add.197), channel_id=1, source_target_pairs={{0,12},{4,0},{8,4},{12,8},{1,13},{5,1},{9,5},{13,9},{2,14},{6,2},{... | collective-permute-start | bytes 1548296 | tf_op jit(solution)/shard_map/ppermute | solution.py:38
  193.9 22.0 %collective-permute-start.27 = (bf16[144,1792]{1,0:T(8,128)(2,1)S(1)}, bf16[144,1792]{1,0:T(8,128)(2,1)S(1)}, u32[]{:S(2)}, u32[]{:S(2)}) collective-permute-start(bf16[144,1792]{1,0:T(8,128)(2,1)S(1)} %add.216), channel_id=1, source_target_pairs={{0,4},{4,8},{8,12},{12,0},{1,5},{5,9},{9,13},{13,1},{2,6},{6,10},{... | collective-permute-start | bytes 1548296 | tf_op jit(solution)/shard_map/ppermute | solution.py:38
  206.6 38.7 %collective-permute-start.11 = (bf16[144,1792]{1,0:T(8,128)(2,1)S(1)}, bf16[144,1792]{1,0:T(8,128)(2,1)S(1)}, u32[]{:S(2)}, u32[]{:S(2)}) collective-permute-start(bf16[144,1792]{1,0:T(8,128)(2,1)S(1)} %add.198), channel_id=1, source_target_pairs={{0,12},{4,0},{8,4},{12,8},{1,13},{5,1},{9,5},{13,9},{2,14},{6,2},{... | collective-permute-start | bytes 1548296 | tf_op jit(solution)/shard_map/ppermute | solution.py:38
  216.2 25.3 %collective-permute-start.29 = (bf16[2,24,1792]{2,1,0:T(8,128)(2,1)S(1)}, bf16[2,24,1792]{2,1,0:T(8,128)(2,1)S(1)}, u32[]{:S(2)}, u32[]{:S(2)}) collective-permute-start(bf16[2,24,1792]{2,1,0:T(8,128)(2,1)S(1)} %bitcast.225), channel_id=1, source_target_pairs={{0,16},{4,20},{8,24},{12,28},{16,32},{20,36},{24,40},{28,44},{32,0... | collective-permute-start | bytes 516104 | tf_op jit(solution)/shard_map/ppermute | solution.py:16
  221.3 23.9 %collective-permute-start.28 = (bf16[2,24,1792]{2,1,0:T(8,128)(2,1)S(1)}, bf16[2,24,1792]{2,1,0:T(8,128)(2,1)S(1)}, u32[]{:S(2)}, u32[]{:S(2)}) collective-permute-start(bf16[2,24,1792]{2,1,0:T(8,128)(2,1)S(1)} %bitcast.223), channel_id=1, source_target_pairs={{0,32},{4,36},{8,40},{12,44},{16,0},{20,4},{24,8},{28,12},{32,16},... | collective-permute-start | bytes 516104 | tf_op jit(solution)/shard_map/ppermute | solution.py:16
  245.5 13.3 %collective-permute-start.13 = (bf16[2,24,1792]{2,1,0:T(8,128)(2,1)S(1)}, bf16[2,24,1792]{2,1,0:T(8,128)(2,1)S(1)}, u32[]{:S(2)}, u32[]{:S(2)}) collective-permute-start(bf16[2,24,1792]{2,1,0:T(8,128)(2,1)S(1)} %bitcast.221), channel_id=1, source_target_pairs={{0,16},{4,20},{8,24},{12,28},{16,32},{20,36},{24,40},{28,44},{32,0... | collective-permute-start | bytes 516104 | tf_op jit(solution)/shard_map/ppermute | solution.py:16
  251.4 16.7 %collective-permute-start.12 = (bf16[2,24,1792]{2,1,0:T(8,128)(2,1)S(1)}, bf16[2,24,1792]{2,1,0:T(8,128)(2,1)S(1)}, u32[]{:S(2)}, u32[]{:S(2)}) collective-permute-start(bf16[2,24,1792]{2,1,0:T(8,128)(2,1)S(1)} %bitcast.219), channel_id=1, source_target_pairs={{0,32},{4,36},{8,40},{12,44},{16,0},{20,4},{24,8},{28,12},{32,16},... | collective-permute-start | bytes 516104 | tf_op jit(solution)/shard_map/ppermute | solution.py:16
  255.3 14.8 %collective-permute-start.30 = (bf16[3,24,1792]{2,1,0:T(8,128)(2,1)S(1)}, bf16[3,24,1792]{2,1,0:T(8,128)(2,1)S(1)}, u32[]{:S(2)}, u32[]{:S(2)}) collective-permute-start(bf16[3,24,1792]{2,1,0:T(8,128)(2,1)S(1)} %get-tuple-element.17), channel_id=1, source_target_pairs={{0,48},{48,0},{1,49},{49,1},{2,50},{50,2},{3,51},{51,3},{4,52},{52... | collective-permute-start | bytes 774152 | tf_op jit(solution)/shard_map/ppermute | solution.py:20
  268.2 10.0 %collective-permute-start.14 = (bf16[3,24,1792]{2,1,0:T(8,128)(2,1)S(1)}, bf16[3,24,1792]{2,1,0:T(8,128)(2,1)S(1)}, u32[]{:S(2)}, u32[]{:S(2)}) collective-permute-start(bf16[3,24,1792]{2,1,0:T(8,128)(2,1)S(1)} %get-tuple-element.27), channel_id=1, source_target_pairs={{0,48},{48,0},{1,49},{49,1},{2,50},{50,2},{3,51},{51,3},{4,52},{52... | collective-permute-start | bytes 774152 | tf_op jit(solution)/shard_map/ppermute | solution.py:20
  270.5 14.3 %collective-permute-start.31 = (bf16[128,1792]{1,0:T(8,128)(2,1)S(1)}, bf16[128,1792]{1,0:T(8,128)(2,1)S(1)}, u32[]{:S(2)}, u32[]{:S(2)}) collective-permute-start(bf16[128,1792]{1,0:T(8,128)(2,1)S(1)} %convolution_convert_fusion.6), channel_id=1, source_target_pairs={{96,0},{192,96},{288,192},{384,288},{480,384},{576,480},{672,576},... | collective-permute-start | bytes 1376264 | tf_op jit(solution)/shard_map/ppermute | solution.py:169
  278.3 0.7 copy-start.8
  279.3 14.7 %collective-permute-start.15 = (bf16[128,1792]{1,0:T(8,128)(2,1)S(1)}, bf16[128,1792]{1,0:T(8,128)(2,1)S(1)}, u32[]{:S(2)}, u32[]{:S(2)}) collective-permute-start(bf16[128,1792]{1,0:T(8,128)(2,1)S(1)} %fusion.4), channel_id=1, source_target_pairs={{0,96},{96,192},{192,288},{288,384},{384,480},{480,576},{576,672},... | collective-permute-start | bytes 1376264 | tf_op jit(solution)/shard_map/ppermute | solution.py:168

commit v3 on v2

--- a/solution.py
+++ b/solution.py
@@ -26,7 +26,7 @@
     near = [half * groups + (group + k) % groups for k in range(groups)]
     far = [(1 - half) * groups + (group + k) % groups for k in range(groups)]
     ids = jnp.stack(near + far).astype(jnp.int32)
-    member = (routes[None, :, 0] == ids[:, None]).astype(jnp.int32)
+    member = (routes[None, :] == ids[:, None]).astype(jnp.int32)
     before = jnp.cumsum(member, axis=1) - member
     slot_ids = jnp.arange(width, dtype=jnp.int32)
     hit = (before[:, None, :] == slot_ids[None, :, None]) & (slot_ids < capacity)[None, :, None]
@@ -38,24 +38,12 @@
     return lax.ppermute(values, "member", [(i, (i + step) % GROUP) for i in range(GROUP)])
 
 
-def dispatch(slots, step):
-    blocks = jnp.concatenate([slots[0], swap(slots[1], "half")], axis=1)
-    part = jnp.stack([blocks[0], hop(blocks[2], -GROUP), hop(blocks[1], GROUP)])
-    part = part.reshape(-1, slots.shape[-1])
-    parts = [part]
-    for _ in range(1, GROUP):
-        part = around(part, step)
-        parts.append(part)
-    return parts
-
-
-def collect(parts, step, groups):
-    total = parts[GROUP - 1]
-    for k in range(GROUP - 2, -1, -1):
-        total = around(total, -step) + parts[k]
-    total = total.reshape(groups, 2, -1, total.shape[-1])
-    blocks = jnp.stack([total[0], hop(total[2], -GROUP), hop(total[1], GROUP)])
-    return jnp.stack([blocks[:, 0], swap(blocks[:, 1], "half")])
+def widen(slots):
+    return jnp.concatenate([slots[0], swap(slots[1], "half")], axis=1)
+
+
+def shift_groups(blocks):
+    return blocks[0], hop(blocks[2], -GROUP), hop(blocks[1], GROUP)
 
 
 def reduce_rows(parts):
@@ -116,14 +104,38 @@
     columns = tokens_fwd.shape[2]
     hidden_width = w_gate.shape[2]
 
-    place_fwd = placing_of(routes_fwd[0], capacity, width)
-    place_bwd = placing_of(routes_bwd[0], capacity, width)
+    together = lax.optimization_barrier
+    place_fwd = placing_of(routes_fwd[0, :, 0], capacity, width)
+    place_bwd = placing_of(routes_bwd[0, :, 0], capacity, width)
     send_fwd = jnp.dot(place_fwd, tokens_fwd[0], preferred_element_type=F32).astype(BF16)
     scaled = (cotangent[0].astype(F32) * gates_bwd[0]).astype(BF16)
     send_bwd = jnp.dot(place_bwd, scaled, preferred_element_type=F32).astype(BF16)
 
-    got_fwd = dispatch(send_fwd.reshape(2, groups, width, columns), 1)
-    got_bwd = dispatch(send_bwd.reshape(2, groups, width, columns), -1)
+    def flat(blocks):
+        return blocks.reshape(-1, columns)
+
+    fwd = widen(send_fwd.reshape(2, groups, width, columns))
+    fwd, bwd = together((shift_groups(fwd), widen(send_bwd.reshape(2, groups, width, columns))))
+    got_fwd = [flat(jnp.stack(fwd))]
+
+    sections = lax.axis_size("section")
+    up = [(i, i + 1) for i in range(sections - 1)]
+    down = [(i + 1, i) for i in range(sections - 1)]
+    send_up = jnp.stack([routes_fwd[0, :, 0].astype(F32), gates_fwd[0, :, 0]])
+    send_down = routes_bwd[0, :, 0].astype(F32)
+    bwd, send_up, send_down = together((bwd, send_up, send_down))
+    from_before = lax.ppermute(send_up, "section", up)
+    from_after = lax.ppermute(send_down, "section", down)
+
+    part, bwd = together((around(got_fwd[0], 1), shift_groups(bwd)))
+    got_fwd.append(part)
+    got_bwd = [flat(jnp.stack(bwd))]
+    for _ in range(2, GROUP):
+        part, bwd = together((around(got_fwd[-1], 1), around(got_bwd[-1], -1)))
+        got_fwd.append(part)
+        got_bwd.append(bwd)
+    last_bwd = around(got_bwd[-1], -1)
+
     partial_fwd = [
         jnp.concatenate(
             [
@@ -135,10 +147,13 @@
         for rows in got_fwd
     ]
     summed = reduce_rows(partial_fwd)
-    gate_pre, up_pre = summed[:, :hidden_width], summed[:, hidden_width:]
+    gate_pre, up_pre = jnp.split(summed, 2, axis=1)
     hidden = gather_rows((gate_pre * jax.nn.sigmoid(gate_pre) * up_pre).astype(BF16))
+    hidden, last_bwd, from_before, from_after = together(
+        (hidden, last_bwd, from_before, from_after)
+    )
+    got_bwd.append(last_bwd)
     out = [jnp.dot(rows, w_down[0], preferred_element_type=F32).astype(BF16) for rows in hidden]
-    back_fwd = collect(out, 1, groups).reshape(-1, columns)
 
     grad_hidden = reduce_rows([contract_last(rows, w_down[0]) for rows in got_bwd])
     saved = saved_half(saved_pre[0], capacity, width, -1)
@@ -148,6 +163,7 @@
     grad_gate = grad_hidden * pre_up * sigmoid_gate * (1.0 + pre_gate * (1.0 - sigmoid_gate))
     grad_up = grad_hidden * pre_gate * sigmoid_gate
     grads = gather_rows(jnp.concatenate([grad_gate, grad_up], axis=1).astype(BF16))
+    total, grads = together((around(out[GROUP - 1], -1), grads))
     grad_out = [
         (
             contract_last(rows[:, :hidden_width], w_gate[0])
@@ -155,19 +171,42 @@
         ).astype(BF16)
         for rows in grads
     ]
-    back_bwd = collect(grad_out, -1, groups).reshape(-1, columns)
+
+    total_bwd = grad_out[GROUP - 1]
+    for k in range(GROUP - 2, 0, -1):
+        total, total_bwd = together((around(total + out[k], -1), around(total_bwd, 1)))
+        total_bwd = total_bwd + grad_out[k]
+
+    def blocks_of(rows):
+        return rows.reshape(groups, 2 * width, columns)
+
+    total, total_bwd = together((shift_groups(blocks_of(total + out[0])), around(total_bwd, 1)))
+
+    def shifted(values, shift):
+        mine, others = values[:, :width], values[:, width:]
+        across = [(2 * i + h, 2 * j + 1 - h) for i, j in shift for h in range(2)]
+        mine = lax.ppermute(mine, "section", shift)
+        others = lax.ppermute(others, ("section", "half"), across)
+        return flat(mine), flat(others)
+
+    moved, total_bwd = together(
+        (shifted(jnp.stack(total), up), shift_groups(blocks_of(total_bwd + grad_out[0])))
+    )
 
     def rows_of(placing, values):
+        mine, others = values
+        cut = mine.shape[0]
         return lax.dot_general(
-            placing, values, (((0,), (0,)), ((), ())), preferred_element_type=F32
+            placing[:cut], mine, (((0,), (0,)), ((), ())), preferred_element_type=F32
+        ) + lax.dot_general(
+            placing[cut:], others, (((0,), (0,)), ((), ())), preferred_element_type=F32
         )
 
-    layer_out = (rows_of(place_fwd, back_fwd) * gates_fwd[0]).astype(BF16)
-    layer_grad = rows_of(place_bwd, back_bwd).astype(BF16)
-    ends = lax.axis_size("section") - 1
-    forwarded = lax.ppermute(layer_out, "section", [(i, i + 1) for i in range(ends)])
-    returned = lax.ppermute(layer_grad, "section", [(i + 1, i) for i in range(ends)])
-    return (forwarded[None], returned[None])
+    place_before = placing_of(from_before[0].astype(jnp.int32), capacity, width)
+    place_after = placing_of(from_after.astype(jnp.int32), capacity, width)
+    forwarded = rows_of(place_before, moved) * from_before[1][:, None]
+    returned = rows_of(place_after, shifted(jnp.stack(total_bwd), down))
+    return (forwarded.astype(BF16)[None], returned.astype(BF16)[None])
 
 
 def solution(mesh):

time: 297 us -> 330 us (1.11)
  the two profiles are of different devices: /device:TPU:102 before, /device:TPU:88 now
where the time goes in v3:
time: 330 us; the launch traced here: 329 us
  waiting for transfers between devices  164 us (50%)
  starting transfers between devices  134 us (41%)
  matrix products  15.6 us (5%)
  other arithmetic  9.1 us (3%)
  local copies, waits for them, and re-layouts  5.1 us (2%)
    ppermute x12, waiting for transfers between devices, around(): lax.ppermute(values, 'member', [(i, (i + step) % GROUP) for i in range(GR...  98.1 us
    ppermute x12, starting transfers between devices, around(): lax.ppermute(values, 'member', [(i, (i + step) % GROUP) for i in range(GR...  48.2 us
    ppermute x8, starting transfers between devices, hop(): lax.ppermute(values, RING, [(i, (i + step) % count) for i in range(count)])  45 us
    ppermute x8, waiting for transfers between devices, hop(): lax.ppermute(values, RING, [(i, (i + step) % count) for i in range(count)])  43.5 us
    ppermute x8, starting transfers between devices, swap(): return lax.ppermute(values, axis, [(0, 1), (1, 0)])  21.1 us
    ppermute x8, waiting for transfers between devices, swap(): return lax.ppermute(values, axis, [(0, 1), (1, 0)])  12.5 us
    ppermute x2, waiting for transfers between devices, shifted(): others = lax.ppermute(others, ('section', 'half'), across)  9.75 us
    ppermute x2, starting transfers between devices, shifted(): others = lax.ppermute(others, ('section', 'half'), across)  6.74 us
  transfers between devices with their start and end apart: 34, of which 23 were waited for; matrix products, arithmetic and copies ran while one was open for 7% of the time, Pallas kernels for 0%

profile of v3, /device:TPU:88, one launch (start us, length us, event | category | flops | bytes accessed | tf_op | source)
XLA Modules:
  0.0 329.2 jit_solution(1084904311332501544)
XLA Ops:
  2.4 1.3 convolution_convert_fusion.5
  3.8 3.5 %collective-permute-start = (bf16[3,24,1792]{2,1,0:T(8,128)(2,1)S(1)}, bf16[3,24,1792]{2,1,0:T(8,128)(2,1)S(1)}, u32[]{:S(2)}, u32[]{:S(2)}) collective-permute-start(bf16[3,24,1792]{2,1,0:T(8,128)(2,1)S(1)} %bitcast.221), channel_id=1, source_target_pairs={{0,48},{48,0},{1,49},{49,1},{2,50},{50,2},{3,51},{51,3},{4,52},{52... | collective-permute-start | bytes 774152 | tf_op jit(solution)/shard_map/ppermute | solution.py:20
  8.4 2.6 collective-permute-start.3
  13.9 1.0 collective-permute-done
  14.9 10.9 %collective-permute-start.2 = (bf16[48,1792]{1,0:T(8,128)(2,1)S(1)}, bf16[48,1792]{1,0:T(8,128)(2,1)S(1)}, u32[]{:S(2)}, u32[]{:S(2)}) collective-permute-start(bf16[48,1792]{1,0:T(8,128)(2,1)S(1)} %get-tuple-element.111), channel_id=1, source_target_pairs={{0,16},{4,20},{8,24},{12,28},{16,32},{20,36},{24,40},{28,44},{32,0... | collective-permute-start | bytes 516104 | tf_op jit(solution)/shard_map/ppermute | solution.py:16
  25.9 4.7 %collective-permute-start.1 = (bf16[48,1792]{1,0:T(8,128)(2,1)S(1)}, bf16[48,1792]{1,0:T(8,128)(2,1)S(1)}, u32[]{:S(2)}, u32[]{:S(2)}) collective-permute-start(bf16[48,1792]{1,0:T(8,128)(2,1)S(1)} %get-tuple-element.113), channel_id=1, source_target_pairs={{0,32},{4,36},{8,40},{12,44},{16,0},{20,4},{24,8},{28,12},{32,16},... | collective-permute-start | bytes 516104 | tf_op jit(solution)/shard_map/ppermute | solution.py:16
  30.6 4.8 %collective-permute-done.2 = bf16[48,1792]{1,0:T(8,128)(2,1)S(1)} collective-permute-done((bf16[48,1792]{1,0:T(8,128)(2,1)S(1)}, bf16[48,1792]{1,0:T(8,128)(2,1)S(1)}, u32[]{:S(2)}, u32[]{:S(2)}) %collective-permute-start.2) | collective-permute-done | bytes 172064 | tf_op jit(solution)/shard_map/ppermute | solution.py:16
  35.4 6.0 %collective-permute-done.1 = bf16[48,1792]{1,0:T(8,128)(2,1)S(1)} collective-permute-done((bf16[48,1792]{1,0:T(8,128)(2,1)S(1)}, bf16[48,1792]{1,0:T(8,128)(2,1)S(1)}, u32[]{:S(2)}, u32[]{:S(2)}) %collective-permute-start.1) | collective-permute-done | bytes 172064 | tf_op jit(solution)/shard_map/ppermute | solution.py:16
  41.4 7.6 %collective-permute-start.6 = (bf16[48,1792]{1,0:T(8,128)(2,1)S(1)}, bf16[48,1792]{1,0:T(8,128)(2,1)S(1)}, u32[]{:S(2)}, u32[]{:S(2)}) collective-permute-start(bf16[48,1792]{1,0:T(8,128)(2,1)S(1)} %get-tuple-element.106), channel_id=1, source_target_pairs={{0,16},{4,20},{8,24},{12,28},{16,32},{20,36},{24,40},{28,44},{32,0... | collective-permute-start | bytes 516104 | tf_op jit(solution)/shard_map/ppermute | solution.py:16
  49.0 2.3 collective-permute-start.5
  51.4 6.3 %collective-permute-start.4 = (bf16[144,1792]{1,0:T(8,128)(2,1)S(1)}, bf16[144,1792]{1,0:T(8,128)(2,1)S(1)}, u32[]{:S(2)}, u32[]{:S(2)}) collective-permute-start(bf16[144,1792]{1,0:T(8,128)(2,1)S(1)} %bitcast.208), channel_id=1, source_target_pairs={{0,4},{4,8},{8,12},{12,0},{1,5},{5,9},{9,13},{13,1},{2,6},{6,10},{... | collective-permute-start | bytes 1548296 | tf_op jit(solution)/shard_map/ppermute | solution.py:38
  58.4 3.5 %collective-permute-done.5 = bf16[48,1792]{1,0:T(8,128)(2,1)S(1)} collective-permute-done((bf16[48,1792]{1,0:T(8,128)(2,1)S(1)}, bf16[48,1792]{1,0:T(8,128)(2,1)S(1)}, u32[]{:S(2)}, u32[]{:S(2)}) %collective-permute-start.5) | collective-permute-done | bytes 172064 | tf_op jit(solution)/shard_map/ppermute | solution.py:16
  61.9 12.0 %collective-permute-done.4 = bf16[144,1792]{1,0:T(8,128)(2,1)S(1)} collective-permute-done((bf16[144,1792]{1,0:T(8,128)(2,1)S(1)}, bf16[144,1792]{1,0:T(8,128)(2,1)S(1)}, u32[]{:S(2)}, u32[]{:S(2)}) %collective-permute-start.4) | collective-permute-done | bytes 516128 | tf_op jit(solution)/shard_map/ppermute | solution.py:38
  74.0 9.8 %collective-permute-start.8 = (bf16[144,1792]{1,0:T(8,128)(2,1)S(1)}, bf16[144,1792]{1,0:T(8,128)(2,1)S(1)}, u32[]{:S(2)}, u32[]{:S(2)}) collective-permute-start(bf16[144,1792]{1,0:T(8,128)(2,1)S(1)} %bitcast.211), channel_id=1, source_target_pairs={{0,12},{4,0},{8,4},{12,8},{1,13},{5,1},{9,5},{13,9},{2,14},{6,2},{... | collective-permute-start | bytes 1548296 | tf_op jit(solution)/shard_map/ppermute | solution.py:38
  83.8 1.9 collective-permute-start.7
  86.4 19.6 %collective-permute-done.8 = bf16[144,1792]{1,0:T(8,128)(2,1)S(1)} collective-permute-done((bf16[144,1792]{1,0:T(8,128)(2,1)S(1)}, bf16[144,1792]{1,0:T(8,128)(2,1)S(1)}, u32[]{:S(2)}, u32[]{:S(2)}) %collective-permute-start.8) | collective-permute-done | bytes 516128 | tf_op jit(solution)/shard_map/ppermute | solution.py:38
  106.0 0.8 collective-permute-done.7
  106.8 3.5 %collective-permute-start.10 = (bf16[144,1792]{1,0:T(8,128)(2,1)S(1)}, bf16[144,1792]{1,0:T(8,128)(2,1)S(1)}, u32[]{:S(2)}, u32[]{:S(2)}) collective-permute-start(bf16[144,1792]{1,0:T(8,128)(2,1)S(1)} %collective-permute-done.8), channel_id=1, source_target_pairs={{0,12},{4,0},{8,4},{12,8},{1,13},{5,1},{9,5},{13,9},{2,14},{6,2},{... | collective-permute-start | bytes 1548296 | tf_op jit(solution)/shard_map/ppermute | solution.py:38
  110.4 2.3 collective-permute-start.9
  113.3 8.8 %collective-permute-done.10 = bf16[144,1792]{1,0:T(8,128)(2,1)S(1)} collective-permute-done((bf16[144,1792]{1,0:T(8,128)(2,1)S(1)}, bf16[144,1792]{1,0:T(8,128)(2,1)S(1)}, u32[]{:S(2)}, u32[]{:S(2)}) %collective-permute-start.10) | collective-permute-done | bytes 516128 | tf_op jit(solution)/shard_map/ppermute | solution.py:38
  122.0 11.9 %collective-permute-done.9 = bf16[144,1792]{1,0:T(8,128)(2,1)S(1)} collective-permute-done((bf16[144,1792]{1,0:T(8,128)(2,1)S(1)}, bf16[144,1792]{1,0:T(8,128)(2,1)S(1)}, u32[]{:S(2)}, u32[]{:S(2)}) %collective-permute-start.9) | collective-permute-done | bytes 516128 | tf_op jit(solution)/shard_map/ppermute | solution.py:38
  134.7 1.9 collective-permute-start.11
  138.5 1.7 pad.4
  140.2 2.3 collective-permute-start.16
  142.5 4.7 %collective-permute-start.15 = (f32[2,128]{1,0:T(2,128)S(1)}, f32[2,128]{1,0:T(2,128)S(1)}, u32[]{:S(2)}, u32[]{:S(2)}) collective-permute-start(f32[2,128]{1,0:T(2,128)S(1)} %pad_maximum_fusion.9), channel_id=1, source_target_pairs={{0,96},{96,192},{192,288},{288,384},{384,480},{480,576},{576,672},... | collective-permute-start | bytes 3080 | tf_op jit(solution)/shard_map/ppermute | solution.py:127
  147.4 4.9 %collective-permute-start.12 = (bf16[288,512]{1,0:T(8,128)(2,1)S(1)}, bf16[288,512]{1,0:T(8,128)(2,1)S(1)}, u32[]{:S(2)}, u32[]{:S(2)}) collective-permute-start(bf16[288,512]{1,0:T(8,128)(2,1)S(1)} %get-tuple-element.84), channel_id=1, source_target_pairs={{0,2},{2,0},{1,3},{3,1},{4,6},{6,4},{5,7},{7,5},{8,10},{10,8},{9,1... | collective-permute-start | bytes 884744 | tf_op jit(solution)/shard_map/ppermute | solution.py:20
  153.3 3.7 %collective-permute-start.14 = (bf16[144,1792]{1,0:T(8,128)(2,1)S(1)}, bf16[144,1792]{1,0:T(8,128)(2,1)S(1)}, u32[]{:S(2)}, u32[]{:S(2)}) collective-permute-start(bf16[144,1792]{1,0:T(8,128)(2,1)S(1)} %collective-permute-done.10), channel_id=1, source_target_pairs={{0,12},{4,0},{8,4},{12,8},{1,13},{5,1},{9,5},{13,9},{2,14},{6,2},{... | collective-permute-start | bytes 1548296 | tf_op jit(solution)/shard_map/ppermute | solution.py:38
  157.0 2.7 collective-permute-done.12
  159.8 1.9 collective-permute-start.13
  162.2 0.9 collective-permute-done.13
  163.9 4.6 %collective-permute-done.14 = bf16[144,1792]{1,0:T(8,128)(2,1)S(1)} collective-permute-done((bf16[144,1792]{1,0:T(8,128)(2,1)S(1)}, bf16[144,1792]{1,0:T(8,128)(2,1)S(1)}, u32[]{:S(2)}, u32[]{:S(2)}) %collective-permute-start.14) | collective-permute-done | bytes 516128 | tf_op jit(solution)/shard_map/ppermute | solution.py:38
  169.7 1.9 collective-permute-start.18
  171.7 1.1 convolution_convert_fusion.3
  173.7 3.8 %collective-permute-start.17 = (bf16[144,1792]{1,0:T(8,128)(2,1)}, bf16[144,1792]{1,0:T(8,128)(2,1)S(1)}, u32[]{:S(2)}, u32[]{:S(2)}) collective-permute-start(bf16[144,1792]{1,0:T(8,128)(2,1)} %convolution_convert_fusion.3), channel_id=1, source_target_pairs={{0,12},{4,0},{8,4},{12,8},{1,13},{5,1},{9,5},{13,9},{2,14},{6,2},{... | collective-permute-start | bytes 1548296 | tf_op jit(solution)/shard_map/ppermute | solution.py:38
  177.6 1.2 convolution_convert_fusion.1
  178.8 1.1 fusion.121
  179.9 2.4 collective-permute-start.19
  182.4 6.8 %collective-permute-done.19 = bf16[288,256]{1,0:T(8,128)(2,1)S(1)} collective-permute-done((bf16[288,256]{1,0:T(8,128)(2,1)S(1)}, bf16[288,256]{1,0:T(8,128)(2,1)S(1)}, u32[]{:S(2)}, u32[]{:S(2)}) %collective-permute-start.19) | collective-permute-done | bytes 147488 | tf_op jit(solution)/shard_map/ppermute | solution.py:20
  189.4 1.9 collective-permute-start.20
  191.8 1.1 collective-permute-done.20
  193.2 5.7 %collective-permute-start.21 = (bf16[144,1792]{1,0:T(8,128)(2,1)S(1)}, bf16[144,1792]{1,0:T(8,128)(2,1)S(1)}, u32[]{:S(2)}, u32[]{:S(2)}) collective-permute-start(bf16[144,1792]{1,0:T(8,128)(2,1)S(1)} %add.247), channel_id=1, source_target_pairs={{0,12},{4,0},{8,4},{12,8},{1,13},{5,1},{9,5},{13,9},{2,14},{6,2},{... | collective-permute-start | bytes 1548296 | tf_op jit(solution)/shard_map/ppermute | solution.py:38
  199.9 1.9 collective-permute-start.22
  203.2 18.1 %collective-permute-done.21 = bf16[144,1792]{1,0:T(8,128)(2,1)S(1)} collective-permute-done((bf16[144,1792]{1,0:T(8,128)(2,1)S(1)}, bf16[144,1792]{1,0:T(8,128)(2,1)S(1)}, u32[]{:S(2)}, u32[]{:S(2)}) %collective-permute-start.21) | collective-permute-done | bytes 516128 | tf_op jit(solution)/shard_map/ppermute | solution.py:38
  221.3 0.8 collective-permute-done.22
  222.3 3.6 %collective-permute-start.23 = (bf16[144,1792]{1,0:T(8,128)(2,1)S(1)}, bf16[144,1792]{1,0:T(8,128)(2,1)S(1)}, u32[]{:S(2)}, u32[]{:S(2)}) collective-permute-start(bf16[144,1792]{1,0:T(8,128)(2,1)S(1)} %add.249), channel_id=1, source_target_pairs={{0,12},{4,0},{8,4},{12,8},{1,13},{5,1},{9,5},{13,9},{2,14},{6,2},{... | collective-permute-start | bytes 1548296 | tf_op jit(solution)/shard_map/ppermute | solution.py:38
  226.0 2.3 collective-permute-start.24
  229.2 8.3 %collective-permute-done.23 = bf16[144,1792]{1,0:T(8,128)(2,1)S(1)} collective-permute-done((bf16[144,1792]{1,0:T(8,128)(2,1)S(1)}, bf16[144,1792]{1,0:T(8,128)(2,1)S(1)}, u32[]{:S(2)}, u32[]{:S(2)}) %collective-permute-start.23) | collective-permute-done | bytes 516128 | tf_op jit(solution)/shard_map/ppermute | solution.py:38
  237.5 13.1 %collective-permute-done.24 = bf16[144,1792]{1,0:T(8,128)(2,1)S(1)} collective-permute-done((bf16[144,1792]{1,0:T(8,128)(2,1)S(1)}, bf16[144,1792]{1,0:T(8,128)(2,1)S(1)}, u32[]{:S(2)}, u32[]{:S(2)}) %collective-permute-start.24) | collective-permute-done | bytes 516128 | tf_op jit(solution)/shard_map/ppermute | solution.py:38
  250.8 3.3 %collective-permute-start.27 = (bf16[144,1792]{1,0:T(8,128)(2,1)S(1)}, bf16[144,1792]{1,0:T(8,128)(2,1)S(1)}, u32[]{:S(2)}, u32[]{:S(2)}) collective-permute-start(bf16[144,1792]{1,0:T(8,128)(2,1)S(1)} %add.254), channel_id=1, source_target_pairs={{0,4},{4,8},{8,12},{12,0},{1,5},{5,9},{9,13},{13,1},{2,6},{6,10},{... | collective-permute-start | bytes 1548296 | tf_op jit(solution)/shard_map/ppermute | solution.py:38
  254.3 4.4 %collective-permute-start.26 = (bf16[48,1792]{1,0:T(8,128)(2,1)S(1)}, bf16[48,1792]{1,0:T(8,128)(2,1)S(1)}, u32[]{:S(2)}, u32[]{:S(2)}) collective-permute-start(bf16[48,1792]{1,0:T(8,128)(2,1)S(1)} %get-tuple-element.103), channel_id=1, source_target_pairs={{0,16},{4,20},{8,24},{12,28},{16,32},{20,36},{24,40},{28,44},{32,0... | collective-permute-start | bytes 516104 | tf_op jit(solution)/shard_map/ppermute | solution.py:16
  258.7 5.3 %collective-permute-start.25 = (bf16[48,1792]{1,0:T(8,128)(2,1)S(1)}, bf16[48,1792]{1,0:T(8,128)(2,1)S(1)}, u32[]{:S(2)}, u32[]{:S(2)}) collective-permute-start(bf16[48,1792]{1,0:T(8,128)(2,1)S(1)} %get-tuple-element.104), channel_id=1, source_target_pairs={{0,32},{4,36},{8,40},{12,44},{16,0},{20,4},{24,8},{28,12},{32,16},... | collective-permute-start | bytes 516104 | tf_op jit(solution)/shard_map/ppermute | solution.py:16
  264.5 15.5 %collective-permute-done.26 = bf16[48,1792]{1,0:T(8,128)(2,1)S(1)} collective-permute-done((bf16[48,1792]{1,0:T(8,128)(2,1)S(1)}, bf16[48,1792]{1,0:T(8,128)(2,1)S(1)}, u32[]{:S(2)}, u32[]{:S(2)}) %collective-permute-start.26) | collective-permute-done | bytes 172064 | tf_op jit(solution)/shard_map/ppermute | solution.py:16
  280.1 3.5 %collective-permute-done.25 = bf16[48,1792]{1,0:T(8,128)(2,1)S(1)} collective-permute-done((bf16[48,1792]{1,0:T(8,128)(2,1)S(1)}, bf16[48,1792]{1,0:T(8,128)(2,1)S(1)}, u32[]{:S(2)}, u32[]{:S(2)}) %collective-permute-start.25) | collective-permute-done | bytes 172064 | tf_op jit(solution)/shard_map/ppermute | solution.py:16
  283.7 3.5 %collective-permute-start.29 = (bf16[3,24,1792]{2,1,0:T(8,128)(2,1)S(1)}, bf16[3,24,1792]{2,1,0:T(8,128)(2,1)S(1)}, u32[]{:S(2)}, u32[]{:S(2)}) collective-permute-start(bf16[3,24,1792]{2,1,0:T(8,128)(2,1)S(1)} %get-tuple-element.101), channel_id=1, source_target_pairs={{0,144},{48,96},{96,240},{144,192},{192,336},{240,288},{288,432},{... | collective-permute-start | bytes 774152 | tf_op jit(solution)/shard_map/ppermute | solution.py:189
  287.2 2.6 collective-permute-start.28
  290.0 4.7 %collective-permute-start.31 = (bf16[48,1792]{1,0:T(8,128)(2,1)S(1)}, bf16[48,1792]{1,0:T(8,128)(2,1)S(1)}, u32[]{:S(2)}, u32[]{:S(2)}) collective-permute-start(bf16[48,1792]{1,0:T(8,128)(2,1)S(1)} %get-tuple-element.98), channel_id=1, source_target_pairs={{0,16},{4,20},{8,24},{12,28},{16,32},{20,36},{24,40},{28,44},{32,0... | collective-permute-start | bytes 516104 | tf_op jit(solution)/shard_map/ppermute | solution.py:16
  294.7 5.0 %collective-permute-start.30 = (bf16[48,1792]{1,0:T(8,128)(2,1)S(1)}, bf16[48,1792]{1,0:T(8,128)(2,1)S(1)}, u32[]{:S(2)}, u32[]{:S(2)}) collective-permute-start(bf16[48,1792]{1,0:T(8,128)(2,1)S(1)} %get-tuple-element.99), channel_id=1, source_target_pairs={{0,32},{4,36},{8,40},{12,44},{16,0},{20,4},{24,8},{28,12},{32,16},... | collective-permute-start | bytes 516104 | tf_op jit(solution)/shard_map/ppermute | solution.py:16
  299.8 4.4 %collective-permute-done.31 = bf16[48,1792]{1,0:T(8,128)(2,1)S(1)} collective-permute-done((bf16[48,1792]{1,0:T(8,128)(2,1)S(1)}, bf16[48,1792]{1,0:T(8,128)(2,1)S(1)}, u32[]{:S(2)}, u32[]{:S(2)}) %collective-permute-start.31) | collective-permute-done | bytes 172064 | tf_op jit(solution)/shard_map/ppermute | solution.py:16
  304.1 5.8 %collective-permute-done.30 = bf16[48,1792]{1,0:T(8,128)(2,1)S(1)} collective-permute-done((bf16[48,1792]{1,0:T(8,128)(2,1)S(1)}, bf16[48,1792]{1,0:T(8,128)(2,1)S(1)}, u32[]{:S(2)}, u32[]{:S(2)}) %collective-permute-start.30) | collective-permute-done | bytes 172064 | tf_op jit(solution)/shard_map/ppermute | solution.py:16
  310.1 3.3 collective-permute-start.32
  313.3 3.2 collective-permute-start.33
  316.9 1.1 fusion.9
  317.9 9.8 %collective-permute-done.33 = bf16[3,24,1792]{2,1,0:T(8,128)(2,1)S(1)} collective-permute-done((bf16[3,24,1792]{2,1,0:T(8,128)(2,1)S(1)}, bf16[3,24,1792]{2,1,0:T(8,128)(2,1)S(1)}, u32[]{:S(2)}, u32[]{:S(2)}) %collective-permute-start.33) | collective-permute-done | bytes 258080 | tf_op jit(solution)/shard_map/ppermute | solution.py:189
  328.1 1.2 fusion.8
  (127 shorter events, 21.2 us)
Async XLA Ops:
  0.6 151.7 %copy-start = (bf16[1,256,1792]{2,1,0:T(8,128)(2,1)S(1)}, bf16[1,256,1792]{2,1,0:T(8,128)(2,1)}, u32[]{:S(2)}) copy-start(bf16[1,256,1792]{2,1,0:T(8,128)(2,1)} %param.19) | copy-start | bytes 2752516
  0.8 0.7 copy-start.12
  0.8 0.8 copy-start.13
  3.7 3.6 %copy-start.10 = (bf16[1,128,1792]{2,1,0:T(8,128)(2,1)S(1)}, bf16[1,128,1792]{2,1,0:T(8,128)(2,1)}, u32[]{:S(2)}) copy-start(bf16[1,128,1792]{2,1,0:T(8,128)(2,1)} %param.13) | copy-start | bytes 1376260
  3.8 11.1 %collective-permute-start = (bf16[3,24,1792]{2,1,0:T(8,128)(2,1)S(1)}, bf16[3,24,1792]{2,1,0:T(8,128)(2,1)S(1)}, u32[]{:S(2)}, u32[]{:S(2)}) collective-permute-start(bf16[3,24,1792]{2,1,0:T(8,128)(2,1)S(1)} %bitcast.221), channel_id=1, source_target_pairs={{0,48},{48,0},{1,49},{49,1},{2,50},{50,2},{3,51},{51,3},{4,52},{52... | collective-permute-start | bytes 774152 | tf_op jit(solution)/shard_map/ppermute | solution.py:20
  7.3 0.7 copy-start.14
  8.3 2.7 copy-start.11
  8.4 22.1 %collective-permute-start.3 = (bf16[3,24,1792]{2,1,0:T(8,128)(2,1)S(1)}, bf16[3,24,1792]{2,1,0:T(8,128)(2,1)S(1)}, u32[]{:S(2)}, u32[]{:S(2)}) collective-permute-start(bf16[3,24,1792]{2,1,0:T(8,128)(2,1)S(1)} %bitcast.220), channel_id=1, source_target_pairs={{0,48},{48,0},{1,49},{49,1},{2,50},{50,2},{3,51},{51,3},{4,52},{52... | collective-permute-start | bytes 774152 | tf_op jit(solution)/shard_map/ppermute | solution.py:20
  13.2 0.7 copy-start.15
  14.9 20.5 %collective-permute-start.2 = (bf16[48,1792]{1,0:T(8,128)(2,1)S(1)}, bf16[48,1792]{1,0:T(8,128)(2,1)S(1)}, u32[]{:S(2)}, u32[]{:S(2)}) collective-permute-start(bf16[48,1792]{1,0:T(8,128)(2,1)S(1)} %get-tuple-element.111), channel_id=1, source_target_pairs={{0,16},{4,20},{8,24},{12,28},{16,32},{20,36},{24,40},{28,44},{32,0... | collective-permute-start | bytes 516104 | tf_op jit(solution)/shard_map/ppermute | solution.py:16
  25.9 15.6 %collective-permute-start.1 = (bf16[48,1792]{1,0:T(8,128)(2,1)S(1)}, bf16[48,1792]{1,0:T(8,128)(2,1)S(1)}, u32[]{:S(2)}, u32[]{:S(2)}) collective-permute-start(bf16[48,1792]{1,0:T(8,128)(2,1)S(1)} %get-tuple-element.113), channel_id=1, source_target_pairs={{0,32},{4,36},{8,40},{12,44},{16,0},{20,4},{24,8},{28,12},{32,16},... | collective-permute-start | bytes 516104 | tf_op jit(solution)/shard_map/ppermute | solution.py:16
  41.4 16.4 %copy-start.1 = (bf16[1,1792,256]{2,1,0:T(8,128)(2,1)S(1)}, bf16[1,1792,256]{2,1,0:T(8,128)(2,1)}, u32[]{:S(2)}) copy-start(bf16[1,1792,256]{2,1,0:T(8,128)(2,1)} %param.18) | copy-start | bytes 2752516
  41.4 17.0 %collective-permute-start.6 = (bf16[48,1792]{1,0:T(8,128)(2,1)S(1)}, bf16[48,1792]{1,0:T(8,128)(2,1)S(1)}, u32[]{:S(2)}, u32[]{:S(2)}) collective-permute-start(bf16[48,1792]{1,0:T(8,128)(2,1)S(1)} %get-tuple-element.106), channel_id=1, source_target_pairs={{0,16},{4,20},{8,24},{12,28},{16,32},{20,36},{24,40},{28,44},{32,0... | collective-permute-start | bytes 516104 | tf_op jit(solution)/shard_map/ppermute | solution.py:16
  49.0 12.8 %collective-permute-start.5 = (bf16[48,1792]{1,0:T(8,128)(2,1)S(1)}, bf16[48,1792]{1,0:T(8,128)(2,1)S(1)}, u32[]{:S(2)}, u32[]{:S(2)}) collective-permute-start(bf16[48,1792]{1,0:T(8,128)(2,1)S(1)} %get-tuple-element.107), channel_id=1, source_target_pairs={{0,32},{4,36},{8,40},{12,44},{16,0},{20,4},{24,8},{28,12},{32,16},... | collective-permute-start | bytes 516104 | tf_op jit(solution)/shard_map/ppermute | solution.py:16
  51.4 6.7 %copy-start.2 = (bf16[1,1792,256]{2,1,0:T(8,128)(2,1)S(1)}, bf16[1,1792,256]{2,1,0:T(8,128)(2,1)}, u32[]{:S(2)}) copy-start(bf16[1,1792,256]{2,1,0:T(8,128)(2,1)} %param.17) | copy-start | bytes 2752516
  51.4 22.5 %collective-permute-start.4 = (bf16[144,1792]{1,0:T(8,128)(2,1)S(1)}, bf16[144,1792]{1,0:T(8,128)(2,1)S(1)}, u32[]{:S(2)}, u32[]{:S(2)}) collective-permute-start(bf16[144,1792]{1,0:T(8,128)(2,1)S(1)} %bitcast.208), channel_id=1, source_target_pairs={{0,4},{4,8},{8,12},{12,0},{1,5},{5,9},{9,13},{13,1},{2,6},{6,10},{... | collective-permute-start | bytes 1548296 | tf_op jit(solution)/shard_map/ppermute | solution.py:38
  74.0 32.0 %collective-permute-start.8 = (bf16[144,1792]{1,0:T(8,128)(2,1)S(1)}, bf16[144,1792]{1,0:T(8,128)(2,1)S(1)}, u32[]{:S(2)}, u32[]{:S(2)}) collective-permute-start(bf16[144,1792]{1,0:T(8,128)(2,1)S(1)} %bitcast.211), channel_id=1, source_target_pairs={{0,12},{4,0},{8,4},{12,8},{1,13},{5,1},{9,5},{13,9},{2,14},{6,2},{... | collective-permute-start | bytes 1548296 | tf_op jit(solution)/shard_map/ppermute | solution.py:38
  83.8 23.0 %collective-permute-start.7 = (bf16[144,1792]{1,0:T(8,128)(2,1)S(1)}, bf16[144,1792]{1,0:T(8,128)(2,1)S(1)}, u32[]{:S(2)}, u32[]{:S(2)}) collective-permute-start(bf16[144,1792]{1,0:T(8,128)(2,1)S(1)} %collective-permute-done.4), channel_id=1, source_target_pairs={{0,4},{4,8},{8,12},{12,0},{1,5},{5,9},{9,13},{13,1},{2,6},{6,10},{... | collective-permute-start | bytes 1548296 | tf_op jit(solution)/shard_map/ppermute | solution.py:38
  106.8 15.2 %collective-permute-start.10 = (bf16[144,1792]{1,0:T(8,128)(2,1)S(1)}, bf16[144,1792]{1,0:T(8,128)(2,1)S(1)}, u32[]{:S(2)}, u32[]{:S(2)}) collective-permute-start(bf16[144,1792]{1,0:T(8,128)(2,1)S(1)} %collective-permute-done.8), channel_id=1, source_target_pairs={{0,12},{4,0},{8,4},{12,8},{1,13},{5,1},{9,5},{13,9},{2,14},{6,2},{... | collective-permute-start | bytes 1548296 | tf_op jit(solution)/shard_map/ppermute | solution.py:38
  110.4 23.6 %collective-permute-start.9 = (bf16[144,1792]{1,0:T(8,128)(2,1)S(1)}, bf16[144,1792]{1,0:T(8,128)(2,1)S(1)}, u32[]{:S(2)}, u32[]{:S(2)}) collective-permute-start(bf16[144,1792]{1,0:T(8,128)(2,1)S(1)} %collective-permute-done.7), channel_id=1, source_target_pairs={{0,4},{4,8},{8,12},{12,0},{1,5},{5,9},{9,13},{13,1},{2,6},{6,10},{... | collective-permute-start | bytes 1548296 | tf_op jit(solution)/shard_map/ppermute | solution.py:38
  134.7 12.6 %collective-permute-start.11 = (f32[288,512]{1,0:T(8,128)S(1)}, f32[288,512]{1,0:T(8,128)S(1)}, u32[]{:S(2)}, u32[]{:S(2)}) collective-permute-start(f32[288,512]{1,0:T(8,128)S(1)} %fusion.54), channel_id=1, source_target_pairs={{0,1},{1,0},{2,3},{3,2},{4,5},{5,4},{6,7},{7,6},{8,9},{9,8},{10,11... | collective-permute-start | bytes 1769480 | tf_op jit(solution)/shard_map/ppermute | solution.py:20
  140.2 23.7 %collective-permute-start.16 = (f32[128]{0:T(128)S(1)}, f32[128]{0:T(128)S(1)}, u32[]{:S(2)}, u32[]{:S(2)}) collective-permute-start(f32[128]{0:T(128)S(1)} %bitcast_convert_fusion), channel_id=1, source_target_pairs={{96,0},{192,96},{288,192},{384,288},{480,384},{576,480},{672,576},... | collective-permute-start | bytes 1544 | tf_op jit(solution)/shard_map/ppermute | solution.py:128
  142.5 21.4 %collective-permute-start.15 = (f32[2,128]{1,0:T(2,128)S(1)}, f32[2,128]{1,0:T(2,128)S(1)}, u32[]{:S(2)}, u32[]{:S(2)}) collective-permute-start(f32[2,128]{1,0:T(2,128)S(1)} %pad_maximum_fusion.9), channel_id=1, source_target_pairs={{0,96},{96,192},{192,288},{288,384},{384,480},{480,576},{576,672},... | collective-permute-start | bytes 3080 | tf_op jit(solution)/shard_map/ppermute | solution.py:127
  147.4 12.2 %collective-permute-start.12 = (bf16[288,512]{1,0:T(8,128)(2,1)S(1)}, bf16[288,512]{1,0:T(8,128)(2,1)S(1)}, u32[]{:S(2)}, u32[]{:S(2)}) collective-permute-start(bf16[288,512]{1,0:T(8,128)(2,1)S(1)} %get-tuple-element.84), channel_id=1, source_target_pairs={{0,2},{2,0},{1,3},{3,1},{4,6},{6,4},{5,7},{7,5},{8,10},{10,8},{9,1... | collective-permute-start | bytes 884744 | tf_op jit(solution)/shard_map/ppermute | solution.py:20
  153.3 15.7 %copy-start.3 = (f32[144,256]{1,0:T(8,128)}, f32[144,256]{1,0:T(8,128)S(1)}, u32[]{:S(2)}) copy-start(f32[144,256]{1,0:T(8,128)S(1)} %fusion.17) | copy-start | bytes 442372
  153.3 15.2 %collective-permute-start.14 = (bf16[144,1792]{1,0:T(8,128)(2,1)S(1)}, bf16[144,1792]{1,0:T(8,128)(2,1)S(1)}, u32[]{:S(2)}, u32[]{:S(2)}) collective-permute-start(bf16[144,1792]{1,0:T(8,128)(2,1)S(1)} %collective-permute-done.10), channel_id=1, source_target_pairs={{0,12},{4,0},{8,4},{12,8},{1,13},{5,1},{9,5},{13,9},{2,14},{6,2},{... | collective-permute-start | bytes 1548296 | tf_op jit(solution)/shard_map/ppermute | solution.py:38
  159.8 3.3 collective-permute-start.13
  162.2 6.7 %copy-start.5 = (f32[144,256]{1,0:T(8,128)}, f32[144,256]{1,0:T(8,128)S(1)}, u32[]{:S(2)}) copy-start(f32[144,256]{1,0:T(8,128)S(1)} %fusion.15) | copy-start | bytes 442372
  169.0 0.8 copy-start.7
  169.7 9.0 %collective-permute-start.18 = (f32[288,256]{1,0:T(8,128)}, f32[288,256]{1,0:T(8,128)}, u32[]{:S(2)}, u32[]{:S(2)}) collective-permute-start(f32[288,256]{1,0:T(8,128)} %fusion.65), channel_id=1, source_target_pairs={{0,1},{1,0},{2,3},{3,2},{4,5},{5,4},{6,7},{7,6},{8,9},{9,8},{10,11... | collective-permute-start | bytes 884744 | tf_op jit(solution)/shard_map/ppermute | solution.py:20
  173.7 5.0 %copy-start.4 = (f32[144,256]{1,0:T(8,128)S(1)}, f32[144,256]{1,0:T(8,128)}, u32[]{:S(2)}) copy-start(f32[144,256]{1,0:T(8,128)} %copy-done.3) | copy-start | bytes 442372
  173.7 5.1 %copy-start.6 = (f32[144,256]{1,0:T(8,128)S(1)}, f32[144,256]{1,0:T(8,128)}, u32[]{:S(2)}) copy-start(f32[144,256]{1,0:T(8,128)} %copy-done.5) | copy-start | bytes 442372
  173.7 5.1 %copy-start.8 = (f32[144,256]{1,0:T(8,128)S(1)}, f32[144,256]{1,0:T(8,128)}, u32[]{:S(2)}) copy-start(f32[144,256]{1,0:T(8,128)} %copy-done.7) | copy-start | bytes 442372
  173.7 19.4 %collective-permute-start.17 = (bf16[144,1792]{1,0:T(8,128)(2,1)}, bf16[144,1792]{1,0:T(8,128)(2,1)S(1)}, u32[]{:S(2)}, u32[]{:S(2)}) collective-permute-start(bf16[144,1792]{1,0:T(8,128)(2,1)} %convolution_convert_fusion.3), channel_id=1, source_target_pairs={{0,12},{4,0},{8,4},{12,8},{1,13},{5,1},{9,5},{13,9},{2,14},{6,2},{... | collective-permute-start | bytes 1548296 | tf_op jit(solution)/shard_map/ppermute | solution.py:38
  178.7 10.5 %copy-start.9 = (bf16[6,2,24,2,256]{4,2,1,0,3:T(8,128)(2,1)S(1)}, bf16[6,2,24,2,256]{4,2,1,0,3:T(8,128)(2,1)}, u32[]{:S(2)}) copy-start(bf16[6,2,24,2,256]{4,2,1,0,3:T(8,128)(2,1)} %pad.4) | copy-start | bytes 884740
  179.9 9.4 %collective-permute-start.19 = (bf16[288,256]{1,0:T(8,128)(2,1)S(1)}, bf16[288,256]{1,0:T(8,128)(2,1)S(1)}, u32[]{:S(2)}, u32[]{:S(2)}) collective-permute-start(bf16[288,256]{1,0:T(8,128)(2,1)S(1)} %get-tuple-element.82), channel_id=1, source_target_pairs={{0,2},{2,0},{1,3},{3,1},{4,6},{6,4},{5,7},{7,5},{8,10},{10,8},{9,1... | collective-permute-start | bytes 442376 | tf_op jit(solution)/shard_map/ppermute | solution.py:20
  189.4 3.5 %collective-permute-start.20 = (bf16[288,512]{1,0:T(8,128)(2,1)S(1)}, bf16[288,512]{1,0:T(8,128)(2,1)S(1)}, u32[]{:S(2)}, u32[]{:S(2)}) collective-permute-start(bf16[288,512]{1,0:T(8,128)(2,1)S(1)} %pad_maximum_fusion.7), channel_id=1, source_target_pairs={{0,1},{1,0},{2,3},{3,2},{4,5},{5,4},{6,7},{7,6},{8,9},{9,8},{10,11... | collective-permute-start | bytes 884744 | tf_op jit(solution)/shard_map/ppermute | solution.py:20
  193.2 28.1 %collective-permute-start.21 = (bf16[144,1792]{1,0:T(8,128)(2,1)S(1)}, bf16[144,1792]{1,0:T(8,128)(2,1)S(1)}, u32[]{:S(2)}, u32[]{:S(2)}) collective-permute-start(bf16[144,1792]{1,0:T(8,128)(2,1)S(1)} %add.247), channel_id=1, source_target_pairs={{0,12},{4,0},{8,4},{12,8},{1,13},{5,1},{9,5},{13,9},{2,14},{6,2},{... | collective-permute-start | bytes 1548296 | tf_op jit(solution)/shard_map/ppermute | solution.py:38
  199.9 22.2 %collective-permute-start.22 = (bf16[144,1792]{1,0:T(8,128)(2,1)S(1)}, bf16[144,1792]{1,0:T(8,128)(2,1)S(1)}, u32[]{:S(2)}, u32[]{:S(2)}) collective-permute-start(bf16[144,1792]{1,0:T(8,128)(2,1)S(1)} %fusion.2), channel_id=1, source_target_pairs={{0,4},{4,8},{8,12},{12,0},{1,5},{5,9},{9,13},{13,1},{2,6},{6,10},{... | collective-permute-start | bytes 1548296 | tf_op jit(solution)/shard_map/ppermute | solution.py:38
  222.3 15.3 %collective-permute-start.23 = (bf16[144,1792]{1,0:T(8,128)(2,1)S(1)}, bf16[144,1792]{1,0:T(8,128)(2,1)S(1)}, u32[]{:S(2)}, u32[]{:S(2)}) collective-permute-start(bf16[144,1792]{1,0:T(8,128)(2,1)S(1)} %add.249), channel_id=1, source_target_pairs={{0,12},{4,0},{8,4},{12,8},{1,13},{5,1},{9,5},{13,9},{2,14},{6,2},{... | collective-permute-start | bytes 1548296 | tf_op jit(solution)/shard_map/ppermute | solution.py:38
  226.0 24.7 %collective-permute-start.24 = (bf16[144,1792]{1,0:T(8,128)(2,1)S(1)}, bf16[144,1792]{1,0:T(8,128)(2,1)S(1)}, u32[]{:S(2)}, u32[]{:S(2)}) collective-permute-start(bf16[144,1792]{1,0:T(8,128)(2,1)S(1)} %add.251), channel_id=1, source_target_pairs={{0,4},{4,8},{8,12},{12,0},{1,5},{5,9},{9,13},{13,1},{2,6},{6,10},{... | collective-permute-start | bytes 1548296 | tf_op jit(solution)/shard_map/ppermute | solution.py:38
  250.8 32.8 %collective-permute-start.27 = (bf16[144,1792]{1,0:T(8,128)(2,1)S(1)}, bf16[144,1792]{1,0:T(8,128)(2,1)S(1)}, u32[]{:S(2)}, u32[]{:S(2)}) collective-permute-start(bf16[144,1792]{1,0:T(8,128)(2,1)S(1)} %add.254), channel_id=1, source_target_pairs={{0,4},{4,8},{8,12},{12,0},{1,5},{5,9},{9,13},{13,1},{2,6},{6,10},{... | collective-permute-start | bytes 1548296 | tf_op jit(solution)/shard_map/ppermute | solution.py:38
  254.3 25.8 %collective-permute-start.26 = (bf16[48,1792]{1,0:T(8,128)(2,1)S(1)}, bf16[48,1792]{1,0:T(8,128)(2,1)S(1)}, u32[]{:S(2)}, u32[]{:S(2)}) collective-permute-start(bf16[48,1792]{1,0:T(8,128)(2,1)S(1)} %get-tuple-element.103), channel_id=1, source_target_pairs={{0,16},{4,20},{8,24},{12,28},{16,32},{20,36},{24,40},{28,44},{32,0... | collective-permute-start | bytes 516104 | tf_op jit(solution)/shard_map/ppermute | solution.py:16
  258.7 24.9 %collective-permute-start.25 = (bf16[48,1792]{1,0:T(8,128)(2,1)S(1)}, bf16[48,1792]{1,0:T(8,128)(2,1)S(1)}, u32[]{:S(2)}, u32[]{:S(2)}) collective-permute-start(bf16[48,1792]{1,0:T(8,128)(2,1)S(1)} %get-tuple-element.104), channel_id=1, source_target_pairs={{0,32},{4,36},{8,40},{12,44},{16,0},{20,4},{24,8},{28,12},{32,16},... | collective-permute-start | bytes 516104 | tf_op jit(solution)/shard_map/ppermute | solution.py:16
  283.7 26.2 %collective-permute-start.29 = (bf16[3,24,1792]{2,1,0:T(8,128)(2,1)S(1)}, bf16[3,24,1792]{2,1,0:T(8,128)(2,1)S(1)}, u32[]{:S(2)}, u32[]{:S(2)}) collective-permute-start(bf16[3,24,1792]{2,1,0:T(8,128)(2,1)S(1)} %get-tuple-element.101), channel_id=1, source_target_pairs={{0,144},{48,96},{96,240},{144,192},{192,336},{240,288},{288,432},{... | collective-permute-start | bytes 774152 | tf_op jit(solution)/shard_map/ppermute | solution.py:189
  287.2 22.7 %collective-permute-start.28 = (bf16[3,24,1792]{2,1,0:T(8,128)(2,1)S(1)}, bf16[3,24,1792]{2,1,0:T(8,128)(2,1)S(1)}, u32[]{:S(2)}, u32[]{:S(2)}) collective-permute-start(bf16[3,24,1792]{2,1,0:T(8,128)(2,1)S(1)} %get-tuple-element.102), channel_id=1, source_target_pairs={{0,96},{96,192},{192,288},{288,384},{384,480},{480,576},{576,672},... | collective-permute-start | bytes 774152 | tf_op jit(solution)/shard_map/ppermute | solution.py:188
  290.0 14.1 %collective-permute-start.31 = (bf16[48,1792]{1,0:T(8,128)(2,1)S(1)}, bf16[48,1792]{1,0:T(8,128)(2,1)S(1)}, u32[]{:S(2)}, u32[]{:S(2)}) collective-permute-start(bf16[48,1792]{1,0:T(8,128)(2,1)S(1)} %get-tuple-element.98), channel_id=1, source_target_pairs={{0,16},{4,20},{8,24},{12,28},{16,32},{20,36},{24,40},{28,44},{32,0... | collective-permute-start | bytes 516104 | tf_op jit(solution)/shard_map/ppermute | solution.py:16
  294.7 15.2 %collective-permute-start.30 = (bf16[48,1792]{1,0:T(8,128)(2,1)S(1)}, bf16[48,1792]{1,0:T(8,128)(2,1)S(1)}, u32[]{:S(2)}, u32[]{:S(2)}) collective-permute-start(bf16[48,1792]{1,0:T(8,128)(2,1)S(1)} %get-tuple-element.99), channel_id=1, source_target_pairs={{0,32},{4,36},{8,40},{12,44},{16,0},{20,4},{24,8},{28,12},{32,16},... | collective-permute-start | bytes 516104 | tf_op jit(solution)/shard_map/ppermute | solution.py:16
  310.1 18.0 %collective-permute-start.32 = (bf16[3,24,1792]{2,1,0:T(8,128)(2,1)S(1)}, bf16[3,24,1792]{2,1,0:T(8,128)(2,1)S(1)}, u32[]{:S(2)}, u32[]{:S(2)}) collective-permute-start(bf16[3,24,1792]{2,1,0:T(8,128)(2,1)S(1)} %get-tuple-element.96), channel_id=1, source_target_pairs={{96,0},{192,96},{288,192},{384,288},{480,384},{576,480},{672,576},... | collective-permute-start | bytes 774152 | tf_op jit(solution)/shard_map/ppermute | solution.py:188
  313.3 14.4 %collective-permute-start.33 = (bf16[3,24,1792]{2,1,0:T(8,128)(2,1)S(1)}, bf16[3,24,1792]{2,1,0:T(8,128)(2,1)S(1)}, u32[]{:S(2)}, u32[]{:S(2)}) collective-permute-start(bf16[3,24,1792]{2,1,0:T(8,128)(2,1)S(1)} %get-tuple-element.97), channel_id=1, source_target_pairs={{96,48},{144,0},{192,144},{240,96},{288,240},{336,192},{384,336},{... | collective-permute-start | bytes 774152 | tf_op jit(solution)/shard_map/ppermute | solution.py:189

commit v4 on v3

--- a/solution.py
+++ b/solution.py
@@ -34,16 +34,60 @@
     return placing.reshape(-1, routes.shape[0])
 
 
-def around(values, step):
-    return lax.ppermute(values, "member", [(i, (i + step) % GROUP) for i in range(GROUP)])
-
-
-def widen(slots):
-    return jnp.concatenate([slots[0], swap(slots[1], "half")], axis=1)
-
-
-def shift_groups(blocks):
-    return blocks[0], hop(blocks[2], -GROUP), hop(blocks[1], GROUP)
+def dispatch(slots):
+    member = lax.axis_index("member")
+    other = swap(slots[1], "half")
+    blocks = jnp.concatenate([slots[0], other], axis=1)
+    own = blocks[0]
+    right = jnp.stack([blocks[0], blocks[1]])
+    left = jnp.stack([blocks[0], blocks[2]])
+    rights, lefts = {}, {}
+    for step in range(1, 8):
+        if step == 4:
+            right, left = right[1], left[1]
+        right, left = hop(right, 1), hop(left, -1)
+        rights[step], lefts[step] = right, left
+    out = [jnp.stack([own, lefts[4], rights[4]])]
+    for s in range(1, GROUP):
+        out.append(
+            jnp.stack(
+                [
+                    jnp.where(member >= s, rights[s][0], lefts[4 - s][0]),
+                    jnp.where(member >= s, lefts[4 - s][1], lefts[8 - s]),
+                    jnp.where(member < s, rights[s][1], rights[s + 4]),
+                ]
+            )
+        )
+    return [part.reshape(-1, slots.shape[-1]) for part in out]
+
+
+def collect(parts):
+    member = lax.axis_index("member")
+
+    def only(mask, values):
+        return jnp.where(mask, values, jnp.zeros_like(values))
+
+    def back(right, left):
+        return lax.optimization_barrier((hop(right, -1), hop(left, 1)))
+
+    right, left = only(member >= 3, parts[3][2]), only(member < 1, parts[1][1])
+    for s in (2, 1):
+        right, left = back(right, left)
+        right = right + only(member >= s, parts[s][2])
+        left = left + only(member < GROUP - s, parts[GROUP - s][1])
+    right, left = back(right, left)
+    right, left = back(right + parts[0][2], left + parts[0][1])
+    right = jnp.stack([only(member >= 3, parts[3][0]), right + only(member < 3, parts[3][2])])
+    left = jnp.stack([only(member < 1, parts[1][0]), left + only(member >= 1, parts[1][1])])
+    for s in (2, 1):
+        t = GROUP - s
+        right, left = back(right, left)
+        right = right + jnp.stack(
+            [only(member >= s, parts[s][0]), only(member < s, parts[s][2])]
+        )
+        left = left + jnp.stack([only(member < t, parts[t][0]), only(member >= t, parts[t][1])])
+    right, left = back(right, left)
+    return jnp.stack([parts[0][0] + right[0] + left[0], right[1], left[1]])
 
 
 def reduce_rows(parts):
@@ -104,37 +148,23 @@
     columns = tokens_fwd.shape[2]
     hidden_width = w_gate.shape[2]
 
-    together = lax.optimization_barrier
     place_fwd = placing_of(routes_fwd[0, :, 0], capacity, width)
     place_bwd = placing_of(routes_bwd[0, :, 0], capacity, width)
     send_fwd = jnp.dot(place_fwd, tokens_fwd[0], preferred_element_type=F32).astype(BF16)
     scaled = (cotangent[0].astype(F32) * gates_bwd[0]).astype(BF16)
     send_bwd = jnp.dot(place_bwd, scaled, preferred_element_type=F32).astype(BF16)
 
-    def flat(blocks):
-        return blocks.reshape(-1, columns)
-
-    fwd = widen(send_fwd.reshape(2, groups, width, columns))
-    fwd, bwd = together((shift_groups(fwd), widen(send_bwd.reshape(2, groups, width, columns))))
-    got_fwd = [flat(jnp.stack(fwd))]
+    got_fwd = dispatch(send_fwd.reshape(2, groups, width, columns))
+    got_bwd = dispatch(send_bwd.reshape(2, groups, width, columns))
 
     sections = lax.axis_size("section")
     up = [(i, i + 1) for i in range(sections - 1)]
     down = [(i + 1, i) for i in range(sections - 1)]
     send_up = jnp.stack([routes_fwd[0, :, 0].astype(F32), gates_fwd[0, :, 0]])
     send_down = routes_bwd[0, :, 0].astype(F32)
-    bwd, send_up, send_down = together((bwd, send_up, send_down))
+    got_fwd, send_up, send_down = lax.optimization_barrier((got_fwd, send_up, send_down))
     from_before = lax.ppermute(send_up, "section", up)
     from_after = lax.ppermute(send_down, "section", down)
-
-    part, bwd = together((around(got_fwd[0], 1), shift_groups(bwd)))
-    got_fwd.append(part)
-    got_bwd = [flat(jnp.stack(bwd))]
-    for _ in range(2, GROUP):
-        part, bwd = together((around(got_fwd[-1], 1), around(got_bwd[-1], -1)))
-        got_fwd.append(part)
-        got_bwd.append(bwd)
-    last_bwd = around(got_bwd[-1], -1)
 
     partial_fwd = [
         jnp.concatenate(
@@ -149,21 +179,16 @@
     summed = reduce_rows(partial_fwd)
     gate_pre, up_pre = jnp.split(summed, 2, axis=1)
     hidden = gather_rows((gate_pre * jax.nn.sigmoid(gate_pre) * up_pre).astype(BF16))
-    hidden, last_bwd, from_before, from_after = together(
-        (hidden, last_bwd, from_before, from_after)
-    )
-    got_bwd.append(last_bwd)
     out = [jnp.dot(rows, w_down[0], preferred_element_type=F32).astype(BF16) for rows in hidden]
 
     grad_hidden = reduce_rows([contract_last(rows, w_down[0]) for rows in got_bwd])
-    saved = saved_half(saved_pre[0], capacity, width, -1)
+    saved = saved_half(saved_pre[0], capacity, width, 1)
     pre_gate = saved[:, 0].astype(F32)
     pre_up = saved[:, 1].astype(F32)
     sigmoid_gate = jax.nn.sigmoid(pre_gate)
     grad_gate = grad_hidden * pre_up * sigmoid_gate * (1.0 + pre_gate * (1.0 - sigmoid_gate))
     grad_up = grad_hidden * pre_gate * sigmoid_gate
     grads = gather_rows(jnp.concatenate([grad_gate, grad_up], axis=1).astype(BF16))
-    total, grads = together((around(out[GROUP - 1], -1), grads))
     grad_out = [
         (
             contract_last(rows[:, :hidden_width], w_gate[0])
@@ -172,26 +197,18 @@
         for rows in grads
     ]
 
-    total_bwd = grad_out[GROUP - 1]
-    for k in range(GROUP - 2, 0, -1):
-        total, total_bwd = together((around(total + out[k], -1), around(total_bwd, 1)))
-        total_bwd = total_bwd + grad_out[k]
-
-    def blocks_of(rows):
-        return rows.reshape(groups, 2 * width, columns)
-
-    total, total_bwd = together((shift_groups(blocks_of(total + out[0])), around(total_bwd, 1)))
+    def collected(parts):
+        return collect([rows.reshape(groups, 2 * width, columns) for rows in parts])
+
+    back_fwd, from_before = lax.optimization_barrier((collected(out), from_before))
+    back_bwd, from_after = lax.optimization_barrier((collected(grad_out), from_after))
 
     def shifted(values, shift):
         mine, others = values[:, :width], values[:, width:]
         across = [(2 * i + h, 2 * j + 1 - h) for i, j in shift for h in range(2)]
         mine = lax.ppermute(mine, "section", shift)
         others = lax.ppermute(others, ("section", "half"), across)
-        return flat(mine), flat(others)
-
-    moved, total_bwd = together(
-        (shifted(jnp.stack(total), up), shift_groups(blocks_of(total_bwd + grad_out[0])))
-    )
+        return mine.reshape(-1, columns), others.reshape(-1, columns)
 
     def rows_of(placing, values):
         mine, others = values
@@ -204,8 +221,8 @@
 
     place_before = placing_of(from_before[0].astype(jnp.int32), capacity, width)
     place_after = placing_of(from_after.astype(jnp.int32), capacity, width)
-    forwarded = rows_of(place_before, moved) * from_before[1][:, None]
-    returned = rows_of(place_after, shifted(jnp.stack(total_bwd), down))
+    forwarded = rows_of(place_before, shifted(back_fwd, up)) * from_before[1][:, None]
+    returned = rows_of(place_after, shifted(back_bwd, down))
     return (forwarded.astype(BF16)[None], returned.astype(BF16)[None])
 
 

time: 330 us -> 309 us (0.936)
  the two profiles are of different devices: /device:TPU:88 before, /device:TPU:32 now
where the time goes in v4:
time: 309 us; the launch traced here: 306 us
  starting transfers between devices  236 us (76%)
  waiting for transfers between devices  37.4 us (12%)
  matrix products  14.1 us (5%)
  other arithmetic  12.5 us (4%)
  local copies, waits for them, and re-layouts  4.17 us (1%)
    ppermute x56, starting transfers between devices, hop(): lax.ppermute(values, RING, [(i, (i + step) % count) for i in range(count)])  194 us
    ppermute x56, waiting for transfers between devices, hop(): lax.ppermute(values, RING, [(i, (i + step) % count) for i in range(count)])  25 us
    ppermute x8, starting transfers between devices, swap(): return lax.ppermute(values, axis, [(0, 1), (1, 0)])  24.2 us
    ppermute x2, starting transfers between devices, shifted(): others = lax.ppermute(others, ('section', 'half'), across)  7.89 us
    ppermute x8, waiting for transfers between devices, swap(): return lax.ppermute(values, axis, [(0, 1), (1, 0)])  7.25 us
  transfers between devices with their start and end apart: 70, of which 22 were waited for; matrix products, arithmetic and copies ran while one was open for 8% of the time, Pallas kernels for 0%

profile of v4, /device:TPU:32, one launch (start us, length us, event | category | flops | bytes accessed | tf_op | source)
XLA Modules:
  0.0 306.2 jit_solution(13538592470213151213)
XLA Ops:
  4.5 3.5 %collective-permute-start.35 = (bf16[3,24,1792]{2,1,0:T(8,128)(2,1)S(1)}, bf16[3,24,1792]{2,1,0:T(8,128)(2,1)S(1)}, u32[]{:S(2)}, u32[]{:S(2)}) collective-permute-start(bf16[3,24,1792]{2,1,0:T(8,128)(2,1)S(1)} %bitcast.361), channel_id=1, source_target_pairs={{0,48},{48,0},{1,49},{49,1},{2,50},{50,2},{3,51},{51,3},{4,52},{52... | collective-permute-start | bytes 774152 | tf_op jit(solution)/shard_map/ppermute | solution.py:20
  9.1 2.4 collective-permute-start
  12.5 3.1 %collective-permute-done.35 = bf16[3,24,1792]{2,1,0:T(8,128)(2,1)S(1)} collective-permute-done((bf16[3,24,1792]{2,1,0:T(8,128)(2,1)S(1)}, bf16[3,24,1792]{2,1,0:T(8,128)(2,1)S(1)}, u32[]{:S(2)}, u32[]{:S(2)}) %collective-permute-start.35) | collective-permute-done | bytes 258080 | tf_op jit(solution)/shard_map/ppermute | solution.py:20
  15.6 14.6 %collective-permute-start.36 = (bf16[2,48,1792]{2,1,0:T(8,128)(2,1)S(1)}, bf16[2,48,1792]{2,1,0:T(8,128)(2,1)}, u32[]{:S(2)}, u32[]{:S(2)}) collective-permute-start(bf16[2,48,1792]{2,1,0:T(8,128)(2,1)S(1)} %pad_maximum_fusion.15), channel_id=1, source_target_pairs={{0,44},{4,0},{8,4},{12,8},{16,12},{20,16},{24,20},{28,24},{32,28},... | collective-permute-start | bytes 1032200 | tf_op jit(solution)/shard_map/ppermute | solution.py:16
  30.2 1.9 collective-permute-start.40
  32.2 1.9 collective-permute-start.5
  35.0 5.1 %collective-permute-start.1 = (bf16[2,48,1792]{2,1,0:T(8,128)(2,1)}, bf16[2,48,1792]{2,1,0:T(8,128)(2,1)}, u32[]{:S(2)}, u32[]{:S(2)}) collective-permute-start(bf16[2,48,1792]{2,1,0:T(8,128)(2,1)} %pad_maximum_fusion.12), channel_id=1, source_target_pairs={{0,44},{4,0},{8,4},{12,8},{16,12},{20,16},{24,20},{28,24},{32,28},... | collective-permute-start | bytes 1032200 | tf_op jit(solution)/shard_map/ppermute | solution.py:16
  40.1 3.9 %collective-permute-start.37 = (bf16[2,48,1792]{2,1,0:T(8,128)(2,1)}, bf16[2,48,1792]{2,1,0:T(8,128)(2,1)S(1)}, u32[]{:S(2)}, u32[]{:S(2)}) collective-permute-start(bf16[2,48,1792]{2,1,0:T(8,128)(2,1)} %collective-permute-done.36), channel_id=1, source_target_pairs={{0,44},{4,0},{8,4},{12,8},{16,12},{20,16},{24,20},{28,24},{32,28},... | collective-permute-start | bytes 1032200 | tf_op jit(solution)/shard_map/ppermute | solution.py:16
  46.3 4.1 %collective-permute-done.5 = bf16[2,48,1792]{2,1,0:T(8,128)(2,1)} collective-permute-done((bf16[2,48,1792]{2,1,0:T(8,128)(2,1)S(1)}, bf16[2,48,1792]{2,1,0:T(8,128)(2,1)}, u32[]{:S(2)}, u32[]{:S(2)}) %collective-permute-start.5) | collective-permute-done | bytes 344096 | tf_op jit(solution)/shard_map/ppermute | solution.py:16
  53.5 5.1 %collective-permute-start.2 = (bf16[2,48,1792]{2,1,0:T(8,128)(2,1)}, bf16[2,48,1792]{2,1,0:T(8,128)(2,1)S(1)}, u32[]{:S(2)}, u32[]{:S(2)}) collective-permute-start(bf16[2,48,1792]{2,1,0:T(8,128)(2,1)} %collective-permute-done.1), channel_id=1, source_target_pairs={{0,44},{4,0},{8,4},{12,8},{16,12},{20,16},{24,20},{28,24},{32,28},... | collective-permute-start | bytes 1032200 | tf_op jit(solution)/shard_map/ppermute | solution.py:16
  58.7 1.9 collective-permute-start.38
  60.6 3.9 %collective-permute-start.42 = (bf16[2,48,1792]{2,1,0:T(8,128)(2,1)S(1)}, bf16[2,48,1792]{2,1,0:T(8,128)(2,1)S(1)}, u32[]{:S(2)}, u32[]{:S(2)}) collective-permute-start(bf16[2,48,1792]{2,1,0:T(8,128)(2,1)S(1)} %collective-permute-done.41), channel_id=1, source_target_pairs={{0,4},{4,8},{8,12},{12,16},{16,20},{20,24},{24,28},{28,32},{32,36}... | collective-permute-start | bytes 1032200 | tf_op jit(solution)/shard_map/ppermute | solution.py:16
  67.5 5.1 %collective-permute-start.3 = (bf16[2,48,1792]{2,1,0:T(8,128)(2,1)S(1)}, bf16[2,48,1792]{2,1,0:T(8,128)(2,1)S(1)}, u32[]{:S(2)}, u32[]{:S(2)}) collective-permute-start(bf16[2,48,1792]{2,1,0:T(8,128)(2,1)S(1)} %collective-permute-done.2), channel_id=1, source_target_pairs={{0,44},{4,0},{8,4},{12,8},{16,12},{20,16},{24,20},{28,24},{32,28},... | collective-permute-start | bytes 1032200 | tf_op jit(solution)/shard_map/ppermute | solution.py:16
  72.7 1.9 collective-permute-start.39
  75.6 3.9 %collective-permute-start.43 = (bf16[48,1792]{1,0:T(8,128)(2,1)S(1)}, bf16[48,1792]{1,0:T(8,128)(2,1)S(1)}, u32[]{:S(2)}, u32[]{:S(2)}) collective-permute-start(bf16[48,1792]{1,0:T(8,128)(2,1)S(1)} %get-tuple-element.142), channel_id=1, source_target_pairs={{0,4},{4,8},{8,12},{12,16},{16,20},{20,24},{24,28},{28,32},{32,36}... | collective-permute-start | bytes 516104 | tf_op jit(solution)/shard_map/ppermute | solution.py:16
  80.6 2.1 collective-permute-start.8
  83.6 5.1 %collective-permute-start.4 = (bf16[48,1792]{1,0:T(8,128)(2,1)S(1)}, bf16[48,1792]{1,0:T(8,128)(2,1)S(1)}, u32[]{:S(2)}, u32[]{:S(2)}) collective-permute-start(bf16[48,1792]{1,0:T(8,128)(2,1)S(1)} %get-tuple-element.149), channel_id=1, source_target_pairs={{0,44},{4,0},{8,4},{12,8},{16,12},{20,16},{24,20},{28,24},{32,28},... | collective-permute-start | bytes 516104 | tf_op jit(solution)/shard_map/ppermute | solution.py:16
  88.8 1.9 collective-permute-start.44
  90.7 3.9 %collective-permute-start.47 = (bf16[48,1792]{1,0:T(8,128)(2,1)S(1)}, bf16[48,1792]{1,0:T(8,128)(2,1)S(1)}, u32[]{:S(2)}, u32[]{:S(2)}) collective-permute-start(bf16[48,1792]{1,0:T(8,128)(2,1)S(1)} %collective-permute-done.43), channel_id=1, source_target_pairs={{0,4},{4,8},{8,12},{12,16},{16,20},{20,24},{24,28},{28,32},{32,36}... | collective-permute-start | bytes 516104 | tf_op jit(solution)/shard_map/ppermute | solution.py:16
  94.7 1.9 collective-permute-start.12
  97.1 5.1 %collective-permute-start.9 = (bf16[48,1792]{1,0:T(8,128)(2,1)S(1)}, bf16[48,1792]{1,0:T(8,128)(2,1)S(1)}, u32[]{:S(2)}, u32[]{:S(2)}) collective-permute-start(bf16[48,1792]{1,0:T(8,128)(2,1)S(1)} %collective-permute-done.4), channel_id=1, source_target_pairs={{0,44},{4,0},{8,4},{12,8},{16,12},{20,16},{24,20},{28,24},{32,28},... | collective-permute-start | bytes 516104 | tf_op jit(solution)/shard_map/ppermute | solution.py:16
  102.4 1.9 collective-permute-start.45
  107.8 5.6 %collective-permute-start.10 = (bf16[48,1792]{1,0:T(8,128)(2,1)S(1)}, bf16[48,1792]{1,0:T(8,128)(2,1)S(1)}, u32[]{:S(2)}, u32[]{:S(2)}) collective-permute-start(bf16[48,1792]{1,0:T(8,128)(2,1)S(1)} %collective-permute-done.9), channel_id=1, source_target_pairs={{0,44},{4,0},{8,4},{12,8},{16,12},{20,16},{24,20},{28,24},{32,28},... | collective-permute-start | bytes 516104 | tf_op jit(solution)/shard_map/ppermute | solution.py:16
  118.3 5.1 %collective-permute-start.46 = (bf16[48,1792]{1,0:T(8,128)(2,1)S(1)}, bf16[48,1792]{1,0:T(8,128)(2,1)S(1)}, u32[]{:S(2)}, u32[]{:S(2)}) collective-permute-start(bf16[48,1792]{1,0:T(8,128)(2,1)S(1)} %collective-permute-done.45), channel_id=1, source_target_pairs={{0,44},{4,0},{8,4},{12,8},{16,12},{20,16},{24,20},{28,24},{32,28},... | collective-permute-start | bytes 516104 | tf_op jit(solution)/shard_map/ppermute | solution.py:16
  125.8 1.9 collective-permute-start.14
  128.2 5.1 %collective-permute-start.11 = (bf16[48,1792]{1,0:T(8,128)(2,1)S(1)}, bf16[48,1792]{1,0:T(8,128)(2,1)S(1)}, u32[]{:S(2)}, u32[]{:S(2)}) collective-permute-start(bf16[48,1792]{1,0:T(8,128)(2,1)S(1)} %collective-permute-done.10), channel_id=1, source_target_pairs={{0,44},{4,0},{8,4},{12,8},{16,12},{20,16},{24,20},{28,24},{32,28},... | collective-permute-start | bytes 516104 | tf_op jit(solution)/shard_map/ppermute | solution.py:16
  143.0 2.4 collective-permute-start.15
  145.5 4.9 %collective-permute-start.51 = (bf16[288,256]{1,0:T(8,128)(2,1)S(1)}, bf16[288,256]{1,0:T(8,128)(2,1)S(1)}, u32[]{:S(2)}, u32[]{:S(2)}) collective-permute-start(bf16[288,256]{1,0:T(8,128)(2,1)S(1)} %get-tuple-element.78), channel_id=1, source_target_pairs={{0,2},{2,0},{1,3},{3,1},{4,6},{6,4},{5,7},{7,5},{8,10},{10,8},{9,1... | collective-permute-start | bytes 442376 | tf_op jit(solution)/shard_map/ppermute | solution.py:20
  150.5 4.2 %collective-permute-done.51 = bf16[288,256]{1,0:T(8,128)(2,1)S(1)} collective-permute-done((bf16[288,256]{1,0:T(8,128)(2,1)S(1)}, bf16[288,256]{1,0:T(8,128)(2,1)S(1)}, u32[]{:S(2)}, u32[]{:S(2)}) %collective-permute-start.51) | collective-permute-done | bytes 147488 | tf_op jit(solution)/shard_map/ppermute | solution.py:20
  154.9 1.9 collective-permute-start.52
  156.8 2.4 collective-permute-start.67
  159.2 3.5 %collective-permute-start.32 = (f32[2,128]{1,0:T(2,128)S(1)}, f32[2,128]{1,0:T(2,128)S(1)}, u32[]{:S(2)}, u32[]{:S(2)}) collective-permute-start(f32[2,128]{1,0:T(2,128)S(1)} %pad_maximum_fusion.21), channel_id=1, source_target_pairs={{0,96},{96,192},{192,288},{288,384},{384,480},{480,576},{576,672},... | collective-permute-start | bytes 3080 | tf_op jit(solution)/shard_map/ppermute | solution.py:166
  162.8 4.9 %collective-permute-start.16 = (bf16[288,512]{1,0:T(8,128)(2,1)S(1)}, bf16[288,512]{1,0:T(8,128)(2,1)S(1)}, u32[]{:S(2)}, u32[]{:S(2)}) collective-permute-start(bf16[288,512]{1,0:T(8,128)(2,1)S(1)} %get-tuple-element.80), channel_id=1, source_target_pairs={{0,2},{2,0},{1,3},{3,1},{4,6},{6,4},{5,7},{7,5},{8,10},{10,8},{9,1... | collective-permute-start | bytes 884744 | tf_op jit(solution)/shard_map/ppermute | solution.py:20
  172.3 5.6 %collective-permute-start.53 = (bf16[48,1792]{1,0:T(8,128)(2,1)S(1)}, bf16[48,1792]{1,0:T(8,128)(2,1)S(1)}, u32[]{:S(2)}, u32[]{:S(2)}) collective-permute-start(bf16[48,1792]{1,0:T(8,128)(2,1)S(1)} %get-tuple-element.96), channel_id=1, source_target_pairs={{0,44},{4,0},{8,4},{12,8},{16,12},{20,16},{24,20},{28,24},{32,28},... | collective-permute-start | bytes 516104 | tf_op jit(solution)/shard_map/ppermute | solution.py:16
  179.5 2.1 collective-permute-start.17
  181.7 5.3 %collective-permute-start.55 = (bf16[48,1792]{1,0:T(8,128)(2,1)S(1)}, bf16[48,1792]{1,0:T(8,128)(2,1)S(1)}, u32[]{:S(2)}, u32[]{:S(2)}) collective-permute-start(bf16[48,1792]{1,0:T(8,128)(2,1)S(1)} %get-tuple-element.105), channel_id=1, source_target_pairs={{0,44},{4,0},{8,4},{12,8},{16,12},{20,16},{24,20},{28,24},{32,28},... | collective-permute-start | bytes 516104 | tf_op jit(solution)/shard_map/ppermute | solution.py:16
  187.0 1.9 collective-permute-start.56
  189.8 5.1 %collective-permute-start.18 = (bf16[48,1792]{1,0:T(8,128)(2,1)S(1)}, bf16[48,1792]{1,0:T(8,128)(2,1)S(1)}, u32[]{:S(2)}, u32[]{:S(2)}) collective-permute-start(bf16[48,1792]{1,0:T(8,128)(2,1)S(1)} %get-tuple-element.118), channel_id=1, source_target_pairs={{0,44},{4,0},{8,4},{12,8},{16,12},{20,16},{24,20},{28,24},{32,28},... | collective-permute-start | bytes 516104 | tf_op jit(solution)/shard_map/ppermute | solution.py:16
  195.6 1.9 collective-permute-start.19
  199.6 5.1 %collective-permute-start.57 = (bf16[48,1792]{1,0:T(8,128)(2,1)S(1)}, bf16[48,1792]{1,0:T(8,128)(2,1)S(1)}, u32[]{:S(2)}, u32[]{:S(2)}) collective-permute-start(bf16[48,1792]{1,0:T(8,128)(2,1)S(1)} %select_add_fusion.3), channel_id=1, source_target_pairs={{0,44},{4,0},{8,4},{12,8},{16,12},{20,16},{24,20},{28,24},{32,28},... | collective-permute-start | bytes 516104 | tf_op jit(solution)/shard_map/ppermute | solution.py:16
  205.4 3.4 %collective-permute-start.20 = (bf16[48,1792]{1,0:T(8,128)(2,1)S(1)}, bf16[48,1792]{1,0:T(8,128)(2,1)S(1)}, u32[]{:S(2)}, u32[]{:S(2)}) collective-permute-start(bf16[48,1792]{1,0:T(8,128)(2,1)S(1)} %get-tuple-element.127), channel_id=1, source_target_pairs={{0,44},{4,0},{8,4},{12,8},{16,12},{20,16},{24,20},{28,24},{32,28},... | collective-permute-start | bytes 516104 | tf_op jit(solution)/shard_map/ppermute | solution.py:16
  208.8 2.5 collective-permute-start.21
  211.3 4.6 %collective-permute-start.59 = (bf16[48,1792]{1,0:T(8,128)(2,1)S(1)}, bf16[48,1792]{1,0:T(8,128)(2,1)S(1)}, u32[]{:S(2)}, u32[]{:S(2)}) collective-permute-start(bf16[48,1792]{1,0:T(8,128)(2,1)S(1)} %get-tuple-element.109), channel_id=1, source_target_pairs={{0,44},{4,0},{8,4},{12,8},{16,12},{20,16},{24,20},{28,24},{32,28},... | collective-permute-start | bytes 516104 | tf_op jit(solution)/shard_map/ppermute | solution.py:16
  215.9 1.9 collective-permute-start.60
  219.8 5.1 %collective-permute-start.22 = (bf16[48,1792]{1,0:T(8,128)(2,1)S(1)}, bf16[48,1792]{1,0:T(8,128)(2,1)S(1)}, u32[]{:S(2)}, u32[]{:S(2)}) collective-permute-start(bf16[48,1792]{1,0:T(8,128)(2,1)S(1)} %select_add_fusion.7), channel_id=1, source_target_pairs={{0,44},{4,0},{8,4},{12,8},{16,12},{20,16},{24,20},{28,24},{32,28},... | collective-permute-start | bytes 516104 | tf_op jit(solution)/shard_map/ppermute | solution.py:16
  225.1 1.9 collective-permute-start.62
  227.9 5.6 %collective-permute-start.24 = (bf16[48,1792]{1,0:T(8,128)(2,1)S(1)}, bf16[48,1792]{1,0:T(8,128)(2,1)S(1)}, u32[]{:S(2)}, u32[]{:S(2)}) collective-permute-start(bf16[48,1792]{1,0:T(8,128)(2,1)S(1)} %get-tuple-element.131), channel_id=1, source_target_pairs={{0,44},{4,0},{8,4},{12,8},{16,12},{20,16},{24,20},{28,24},{32,28},... | collective-permute-start | bytes 516104 | tf_op jit(solution)/shard_map/ppermute | solution.py:16
  236.7 5.6 %collective-permute-start.61 = (bf16[2,48,1792]{2,1,0:T(8,128)(2,1)S(1)}, bf16[2,48,1792]{2,1,0:T(8,128)(2,1)S(1)}, u32[]{:S(2)}, u32[]{:S(2)}) collective-permute-start(bf16[2,48,1792]{2,1,0:T(8,128)(2,1)S(1)} %pad_maximum_fusion.16), channel_id=1, source_target_pairs={{0,44},{4,0},{8,4},{12,8},{16,12},{20,16},{24,20},{28,24},{32,28},... | collective-permute-start | bytes 1032200 | tf_op jit(solution)/shard_map/ppermute | solution.py:16
  244.4 5.1 %collective-permute-start.26 = (bf16[2,48,1792]{2,1,0:T(8,128)(2,1)S(1)}, bf16[2,48,1792]{2,1,0:T(8,128)(2,1)S(1)}, u32[]{:S(2)}, u32[]{:S(2)}) collective-permute-start(bf16[2,48,1792]{2,1,0:T(8,128)(2,1)S(1)} %pad_maximum_fusion.13), channel_id=1, source_target_pairs={{0,44},{4,0},{8,4},{12,8},{16,12},{20,16},{24,20},{28,24},{32,28},... | collective-permute-start | bytes 1032200 | tf_op jit(solution)/shard_map/ppermute | solution.py:16
  250.0 2.1 collective-permute-start.64
  252.2 3.8 %collective-permute-done.27 = bf16[2,48,1792]{2,1,0:T(8,128)(2,1)S(1)} collective-permute-done((bf16[2,48,1792]{2,1,0:T(8,128)(2,1)S(1)}, bf16[2,48,1792]{2,1,0:T(8,128)(2,1)S(1)}, u32[]{:S(2)}, u32[]{:S(2)}) %collective-permute-start.27) | collective-permute-done | bytes 344096 | tf_op jit(solution)/shard_map/ppermute | solution.py:16
  258.1 3.8 %collective-permute-start.29 = (bf16[2,48,1792]{2,1,0:T(8,128)(2,1)S(1)}, bf16[2,48,1792]{2,1,0:T(8,128)(2,1)S(1)}, u32[]{:S(2)}, u32[]{:S(2)}) collective-permute-start(bf16[2,48,1792]{2,1,0:T(8,128)(2,1)S(1)} %maximum_add_fusion.1), channel_id=1, source_target_pairs={{0,4},{4,8},{8,12},{12,16},{16,20},{20,24},{24,28},{28,32},{32,36}... | collective-permute-start | bytes 1032200 | tf_op jit(solution)/shard_map/ppermute | solution.py:16
  261.9 2.3 collective-permute-done.64
  264.3 4.2 %collective-permute-start.28 = (bf16[2,48,1792]{2,1,0:T(8,128)(2,1)S(1)}, bf16[2,48,1792]{2,1,0:T(8,128)(2,1)S(1)}, u32[]{:S(2)}, u32[]{:S(2)}) collective-permute-start(bf16[2,48,1792]{2,1,0:T(8,128)(2,1)S(1)} %maximum_add_fusion), channel_id=1, source_target_pairs={{0,44},{4,0},{8,4},{12,8},{16,12},{20,16},{24,20},{28,24},{32,28},... | collective-permute-start | bytes 1032200 | tf_op jit(solution)/shard_map/ppermute | solution.py:16
  272.0 3.8 %collective-permute-start.65 = (bf16[2,48,1792]{2,1,0:T(8,128)(2,1)S(1)}, bf16[2,48,1792]{2,1,0:T(8,128)(2,1)S(1)}, u32[]{:S(2)}, u32[]{:S(2)}) collective-permute-start(bf16[2,48,1792]{2,1,0:T(8,128)(2,1)S(1)} %maximum_add_fusion.6), channel_id=1, source_target_pairs={{0,44},{4,0},{8,4},{12,8},{16,12},{20,16},{24,20},{28,24},{32,28},... | collective-permute-start | bytes 1032200 | tf_op jit(solution)/shard_map/ppermute | solution.py:16
  276.7 1.9 collective-permute-start.31
  278.7 2.7 collective-permute-done.66
  281.4 2.9 collective-permute-start.30
  284.5 3.6 %collective-permute-start.69 = (bf16[3,24,1792]{2,1,0:T(8,128)(2,1)S(1)}, bf16[3,24,1792]{2,1,0:T(8,128)(2,1)S(1)}, u32[]{:S(2)}, u32[]{:S(2)}) collective-permute-start(bf16[3,24,1792]{2,1,0:T(8,128)(2,1)S(1)} %get-tuple-element.93), channel_id=1, source_target_pairs={{96,48},{144,0},{192,144},{240,96},{288,240},{336,192},{384,336},{... | collective-permute-start | bytes 774152 | tf_op jit(solution)/shard_map/ppermute | solution.py:210
  288.1 1.9 collective-permute-start.68
  291.3 4.3 %collective-permute-start.34 = (bf16[3,24,1792]{2,1,0:T(8,128)(2,1)S(1)}, bf16[3,24,1792]{2,1,0:T(8,128)(2,1)S(1)}, u32[]{:S(2)}, u32[]{:S(2)}) collective-permute-start(bf16[3,24,1792]{2,1,0:T(8,128)(2,1)S(1)} %get-tuple-element.115), channel_id=1, source_target_pairs={{0,144},{48,96},{96,240},{144,192},{192,336},{240,288},{288,432},{... | collective-permute-start | bytes 774152 | tf_op jit(solution)/shard_map/ppermute | solution.py:210
  295.6 2.3 collective-permute-start.33
  299.6 2.1 collective-permute-done.34
  302.0 3.1 collective-permute-done.33
  (235 shorter events, 69.7 us)
Async XLA Ops:
  4.5 11.1 %collective-permute-start.35 = (bf16[3,24,1792]{2,1,0:T(8,128)(2,1)S(1)}, bf16[3,24,1792]{2,1,0:T(8,128)(2,1)S(1)}, u32[]{:S(2)}, u32[]{:S(2)}) collective-permute-start(bf16[3,24,1792]{2,1,0:T(8,128)(2,1)S(1)} %bitcast.361), channel_id=1, source_target_pairs={{0,48},{48,0},{1,49},{49,1},{2,50},{50,2},{3,51},{51,3},{4,52},{52... | collective-permute-start | bytes 774152 | tf_op jit(solution)/shard_map/ppermute | solution.py:20
  9.1 23.1 %collective-permute-start = (bf16[3,24,1792]{2,1,0:T(8,128)(2,1)}, bf16[3,24,1792]{2,1,0:T(8,128)(2,1)S(1)}, u32[]{:S(2)}, u32[]{:S(2)}) collective-permute-start(bf16[3,24,1792]{2,1,0:T(8,128)(2,1)} %bitcast.10), channel_id=1, source_target_pairs={{0,48},{48,0},{1,49},{49,1},{2,50},{50,2},{3,51},{51,3},{4,52},{52... | collective-permute-start | bytes 774152 | tf_op jit(solution)/shard_map/ppermute | solution.py:20
  15.6 24.5 %collective-permute-start.36 = (bf16[2,48,1792]{2,1,0:T(8,128)(2,1)S(1)}, bf16[2,48,1792]{2,1,0:T(8,128)(2,1)}, u32[]{:S(2)}, u32[]{:S(2)}) collective-permute-start(bf16[2,48,1792]{2,1,0:T(8,128)(2,1)S(1)} %pad_maximum_fusion.15), channel_id=1, source_target_pairs={{0,44},{4,0},{8,4},{12,8},{16,12},{20,16},{24,20},{28,24},{32,28},... | collective-permute-start | bytes 1032200 | tf_op jit(solution)/shard_map/ppermute | solution.py:16
  30.2 14.1 %collective-permute-start.40 = (bf16[2,48,1792]{2,1,0:T(8,128)(2,1)S(1)}, bf16[2,48,1792]{2,1,0:T(8,128)(2,1)S(1)}, u32[]{:S(2)}, u32[]{:S(2)}) collective-permute-start(bf16[2,48,1792]{2,1,0:T(8,128)(2,1)S(1)} %pad_maximum_fusion.10), channel_id=1, source_target_pairs={{0,4},{4,8},{8,12},{12,16},{16,20},{20,24},{24,28},{28,32},{32,36}... | collective-permute-start | bytes 1032200 | tf_op jit(solution)/shard_map/ppermute | solution.py:16
  32.2 18.2 %collective-permute-start.5 = (bf16[2,48,1792]{2,1,0:T(8,128)(2,1)S(1)}, bf16[2,48,1792]{2,1,0:T(8,128)(2,1)}, u32[]{:S(2)}, u32[]{:S(2)}) collective-permute-start(bf16[2,48,1792]{2,1,0:T(8,128)(2,1)S(1)} %pad_maximum_fusion.11), channel_id=1, source_target_pairs={{0,4},{4,8},{8,12},{12,16},{16,20},{20,24},{24,28},{28,32},{32,36}... | collective-permute-start | bytes 1032200 | tf_op jit(solution)/shard_map/ppermute | solution.py:16
  35.0 18.6 %collective-permute-start.1 = (bf16[2,48,1792]{2,1,0:T(8,128)(2,1)}, bf16[2,48,1792]{2,1,0:T(8,128)(2,1)}, u32[]{:S(2)}, u32[]{:S(2)}) collective-permute-start(bf16[2,48,1792]{2,1,0:T(8,128)(2,1)} %pad_maximum_fusion.12), channel_id=1, source_target_pairs={{0,44},{4,0},{8,4},{12,8},{16,12},{20,16},{24,20},{28,24},{32,28},... | collective-permute-start | bytes 1032200 | tf_op jit(solution)/shard_map/ppermute | solution.py:16
  40.1 18.6 %collective-permute-start.37 = (bf16[2,48,1792]{2,1,0:T(8,128)(2,1)}, bf16[2,48,1792]{2,1,0:T(8,128)(2,1)S(1)}, u32[]{:S(2)}, u32[]{:S(2)}) collective-permute-start(bf16[2,48,1792]{2,1,0:T(8,128)(2,1)} %collective-permute-done.36), channel_id=1, source_target_pairs={{0,44},{4,0},{8,4},{12,8},{16,12},{20,16},{24,20},{28,24},{32,28},... | collective-permute-start | bytes 1032200 | tf_op jit(solution)/shard_map/ppermute | solution.py:16
  44.3 16.3 %collective-permute-start.41 = (bf16[2,48,1792]{2,1,0:T(8,128)(2,1)S(1)}, bf16[2,48,1792]{2,1,0:T(8,128)(2,1)S(1)}, u32[]{:S(2)}, u32[]{:S(2)}) collective-permute-start(bf16[2,48,1792]{2,1,0:T(8,128)(2,1)S(1)} %collective-permute-done.40), channel_id=1, source_target_pairs={{0,4},{4,8},{8,12},{12,16},{16,20},{20,24},{24,28},{28,32},{32,36}... | collective-permute-start | bytes 1032200 | tf_op jit(solution)/shard_map/ppermute | solution.py:16
  50.4 15.2 %collective-permute-start.6 = (bf16[2,48,1792]{2,1,0:T(8,128)(2,1)}, bf16[2,48,1792]{2,1,0:T(8,128)(2,1)S(1)}, u32[]{:S(2)}, u32[]{:S(2)}) collective-permute-start(bf16[2,48,1792]{2,1,0:T(8,128)(2,1)} %collective-permute-done.5), channel_id=1, source_target_pairs={{0,4},{4,8},{8,12},{12,16},{16,20},{20,24},{24,28},{28,32},{32,36}... | collective-permute-start | bytes 1032200 | tf_op jit(solution)/shard_map/ppermute | solution.py:16
  53.5 14.0 %collective-permute-start.2 = (bf16[2,48,1792]{2,1,0:T(8,128)(2,1)}, bf16[2,48,1792]{2,1,0:T(8,128)(2,1)S(1)}, u32[]{:S(2)}, u32[]{:S(2)}) collective-permute-start(bf16[2,48,1792]{2,1,0:T(8,128)(2,1)} %collective-permute-done.1), channel_id=1, source_target_pairs={{0,44},{4,0},{8,4},{12,8},{16,12},{20,16},{24,20},{28,24},{32,28},... | collective-permute-start | bytes 1032200 | tf_op jit(solution)/shard_map/ppermute | solution.py:16
  58.7 14.0 %collective-permute-start.38 = (bf16[2,48,1792]{2,1,0:T(8,128)(2,1)S(1)}, bf16[2,48,1792]{2,1,0:T(8,128)(2,1)S(1)}, u32[]{:S(2)}, u32[]{:S(2)}) collective-permute-start(bf16[2,48,1792]{2,1,0:T(8,128)(2,1)S(1)} %collective-permute-done.37), channel_id=1, source_target_pairs={{0,44},{4,0},{8,4},{12,8},{16,12},{20,16},{24,20},{28,24},{32,28},... | collective-permute-start | bytes 1032200 | tf_op jit(solution)/shard_map/ppermute | solution.py:16
  60.6 14.0 %collective-permute-start.42 = (bf16[2,48,1792]{2,1,0:T(8,128)(2,1)S(1)}, bf16[2,48,1792]{2,1,0:T(8,128)(2,1)S(1)}, u32[]{:S(2)}, u32[]{:S(2)}) collective-permute-start(bf16[2,48,1792]{2,1,0:T(8,128)(2,1)S(1)} %collective-permute-done.41), channel_id=1, source_target_pairs={{0,4},{4,8},{8,12},{12,16},{16,20},{20,24},{24,28},{28,32},{32,36}... | collective-permute-start | bytes 1032200 | tf_op jit(solution)/shard_map/ppermute | solution.py:16
  65.6 14.1 %collective-permute-start.7 = (bf16[2,48,1792]{2,1,0:T(8,128)(2,1)S(1)}, bf16[2,48,1792]{2,1,0:T(8,128)(2,1)S(1)}, u32[]{:S(2)}, u32[]{:S(2)}) collective-permute-start(bf16[2,48,1792]{2,1,0:T(8,128)(2,1)S(1)} %collective-permute-done.6), channel_id=1, source_target_pairs={{0,4},{4,8},{8,12},{12,16},{16,20},{20,24},{24,28},{28,32},{32,36}... | collective-permute-start | bytes 1032200 | tf_op jit(solution)/shard_map/ppermute | solution.py:16
  67.5 15.1 %collective-permute-start.3 = (bf16[2,48,1792]{2,1,0:T(8,128)(2,1)S(1)}, bf16[2,48,1792]{2,1,0:T(8,128)(2,1)S(1)}, u32[]{:S(2)}, u32[]{:S(2)}) collective-permute-start(bf16[2,48,1792]{2,1,0:T(8,128)(2,1)S(1)} %collective-permute-done.2), channel_id=1, source_target_pairs={{0,44},{4,0},{8,4},{12,8},{16,12},{20,16},{24,20},{28,24},{32,28},... | collective-permute-start | bytes 1032200 | tf_op jit(solution)/shard_map/ppermute | solution.py:16
  72.7 16.0 %collective-permute-start.39 = (bf16[48,1792]{1,0:T(8,128)(2,1)S(1)}, bf16[48,1792]{1,0:T(8,128)(2,1)S(1)}, u32[]{:S(2)}, u32[]{:S(2)}) collective-permute-start(bf16[48,1792]{1,0:T(8,128)(2,1)S(1)} %get-tuple-element.140), channel_id=1, source_target_pairs={{0,44},{4,0},{8,4},{12,8},{16,12},{20,16},{24,20},{28,24},{32,28},... | collective-permute-start | bytes 516104 | tf_op jit(solution)/shard_map/ppermute | solution.py:16
  75.6 15.1 %collective-permute-start.43 = (bf16[48,1792]{1,0:T(8,128)(2,1)S(1)}, bf16[48,1792]{1,0:T(8,128)(2,1)S(1)}, u32[]{:S(2)}, u32[]{:S(2)}) collective-permute-start(bf16[48,1792]{1,0:T(8,128)(2,1)S(1)} %get-tuple-element.142), channel_id=1, source_target_pairs={{0,4},{4,8},{8,12},{12,16},{16,20},{20,24},{24,28},{28,32},{32,36}... | collective-permute-start | bytes 516104 | tf_op jit(solution)/shard_map/ppermute | solution.py:16
  80.6 14.1 %collective-permute-start.8 = (bf16[48,1792]{1,0:T(8,128)(2,1)S(1)}, bf16[48,1792]{1,0:T(8,128)(2,1)S(1)}, u32[]{:S(2)}, u32[]{:S(2)}) collective-permute-start(bf16[48,1792]{1,0:T(8,128)(2,1)S(1)} %get-tuple-element.147), channel_id=1, source_target_pairs={{0,4},{4,8},{8,12},{12,16},{16,20},{20,24},{24,28},{28,32},{32,36}... | collective-permute-start | bytes 516104 | tf_op jit(solution)/shard_map/ppermute | solution.py:16
  83.6 13.5 %collective-permute-start.4 = (bf16[48,1792]{1,0:T(8,128)(2,1)S(1)}, bf16[48,1792]{1,0:T(8,128)(2,1)S(1)}, u32[]{:S(2)}, u32[]{:S(2)}) collective-permute-start(bf16[48,1792]{1,0:T(8,128)(2,1)S(1)} %get-tuple-element.149), channel_id=1, source_target_pairs={{0,44},{4,0},{8,4},{12,8},{16,12},{20,16},{24,20},{28,24},{32,28},... | collective-permute-start | bytes 516104 | tf_op jit(solution)/shard_map/ppermute | solution.py:16
  88.8 13.6 %collective-permute-start.44 = (bf16[48,1792]{1,0:T(8,128)(2,1)S(1)}, bf16[48,1792]{1,0:T(8,128)(2,1)S(1)}, u32[]{:S(2)}, u32[]{:S(2)}) collective-permute-start(bf16[48,1792]{1,0:T(8,128)(2,1)S(1)} %collective-permute-done.39), channel_id=1, source_target_pairs={{0,44},{4,0},{8,4},{12,8},{16,12},{20,16},{24,20},{28,24},{32,28},... | collective-permute-start | bytes 516104 | tf_op jit(solution)/shard_map/ppermute | solution.py:16
  90.7 22.7 %collective-permute-start.47 = (bf16[48,1792]{1,0:T(8,128)(2,1)S(1)}, bf16[48,1792]{1,0:T(8,128)(2,1)S(1)}, u32[]{:S(2)}, u32[]{:S(2)}) collective-permute-start(bf16[48,1792]{1,0:T(8,128)(2,1)S(1)} %collective-permute-done.43), channel_id=1, source_target_pairs={{0,4},{4,8},{8,12},{12,16},{16,20},{20,24},{24,28},{28,32},{32,36}... | collective-permute-start | bytes 516104 | tf_op jit(solution)/shard_map/ppermute | solution.py:16
  94.7 20.7 %collective-permute-start.12 = (bf16[48,1792]{1,0:T(8,128)(2,1)S(1)}, bf16[48,1792]{1,0:T(8,128)(2,1)S(1)}, u32[]{:S(2)}, u32[]{:S(2)}) collective-permute-start(bf16[48,1792]{1,0:T(8,128)(2,1)S(1)} %collective-permute-done.8), channel_id=1, source_target_pairs={{0,4},{4,8},{8,12},{12,16},{16,20},{20,24},{24,28},{28,32},{32,36}... | collective-permute-start | bytes 516104 | tf_op jit(solution)/shard_map/ppermute | solution.py:16
  97.1 9.8 %collective-permute-start.9 = (bf16[48,1792]{1,0:T(8,128)(2,1)S(1)}, bf16[48,1792]{1,0:T(8,128)(2,1)S(1)}, u32[]{:S(2)}, u32[]{:S(2)}) collective-permute-start(bf16[48,1792]{1,0:T(8,128)(2,1)S(1)} %collective-permute-done.4), channel_id=1, source_target_pairs={{0,44},{4,0},{8,4},{12,8},{16,12},{20,16},{24,20},{28,24},{32,28},... | collective-permute-start | bytes 516104 | tf_op jit(solution)/shard_map/ppermute | solution.py:16
  102.4 15.9 %collective-permute-start.45 = (bf16[48,1792]{1,0:T(8,128)(2,1)S(1)}, bf16[48,1792]{1,0:T(8,128)(2,1)S(1)}, u32[]{:S(2)}, u32[]{:S(2)}) collective-permute-start(bf16[48,1792]{1,0:T(8,128)(2,1)S(1)} %collective-permute-done.44), channel_id=1, source_target_pairs={{0,44},{4,0},{8,4},{12,8},{16,12},{20,16},{24,20},{28,24},{32,28},... | collective-permute-start | bytes 516104 | tf_op jit(solution)/shard_map/ppermute | solution.py:16
  107.8 20.4 %collective-permute-start.10 = (bf16[48,1792]{1,0:T(8,128)(2,1)S(1)}, bf16[48,1792]{1,0:T(8,128)(2,1)S(1)}, u32[]{:S(2)}, u32[]{:S(2)}) collective-permute-start(bf16[48,1792]{1,0:T(8,128)(2,1)S(1)} %collective-permute-done.9), channel_id=1, source_target_pairs={{0,44},{4,0},{8,4},{12,8},{16,12},{20,16},{24,20},{28,24},{32,28},... | collective-permute-start | bytes 516104 | tf_op jit(solution)/shard_map/ppermute | solution.py:16
  113.4 10.3 %collective-permute-start.48 = (bf16[48,1792]{1,0:T(8,128)(2,1)S(1)}, bf16[48,1792]{1,0:T(8,128)(2,1)S(1)}, u32[]{:S(2)}, u32[]{:S(2)}) collective-permute-start(bf16[48,1792]{1,0:T(8,128)(2,1)S(1)} %collective-permute-done.47), channel_id=1, source_target_pairs={{0,4},{4,8},{8,12},{12,16},{16,20},{20,24},{24,28},{28,32},{32,36}... | collective-permute-start | bytes 516104 | tf_op jit(solution)/shard_map/ppermute | solution.py:16
  115.4 10.3 %collective-permute-start.13 = (bf16[48,1792]{1,0:T(8,128)(2,1)S(1)}, bf16[48,1792]{1,0:T(8,128)(2,1)S(1)}, u32[]{:S(2)}, u32[]{:S(2)}) collective-permute-start(bf16[48,1792]{1,0:T(8,128)(2,1)S(1)} %collective-permute-done.12), channel_id=1, source_target_pairs={{0,4},{4,8},{8,12},{12,16},{16,20},{20,24},{24,28},{28,32},{32,36}... | collective-permute-start | bytes 516104 | tf_op jit(solution)/shard_map/ppermute | solution.py:16
  118.3 20.8 %collective-permute-start.46 = (bf16[48,1792]{1,0:T(8,128)(2,1)S(1)}, bf16[48,1792]{1,0:T(8,128)(2,1)S(1)}, u32[]{:S(2)}, u32[]{:S(2)}) collective-permute-start(bf16[48,1792]{1,0:T(8,128)(2,1)S(1)} %collective-permute-done.45), channel_id=1, source_target_pairs={{0,44},{4,0},{8,4},{12,8},{16,12},{20,16},{24,20},{28,24},{32,28},... | collective-permute-start | bytes 516104 | tf_op jit(solution)/shard_map/ppermute | solution.py:16
  123.7 16.0 %collective-permute-start.49 = (bf16[48,1792]{1,0:T(8,128)(2,1)S(1)}, bf16[48,1792]{1,0:T(8,128)(2,1)S(1)}, u32[]{:S(2)}, u32[]{:S(2)}) collective-permute-start(bf16[48,1792]{1,0:T(8,128)(2,1)S(1)} %collective-permute-done.48), channel_id=1, source_target_pairs={{0,4},{4,8},{8,12},{12,16},{16,20},{20,24},{24,28},{28,32},{32,36}... | collective-permute-start | bytes 516104 | tf_op jit(solution)/shard_map/ppermute | solution.py:16
  143.0 19.7 %collective-permute-start.15 = (f32[288,512]{1,0:T(8,128)S(1)}, f32[288,512]{1,0:T(8,128)S(1)}, u32[]{:S(2)}, u32[]{:S(2)}) collective-permute-start(f32[288,512]{1,0:T(8,128)S(1)} %fusion.55), channel_id=1, source_target_pairs={{0,1},{1,0},{2,3},{3,2},{4,5},{5,4},{6,7},{7,6},{8,9},{9,8},{10,11... | collective-permute-start | bytes 1769480 | tf_op jit(solution)/shard_map/ppermute | solution.py:20
  145.5 9.2 %collective-permute-start.51 = (bf16[288,256]{1,0:T(8,128)(2,1)S(1)}, bf16[288,256]{1,0:T(8,128)(2,1)S(1)}, u32[]{:S(2)}, u32[]{:S(2)}) collective-permute-start(bf16[288,256]{1,0:T(8,128)(2,1)S(1)} %get-tuple-element.78), channel_id=1, source_target_pairs={{0,2},{2,0},{1,3},{3,1},{4,6},{6,4},{5,7},{7,5},{8,10},{10,8},{9,1... | collective-permute-start | bytes 442376 | tf_op jit(solution)/shard_map/ppermute | solution.py:20
  154.9 12.9 %collective-permute-start.52 = (bf16[288,512]{1,0:T(8,128)(2,1)S(1)}, bf16[288,512]{1,0:T(8,128)(2,1)S(1)}, u32[]{:S(2)}, u32[]{:S(2)}) collective-permute-start(bf16[288,512]{1,0:T(8,128)(2,1)S(1)} %pad_maximum_fusion.20), channel_id=1, source_target_pairs={{0,1},{1,0},{2,3},{3,2},{4,5},{5,4},{6,7},{7,6},{8,9},{9,8},{10,11... | collective-permute-start | bytes 884744 | tf_op jit(solution)/shard_map/ppermute | solution.py:20
  156.8 127.6 %collective-permute-start.67 = (f32[128]{0:T(128)S(1)}, f32[128]{0:T(128)S(1)}, u32[]{:S(2)}, u32[]{:S(2)}) collective-permute-start(f32[128]{0:T(128)S(1)} %copy-done.11), channel_id=1, source_target_pairs={{96,0},{192,96},{288,192},{384,288},{480,384},{576,480},{672,576},... | collective-permute-start | bytes 1544 | tf_op jit(solution)/shard_map/ppermute | solution.py:167
  159.2 131.4 %collective-permute-start.32 = (f32[2,128]{1,0:T(2,128)S(1)}, f32[2,128]{1,0:T(2,128)S(1)}, u32[]{:S(2)}, u32[]{:S(2)}) collective-permute-start(f32[2,128]{1,0:T(2,128)S(1)} %pad_maximum_fusion.21), channel_id=1, source_target_pairs={{0,96},{96,192},{192,288},{288,384},{384,480},{480,576},{576,672},... | collective-permute-start | bytes 3080 | tf_op jit(solution)/shard_map/ppermute | solution.py:166
  162.8 16.5 %collective-permute-start.16 = (bf16[288,512]{1,0:T(8,128)(2,1)S(1)}, bf16[288,512]{1,0:T(8,128)(2,1)S(1)}, u32[]{:S(2)}, u32[]{:S(2)}) collective-permute-start(bf16[288,512]{1,0:T(8,128)(2,1)S(1)} %get-tuple-element.80), channel_id=1, source_target_pairs={{0,2},{2,0},{1,3},{3,1},{4,6},{6,4},{5,7},{7,5},{8,10},{10,8},{9,1... | collective-permute-start | bytes 884744 | tf_op jit(solution)/shard_map/ppermute | solution.py:20
  169.9 11.8 %collective-permute-start.54 = (bf16[48,1792]{1,0:T(8,128)(2,1)S(1)}, bf16[48,1792]{1,0:T(8,128)(2,1)S(1)}, u32[]{:S(2)}, u32[]{:S(2)}) collective-permute-start(bf16[48,1792]{1,0:T(8,128)(2,1)S(1)} %get-tuple-element.101), channel_id=1, source_target_pairs={{0,4},{4,8},{8,12},{12,16},{16,20},{20,24},{24,28},{28,32},{32,36}... | collective-permute-start | bytes 516104 | tf_op jit(solution)/shard_map/ppermute | solution.py:16
  172.3 9.3 %collective-permute-start.53 = (bf16[48,1792]{1,0:T(8,128)(2,1)S(1)}, bf16[48,1792]{1,0:T(8,128)(2,1)S(1)}, u32[]{:S(2)}, u32[]{:S(2)}) collective-permute-start(bf16[48,1792]{1,0:T(8,128)(2,1)S(1)} %get-tuple-element.96), channel_id=1, source_target_pairs={{0,44},{4,0},{8,4},{12,8},{16,12},{20,16},{24,20},{28,24},{32,28},... | collective-permute-start | bytes 516104 | tf_op jit(solution)/shard_map/ppermute | solution.py:16
  179.5 9.4 %collective-permute-start.17 = (bf16[288,256]{1,0:T(8,128)(2,1)S(1)}, bf16[288,256]{1,0:T(8,128)(2,1)S(1)}, u32[]{:S(2)}, u32[]{:S(2)}) collective-permute-start(bf16[288,256]{1,0:T(8,128)(2,1)S(1)} %fusion.64), channel_id=1, source_target_pairs={{0,1},{1,0},{2,3},{3,2},{4,5},{5,4},{6,7},{7,6},{8,9},{9,8},{10,11... | collective-permute-start | bytes 442376 | tf_op jit(solution)/shard_map/ppermute | solution.py:20
  181.7 13.9 %collective-permute-start.55 = (bf16[48,1792]{1,0:T(8,128)(2,1)S(1)}, bf16[48,1792]{1,0:T(8,128)(2,1)S(1)}, u32[]{:S(2)}, u32[]{:S(2)}) collective-permute-start(bf16[48,1792]{1,0:T(8,128)(2,1)S(1)} %get-tuple-element.105), channel_id=1, source_target_pairs={{0,44},{4,0},{8,4},{12,8},{16,12},{20,16},{24,20},{28,24},{32,28},... | collective-permute-start | bytes 516104 | tf_op jit(solution)/shard_map/ppermute | solution.py:16
  187.0 10.5 %collective-permute-start.56 = (bf16[48,1792]{1,0:T(8,128)(2,1)S(1)}, bf16[48,1792]{1,0:T(8,128)(2,1)S(1)}, u32[]{:S(2)}, u32[]{:S(2)}) collective-permute-start(bf16[48,1792]{1,0:T(8,128)(2,1)S(1)} %get-tuple-element.106), channel_id=1, source_target_pairs={{0,4},{4,8},{8,12},{12,16},{16,20},{20,24},{24,28},{28,32},{32,36}... | collective-permute-start | bytes 516104 | tf_op jit(solution)/shard_map/ppermute | solution.py:16
  189.8 9.8 %collective-permute-start.18 = (bf16[48,1792]{1,0:T(8,128)(2,1)S(1)}, bf16[48,1792]{1,0:T(8,128)(2,1)S(1)}, u32[]{:S(2)}, u32[]{:S(2)}) collective-permute-start(bf16[48,1792]{1,0:T(8,128)(2,1)S(1)} %get-tuple-element.118), channel_id=1, source_target_pairs={{0,44},{4,0},{8,4},{12,8},{16,12},{20,16},{24,20},{28,24},{32,28},... | collective-permute-start | bytes 516104 | tf_op jit(solution)/shard_map/ppermute | solution.py:16
  195.6 9.6 %collective-permute-start.19 = (bf16[48,1792]{1,0:T(8,128)(2,1)S(1)}, bf16[48,1792]{1,0:T(8,128)(2,1)S(1)}, u32[]{:S(2)}, u32[]{:S(2)}) collective-permute-start(bf16[48,1792]{1,0:T(8,128)(2,1)S(1)} %get-tuple-element.123), channel_id=1, source_target_pairs={{0,4},{4,8},{8,12},{12,16},{16,20},{20,24},{24,28},{28,32},{32,36}... | collective-permute-start | bytes 516104 | tf_op jit(solution)/shard_map/ppermute | solution.py:16
  197.6 11.1 %collective-permute-start.58 = (bf16[48,1792]{1,0:T(8,128)(2,1)S(1)}, bf16[48,1792]{1,0:T(8,128)(2,1)S(1)}, u32[]{:S(2)}, u32[]{:S(2)}) collective-permute-start(bf16[48,1792]{1,0:T(8,128)(2,1)S(1)} %select_add_fusion.2), channel_id=1, source_target_pairs={{0,4},{4,8},{8,12},{12,16},{16,20},{20,24},{24,28},{28,32},{32,36}... | collective-permute-start | bytes 516104 | tf_op jit(solution)/shard_map/ppermute | solution.py:16
  199.6 11.6 %collective-permute-start.57 = (bf16[48,1792]{1,0:T(8,128)(2,1)S(1)}, bf16[48,1792]{1,0:T(8,128)(2,1)S(1)}, u32[]{:S(2)}, u32[]{:S(2)}) collective-permute-start(bf16[48,1792]{1,0:T(8,128)(2,1)S(1)} %select_add_fusion.3), channel_id=1, source_target_pairs={{0,44},{4,0},{8,4},{12,8},{16,12},{20,16},{24,20},{28,24},{32,28},... | collective-permute-start | bytes 516104 | tf_op jit(solution)/shard_map/ppermute | solution.py:16
  205.4 10.5 %collective-permute-start.20 = (bf16[48,1792]{1,0:T(8,128)(2,1)S(1)}, bf16[48,1792]{1,0:T(8,128)(2,1)S(1)}, u32[]{:S(2)}, u32[]{:S(2)}) collective-permute-start(bf16[48,1792]{1,0:T(8,128)(2,1)S(1)} %get-tuple-element.127), channel_id=1, source_target_pairs={{0,44},{4,0},{8,4},{12,8},{16,12},{20,16},{24,20},{28,24},{32,28},... | collective-permute-start | bytes 516104 | tf_op jit(solution)/shard_map/ppermute | solution.py:16
  208.8 9.1 %collective-permute-start.21 = (bf16[48,1792]{1,0:T(8,128)(2,1)S(1)}, bf16[48,1792]{1,0:T(8,128)(2,1)S(1)}, u32[]{:S(2)}, u32[]{:S(2)}) collective-permute-start(bf16[48,1792]{1,0:T(8,128)(2,1)S(1)} %get-tuple-element.128), channel_id=1, source_target_pairs={{0,4},{4,8},{8,12},{12,16},{16,20},{20,24},{24,28},{28,32},{32,36}... | collective-permute-start | bytes 516104 | tf_op jit(solution)/shard_map/ppermute | solution.py:16
  215.9 9.1 %collective-permute-start.60 = (bf16[48,1792]{1,0:T(8,128)(2,1)S(1)}, bf16[48,1792]{1,0:T(8,128)(2,1)S(1)}, u32[]{:S(2)}, u32[]{:S(2)}) collective-permute-start(bf16[48,1792]{1,0:T(8,128)(2,1)S(1)} %get-tuple-element.108), channel_id=1, source_target_pairs={{0,4},{4,8},{8,12},{12,16},{16,20},{20,24},{24,28},{28,32},{32,36}... | collective-permute-start | bytes 516104 | tf_op jit(solution)/shard_map/ppermute | solution.py:16
  217.9 9.2 %collective-permute-start.23 = (bf16[48,1792]{1,0:T(8,128)(2,1)S(1)}, bf16[48,1792]{1,0:T(8,128)(2,1)S(1)}, u32[]{:S(2)}, u32[]{:S(2)}) collective-permute-start(bf16[48,1792]{1,0:T(8,128)(2,1)S(1)} %select_add_fusion.6), channel_id=1, source_target_pairs={{0,4},{4,8},{8,12},{12,16},{16,20},{20,24},{24,28},{28,32},{32,36}... | collective-permute-start | bytes 516104 | tf_op jit(solution)/shard_map/ppermute | solution.py:16
  225.1 19.3 %collective-permute-start.62 = (bf16[2,48,1792]{2,1,0:T(8,128)(2,1)S(1)}, bf16[2,48,1792]{2,1,0:T(8,128)(2,1)S(1)}, u32[]{:S(2)}, u32[]{:S(2)}) collective-permute-start(bf16[2,48,1792]{2,1,0:T(8,128)(2,1)S(1)} %pad_maximum_fusion.17), channel_id=1, source_target_pairs={{0,4},{4,8},{8,12},{12,16},{16,20},{20,24},{24,28},{28,32},{32,36}... | collective-permute-start | bytes 1032200 | tf_op jit(solution)/shard_map/ppermute | solution.py:16
  227.9 8.7 %collective-permute-start.24 = (bf16[48,1792]{1,0:T(8,128)(2,1)S(1)}, bf16[48,1792]{1,0:T(8,128)(2,1)S(1)}, u32[]{:S(2)}, u32[]{:S(2)}) collective-permute-start(bf16[48,1792]{1,0:T(8,128)(2,1)S(1)} %get-tuple-element.131), channel_id=1, source_target_pairs={{0,44},{4,0},{8,4},{12,8},{16,12},{20,16},{24,20},{28,24},{32,28},... | collective-permute-start | bytes 516104 | tf_op jit(solution)/shard_map/ppermute | solution.py:16
  236.7 13.3 %collective-permute-start.61 = (bf16[2,48,1792]{2,1,0:T(8,128)(2,1)S(1)}, bf16[2,48,1792]{2,1,0:T(8,128)(2,1)S(1)}, u32[]{:S(2)}, u32[]{:S(2)}) collective-permute-start(bf16[2,48,1792]{2,1,0:T(8,128)(2,1)S(1)} %pad_maximum_fusion.16), channel_id=1, source_target_pairs={{0,44},{4,0},{8,4},{12,8},{16,12},{20,16},{24,20},{28,24},{32,28},... | collective-permute-start | bytes 1032200 | tf_op jit(solution)/shard_map/ppermute | solution.py:16
  242.4 13.6 %collective-permute-start.27 = (bf16[2,48,1792]{2,1,0:T(8,128)(2,1)S(1)}, bf16[2,48,1792]{2,1,0:T(8,128)(2,1)S(1)}, u32[]{:S(2)}, u32[]{:S(2)}) collective-permute-start(bf16[2,48,1792]{2,1,0:T(8,128)(2,1)S(1)} %pad_maximum_fusion.14), channel_id=1, source_target_pairs={{0,4},{4,8},{8,12},{12,16},{16,20},{20,24},{24,28},{28,32},{32,36}... | collective-permute-start | bytes 1032200 | tf_op jit(solution)/shard_map/ppermute | solution.py:16
  244.4 13.6 %collective-permute-start.26 = (bf16[2,48,1792]{2,1,0:T(8,128)(2,1)S(1)}, bf16[2,48,1792]{2,1,0:T(8,128)(2,1)S(1)}, u32[]{:S(2)}, u32[]{:S(2)}) collective-permute-start(bf16[2,48,1792]{2,1,0:T(8,128)(2,1)S(1)} %pad_maximum_fusion.13), channel_id=1, source_target_pairs={{0,44},{4,0},{8,4},{12,8},{16,12},{20,16},{24,20},{28,24},{32,28},... | collective-permute-start | bytes 1032200 | tf_op jit(solution)/shard_map/ppermute | solution.py:16
  250.0 14.3 %collective-permute-start.64 = (bf16[2,48,1792]{2,1,0:T(8,128)(2,1)S(1)}, bf16[2,48,1792]{2,1,0:T(8,128)(2,1)S(1)}, u32[]{:S(2)}, u32[]{:S(2)}) collective-permute-start(bf16[2,48,1792]{2,1,0:T(8,128)(2,1)S(1)} %maximum_add_fusion.5), channel_id=1, source_target_pairs={{0,4},{4,8},{8,12},{12,16},{16,20},{20,24},{24,28},{28,32},{32,36}... | collective-permute-start | bytes 1032200 | tf_op jit(solution)/shard_map/ppermute | solution.py:16
  256.0 12.5 %collective-permute-start.63 = (bf16[2,48,1792]{2,1,0:T(8,128)(2,1)S(1)}, bf16[2,48,1792]{2,1,0:T(8,128)(2,1)S(1)}, u32[]{:S(2)}, u32[]{:S(2)}) collective-permute-start(bf16[2,48,1792]{2,1,0:T(8,128)(2,1)S(1)} %maximum_add_fusion.4), channel_id=1, source_target_pairs={{0,44},{4,0},{8,4},{12,8},{16,12},{20,16},{24,20},{28,24},{32,28},... | collective-permute-start | bytes 1032200 | tf_op jit(solution)/shard_map/ppermute | solution.py:16
  258.1 13.9 %collective-permute-start.29 = (bf16[2,48,1792]{2,1,0:T(8,128)(2,1)S(1)}, bf16[2,48,1792]{2,1,0:T(8,128)(2,1)S(1)}, u32[]{:S(2)}, u32[]{:S(2)}) collective-permute-start(bf16[2,48,1792]{2,1,0:T(8,128)(2,1)S(1)} %maximum_add_fusion.1), channel_id=1, source_target_pairs={{0,4},{4,8},{8,12},{12,16},{16,20},{20,24},{24,28},{28,32},{32,36}... | collective-permute-start | bytes 1032200 | tf_op jit(solution)/shard_map/ppermute | solution.py:16
  264.3 12.4 %collective-permute-start.28 = (bf16[2,48,1792]{2,1,0:T(8,128)(2,1)S(1)}, bf16[2,48,1792]{2,1,0:T(8,128)(2,1)S(1)}, u32[]{:S(2)}, u32[]{:S(2)}) collective-permute-start(bf16[2,48,1792]{2,1,0:T(8,128)(2,1)S(1)} %maximum_add_fusion), channel_id=1, source_target_pairs={{0,44},{4,0},{8,4},{12,8},{16,12},{20,16},{24,20},{28,24},{32,28},... | collective-permute-start | bytes 1032200 | tf_op jit(solution)/shard_map/ppermute | solution.py:16
  268.5 12.8 %collective-permute-start.66 = (bf16[2,48,1792]{2,1,0:T(8,128)(2,1)S(1)}, bf16[2,48,1792]{2,1,0:T(8,128)(2,1)S(1)}, u32[]{:S(2)}, u32[]{:S(2)}) collective-permute-start(bf16[2,48,1792]{2,1,0:T(8,128)(2,1)S(1)} %maximum_add_fusion.7), channel_id=1, source_target_pairs={{0,4},{4,8},{8,12},{12,16},{16,20},{20,24},{24,28},{28,32},{32,36}... | collective-permute-start | bytes 1032200 | tf_op jit(solution)/shard_map/ppermute | solution.py:16
  272.0 12.3 %collective-permute-start.65 = (bf16[2,48,1792]{2,1,0:T(8,128)(2,1)S(1)}, bf16[2,48,1792]{2,1,0:T(8,128)(2,1)S(1)}, u32[]{:S(2)}, u32[]{:S(2)}) collective-permute-start(bf16[2,48,1792]{2,1,0:T(8,128)(2,1)S(1)} %maximum_add_fusion.6), channel_id=1, source_target_pairs={{0,44},{4,0},{8,4},{12,8},{16,12},{20,16},{24,20},{28,24},{32,28},... | collective-permute-start | bytes 1032200 | tf_op jit(solution)/shard_map/ppermute | solution.py:16
  276.7 13.3 %collective-permute-start.31 = (bf16[2,48,1792]{2,1,0:T(8,128)(2,1)S(1)}, bf16[2,48,1792]{2,1,0:T(8,128)(2,1)S(1)}, u32[]{:S(2)}, u32[]{:S(2)}) collective-permute-start(bf16[2,48,1792]{2,1,0:T(8,128)(2,1)S(1)} %maximum_add_fusion.3), channel_id=1, source_target_pairs={{0,4},{4,8},{8,12},{12,16},{16,20},{20,24},{24,28},{28,32},{32,36}... | collective-permute-start | bytes 1032200 | tf_op jit(solution)/shard_map/ppermute | solution.py:16
  281.4 9.1 %collective-permute-start.30 = (bf16[2,48,1792]{2,1,0:T(8,128)(2,1)S(1)}, bf16[2,48,1792]{2,1,0:T(8,128)(2,1)S(1)}, u32[]{:S(2)}, u32[]{:S(2)}) collective-permute-start(bf16[2,48,1792]{2,1,0:T(8,128)(2,1)S(1)} %maximum_add_fusion.2), channel_id=1, source_target_pairs={{0,44},{4,0},{8,4},{12,8},{16,12},{20,16},{24,20},{28,24},{32,28},... | collective-permute-start | bytes 1032200 | tf_op jit(solution)/shard_map/ppermute | solution.py:16
  284.5 13.6 %collective-permute-start.69 = (bf16[3,24,1792]{2,1,0:T(8,128)(2,1)S(1)}, bf16[3,24,1792]{2,1,0:T(8,128)(2,1)S(1)}, u32[]{:S(2)}, u32[]{:S(2)}) collective-permute-start(bf16[3,24,1792]{2,1,0:T(8,128)(2,1)S(1)} %get-tuple-element.93), channel_id=1, source_target_pairs={{96,48},{144,0},{192,144},{240,96},{288,240},{336,192},{384,336},{... | collective-permute-start | bytes 774152 | tf_op jit(solution)/shard_map/ppermute | solution.py:210
  288.1 10.3 %collective-permute-start.68 = (bf16[3,24,1792]{2,1,0:T(8,128)(2,1)S(1)}, bf16[3,24,1792]{2,1,0:T(8,128)(2,1)S(1)}, u32[]{:S(2)}, u32[]{:S(2)}) collective-permute-start(bf16[3,24,1792]{2,1,0:T(8,128)(2,1)S(1)} %get-tuple-element.92), channel_id=1, source_target_pairs={{96,0},{192,96},{288,192},{384,288},{480,384},{576,480},{672,576},... | collective-permute-start | bytes 774152 | tf_op jit(solution)/shard_map/ppermute | solution.py:209
  291.3 10.3 %collective-permute-start.34 = (bf16[3,24,1792]{2,1,0:T(8,128)(2,1)S(1)}, bf16[3,24,1792]{2,1,0:T(8,128)(2,1)S(1)}, u32[]{:S(2)}, u32[]{:S(2)}) collective-permute-start(bf16[3,24,1792]{2,1,0:T(8,128)(2,1)S(1)} %get-tuple-element.115), channel_id=1, source_target_pairs={{0,144},{48,96},{96,240},{144,192},{192,336},{240,288},{288,432},{... | collective-permute-start | bytes 774152 | tf_op jit(solution)/shard_map/ppermute | solution.py:210
  295.6 9.4 %collective-permute-start.33 = (bf16[3,24,1792]{2,1,0:T(8,128)(2,1)S(1)}, bf16[3,24,1792]{2,1,0:T(8,128)(2,1)S(1)}, u32[]{:S(2)}, u32[]{:S(2)}) collective-permute-start(bf16[3,24,1792]{2,1,0:T(8,128)(2,1)S(1)} %get-tuple-element.114), channel_id=1, source_target_pairs={{0,96},{96,192},{192,288},{288,384},{384,480},{480,576},{576,672},... | collective-permute-start | bytes 774152 | tf_op jit(solution)/shard_map/ppermute | solution.py:209
  (18 other events, 230.4 us)

commit v5 on v2

--- a/solution.py
+++ b/solution.py
@@ -26,7 +26,7 @@
     near = [half * groups + (group + k) % groups for k in range(groups)]
     far = [(1 - half) * groups + (group + k) % groups for k in range(groups)]
     ids = jnp.stack(near + far).astype(jnp.int32)
-    member = (routes[None, :, 0] == ids[:, None]).astype(jnp.int32)
+    member = (routes[None, :] == ids[:, None]).astype(jnp.int32)
     before = jnp.cumsum(member, axis=1) - member
     slot_ids = jnp.arange(width, dtype=jnp.int32)
     hit = (before[:, None, :] == slot_ids[None, :, None]) & (slot_ids < capacity)[None, :, None]
@@ -55,7 +55,7 @@
         total = around(total, -step) + parts[k]
     total = total.reshape(groups, 2, -1, total.shape[-1])
     blocks = jnp.stack([total[0], hop(total[2], -GROUP), hop(total[1], GROUP)])
-    return jnp.stack([blocks[:, 0], swap(blocks[:, 1], "half")])
+    return blocks[:, 0], blocks[:, 1]
 
 
 def reduce_rows(parts):
@@ -116,14 +116,27 @@
     columns = tokens_fwd.shape[2]
     hidden_width = w_gate.shape[2]
 
-    place_fwd = placing_of(routes_fwd[0], capacity, width)
-    place_bwd = placing_of(routes_bwd[0], capacity, width)
+    place_fwd = placing_of(routes_fwd[0, :, 0], capacity, width)
+    place_bwd = placing_of(routes_bwd[0, :, 0], capacity, width)
     send_fwd = jnp.dot(place_fwd, tokens_fwd[0], preferred_element_type=F32).astype(BF16)
     scaled = (cotangent[0].astype(F32) * gates_bwd[0]).astype(BF16)
     send_bwd = jnp.dot(place_bwd, scaled, preferred_element_type=F32).astype(BF16)
 
     got_fwd = dispatch(send_fwd.reshape(2, groups, width, columns), 1)
     got_bwd = dispatch(send_bwd.reshape(2, groups, width, columns), -1)
+
+    sections = lax.axis_size("section")
+    up = [(i, i + 1) for i in range(sections - 1)]
+    down = [(i + 1, i) for i in range(sections - 1)]
+    send_up = jnp.stack([routes_fwd[0, :, 0].astype(F32), gates_fwd[0, :, 0]])
+    send_down = routes_bwd[0, :, 0].astype(F32)
+    got_fwd[1], send_up, send_down = lax.optimization_barrier((got_fwd[1], send_up, send_down))
+    from_before = lax.ppermute(send_up, "section", up)
+    from_after = lax.ppermute(send_down, "section", down)
+    got_fwd[3], from_before, from_after = lax.optimization_barrier(
+        (got_fwd[3], from_before, from_after)
+    )
+
     partial_fwd = [
         jnp.concatenate(
             [
@@ -138,7 +151,7 @@
     gate_pre, up_pre = summed[:, :hidden_width], summed[:, hidden_width:]
     hidden = gather_rows((gate_pre * jax.nn.sigmoid(gate_pre) * up_pre).astype(BF16))
     out = [jnp.dot(rows, w_down[0], preferred_element_type=F32).astype(BF16) for rows in hidden]
-    back_fwd = collect(out, 1, groups).reshape(-1, columns)
+    back_fwd = collect(out, 1, groups)
 
     grad_hidden = reduce_rows([contract_last(rows, w_down[0]) for rows in got_bwd])
     saved = saved_half(saved_pre[0], capacity, width, -1)
@@ -155,19 +168,28 @@
         ).astype(BF16)
         for rows in grads
     ]
-    back_bwd = collect(grad_out, -1, groups).reshape(-1, columns)
+    back_bwd = collect(grad_out, -1, groups)
+
+    def shifted(values, shift):
+        across = [(2 * i + h, 2 * j + 1 - h) for i, j in shift for h in range(2)]
+        mine = lax.ppermute(values[0], "section", shift)
+        others = lax.ppermute(values[1], ("section", "half"), across)
+        return mine.reshape(-1, columns), others.reshape(-1, columns)
 
     def rows_of(placing, values):
+        mine, others = values
+        cut = mine.shape[0]
         return lax.dot_general(
-            placing, values, (((0,), (0,)), ((), ())), preferred_element_type=F32
+            placing[:cut], mine, (((0,), (0,)), ((), ())), preferred_element_type=F32
+        ) + lax.dot_general(
+            placing[cut:], others, (((0,), (0,)), ((), ())), preferred_element_type=F32
         )
 
-    layer_out = (rows_of(place_fwd, back_fwd) * gates_fwd[0]).astype(BF16)
-    layer_grad = rows_of(place_bwd, back_bwd).astype(BF16)
-    ends = lax.axis_size("section") - 1
-    forwarded = lax.ppermute(layer_out, "section", [(i, i + 1) for i in range(ends)])
-    returned = lax.ppermute(layer_grad, "section", [(i + 1, i) for i in range(ends)])
-    return (forwarded[None], returned[None])
+    place_before = placing_of(from_before[0].astype(jnp.int32), capacity, width)
+    place_after = placing_of(from_after.astype(jnp.int32), capacity, width)
+    forwarded = rows_of(place_before, shifted(back_fwd, up)) * from_before[1][:, None]
+    returned = rows_of(place_after, shifted(back_bwd, down))
+    return (forwarded.astype(BF16)[None], returned.astype(BF16)[None])
 
 
 def solution(mesh):

time: 297 us -> 337 us (1.13)
  the two profiles are of different devices: /device:TPU:102 before, /device:TPU:24 now
where the time goes in v5:
time: 337 us; the launch traced here: 335 us
  waiting for transfers between devices  172 us (51%)
  starting transfers between devices  126 us (37%)
  matrix products  15.1 us (4%)
  other arithmetic  12.4 us (4%)
  local copies, waits for them, and re-layouts  7.97 us (2%)
    ppermute x12, waiting for transfers between devices, around(): lax.ppermute(values, 'member', [(i, (i + step) % GROUP) for i in range(GR...  123 us
    ppermute x8, starting transfers between devices, hop(): lax.ppermute(values, RING, [(i, (i + step) % count) for i in range(count)])  46 us
    ppermute x12, starting transfers between devices, around(): lax.ppermute(values, 'member', [(i, (i + step) % GROUP) for i in range(GR...  37.3 us
    ppermute x8, waiting for transfers between devices, hop(): lax.ppermute(values, RING, [(i, (i + step) % count) for i in range(count)])  27.4 us
    ppermute x8, starting transfers between devices, swap(): return lax.ppermute(values, axis, [(0, 1), (1, 0)])  24.4 us
    ppermute x8, waiting for transfers between devices, swap(): return lax.ppermute(values, axis, [(0, 1), (1, 0)])  11.3 us
    ppermute x2, starting transfers between devices, shifted(): others = lax.ppermute(values[1], ('section', 'half'), across)  7.65 us
  transfers between devices with their start and end apart: 34, of which 21 were waited for; matrix products, arithmetic and copies ran while one was open for 8% of the time, Pallas kernels for 0%

profile of v5, /device:TPU:24, one launch (start us, length us, event | category | flops | bytes accessed | tf_op | source)
XLA Modules:
  0.0 335.4 jit_solution(16485243237266785069)
XLA Ops:
  2.1 1.3 convolution_convert_fusion.5
  3.5 3.5 %collective-permute-start = (bf16[3,24,1792]{2,1,0:T(8,128)(2,1)S(1)}, bf16[3,24,1792]{2,1,0:T(8,128)(2,1)S(1)}, u32[]{:S(2)}, u32[]{:S(2)}) collective-permute-start(bf16[3,24,1792]{2,1,0:T(8,128)(2,1)S(1)} %bitcast.230), channel_id=1, source_target_pairs={{0,48},{48,0},{1,49},{49,1},{2,50},{50,2},{3,51},{51,3},{4,52},{52... | collective-permute-start | bytes 774152 | tf_op jit(solution)/shard_map/ppermute | solution.py:20
  11.1 2.3 collective-permute-done
  13.5 11.0 %collective-permute-start.2 = (bf16[48,1792]{1,0:T(8,128)(2,1)S(1)}, bf16[48,1792]{1,0:T(8,128)(2,1)S(1)}, u32[]{:S(2)}, u32[]{:S(2)}) collective-permute-start(bf16[48,1792]{1,0:T(8,128)(2,1)S(1)} %get-tuple-element.44), channel_id=1, source_target_pairs={{0,16},{4,20},{8,24},{12,28},{16,32},{20,36},{24,40},{28,44},{32,0... | collective-permute-start | bytes 516104 | tf_op jit(solution)/shard_map/ppermute | solution.py:16
  24.5 5.6 %collective-permute-start.1 = (bf16[48,1792]{1,0:T(8,128)(2,1)S(1)}, bf16[48,1792]{1,0:T(8,128)(2,1)S(1)}, u32[]{:S(2)}, u32[]{:S(2)}) collective-permute-start(bf16[48,1792]{1,0:T(8,128)(2,1)S(1)} %get-tuple-element.45), channel_id=1, source_target_pairs={{0,32},{4,36},{8,40},{12,44},{16,0},{20,4},{24,8},{28,12},{32,16},... | collective-permute-start | bytes 516104 | tf_op jit(solution)/shard_map/ppermute | solution.py:16
  30.1 1.8 collective-permute-done.2
  32.0 14.2 %collective-permute-done.1 = bf16[48,1792]{1,0:T(8,128)(2,1)S(1)} collective-permute-done((bf16[48,1792]{1,0:T(8,128)(2,1)S(1)}, bf16[48,1792]{1,0:T(8,128)(2,1)S(1)}, u32[]{:S(2)}, u32[]{:S(2)}) %collective-permute-start.1) | collective-permute-done | bytes 172064 | tf_op jit(solution)/shard_map/ppermute | solution.py:16
  46.2 2.1 collective-permute-start.3
  48.9 15.0 %collective-permute-done.3 = bf16[144,1792]{1,0:T(8,128)(2,1)S(1)} collective-permute-done((bf16[144,1792]{1,0:T(8,128)(2,1)S(1)}, bf16[144,1792]{1,0:T(8,128)(2,1)S(1)}, u32[]{:S(2)}, u32[]{:S(2)}) %collective-permute-start.3) | collective-permute-done | bytes 516128 | tf_op jit(solution)/shard_map/ppermute | solution.py:38
  64.0 4.7 %collective-permute-start.6 = (f32[2,128]{1,0:T(2,128)S(1)}, f32[2,128]{1,0:T(2,128)S(1)}, u32[]{:S(2)}, u32[]{:S(2)}) collective-permute-start(f32[2,128]{1,0:T(2,128)S(1)} %pad_maximum_fusion.9), channel_id=1, source_target_pairs={{0,96},{96,192},{192,288},{288,384},{384,480},{480,576},{576,672},... | collective-permute-start | bytes 3080 | tf_op jit(solution)/shard_map/ppermute | solution.py:134
  68.7 1.9 collective-permute-start.7
  70.6 1.9 collective-permute-start.4
  73.2 12.8 %collective-permute-done.4 = bf16[144,1792]{1,0:T(8,128)(2,1)S(1)} collective-permute-done((bf16[144,1792]{1,0:T(8,128)(2,1)S(1)}, bf16[144,1792]{1,0:T(8,128)(2,1)S(1)}, u32[]{:S(2)}, u32[]{:S(2)}) %collective-permute-start.4) | collective-permute-done | bytes 516128 | tf_op jit(solution)/shard_map/ppermute | solution.py:38
  86.0 1.9 collective-permute-start.5
  88.6 11.8 %collective-permute-done.5 = bf16[144,1792]{1,0:T(8,128)(2,1)S(1)} collective-permute-done((bf16[144,1792]{1,0:T(8,128)(2,1)S(1)}, bf16[144,1792]{1,0:T(8,128)(2,1)S(1)}, u32[]{:S(2)}, u32[]{:S(2)}) %collective-permute-start.5) | collective-permute-done | bytes 516128 | tf_op jit(solution)/shard_map/ppermute | solution.py:38
  101.4 0.9 fusion.55
  102.3 1.9 collective-permute-start.8
  106.1 0.9 reduce_window_sum.27
  107.3 0.9 reduce_window_sum.32
  110.4 1.4 convolution_convert_fusion
  111.8 3.3 collective-permute-start.18
  116.6 5.7 %collective-permute-done.18 = bf16[3,24,1792]{2,1,0:T(8,128)(2,1)S(1)} collective-permute-done((bf16[3,24,1792]{2,1,0:T(8,128)(2,1)S(1)}, bf16[3,24,1792]{2,1,0:T(8,128)(2,1)S(1)}, u32[]{:S(2)}, u32[]{:S(2)}) %collective-permute-start.18) | collective-permute-done | bytes 258080 | tf_op jit(solution)/shard_map/ppermute | solution.py:20
  122.4 3.7 %collective-permute-start.20 = (bf16[48,1792]{1,0:T(8,128)(2,1)S(1)}, bf16[48,1792]{1,0:T(8,128)(2,1)S(1)}, u32[]{:S(2)}, u32[]{:S(2)}) collective-permute-start(bf16[48,1792]{1,0:T(8,128)(2,1)S(1)} %get-tuple-element.34), channel_id=1, source_target_pairs={{0,16},{4,20},{8,24},{12,28},{16,32},{20,36},{24,40},{28,44},{32,0... | collective-permute-start | bytes 516104 | tf_op jit(solution)/shard_map/ppermute | solution.py:16
  126.0 6.2 %collective-permute-start.19 = (bf16[48,1792]{1,0:T(8,128)(2,1)S(1)}, bf16[48,1792]{1,0:T(8,128)(2,1)S(1)}, u32[]{:S(2)}, u32[]{:S(2)}) collective-permute-start(bf16[48,1792]{1,0:T(8,128)(2,1)S(1)} %get-tuple-element.35), channel_id=1, source_target_pairs={{0,32},{4,36},{8,40},{12,44},{16,0},{20,4},{24,8},{28,12},{32,16},... | collective-permute-start | bytes 516104 | tf_op jit(solution)/shard_map/ppermute | solution.py:16
  132.3 1.2 fusion.144
  133.5 4.9 %collective-permute-start.9 = (bf16[288,512]{1,0:T(8,128)(2,1)S(1)}, bf16[288,512]{1,0:T(8,128)(2,1)S(1)}, u32[]{:S(2)}, u32[]{:S(2)}) collective-permute-start(bf16[288,512]{1,0:T(8,128)(2,1)S(1)} %get-tuple-element.16), channel_id=1, source_target_pairs={{0,2},{2,0},{1,3},{3,1},{4,6},{6,4},{5,7},{7,5},{8,10},{10,8},{9,1... | collective-permute-start | bytes 884744 | tf_op jit(solution)/shard_map/ppermute | solution.py:20
  138.4 5.1 %collective-permute-done.20 = bf16[48,1792]{1,0:T(8,128)(2,1)S(1)} collective-permute-done((bf16[48,1792]{1,0:T(8,128)(2,1)S(1)}, bf16[48,1792]{1,0:T(8,128)(2,1)S(1)}, u32[]{:S(2)}, u32[]{:S(2)}) %collective-permute-start.20) | collective-permute-done | bytes 172064 | tf_op jit(solution)/shard_map/ppermute | solution.py:16
  143.6 4.3 %collective-permute-done.19 = bf16[48,1792]{1,0:T(8,128)(2,1)S(1)} collective-permute-done((bf16[48,1792]{1,0:T(8,128)(2,1)S(1)}, bf16[48,1792]{1,0:T(8,128)(2,1)S(1)}, u32[]{:S(2)}, u32[]{:S(2)}) %collective-permute-start.19) | collective-permute-done | bytes 172064 | tf_op jit(solution)/shard_map/ppermute | solution.py:16
  147.9 1.9 collective-permute-start.21
  150.5 1.9 collective-permute-start.10
  152.4 10.9 %collective-permute-done.21 = bf16[144,1792]{1,0:T(8,128)(2,1)S(1)} collective-permute-done((bf16[144,1792]{1,0:T(8,128)(2,1)S(1)}, bf16[144,1792]{1,0:T(8,128)(2,1)S(1)}, u32[]{:S(2)}, u32[]{:S(2)}) %collective-permute-start.21) | collective-permute-done | bytes 516128 | tf_op jit(solution)/shard_map/ppermute | solution.py:38
  163.3 4.0 %collective-permute-start.22 = (bf16[144,1792]{1,0:T(8,128)(2,1)S(1)}, bf16[144,1792]{1,0:T(8,128)(2,1)S(1)}, u32[]{:S(2)}, u32[]{:S(2)}) collective-permute-start(bf16[144,1792]{1,0:T(8,128)(2,1)S(1)} %collective-permute-done.21), channel_id=1, source_target_pairs={{0,12},{4,0},{8,4},{12,8},{1,13},{5,1},{9,5},{13,9},{2,14},{6,2},{... | collective-permute-start | bytes 1548296 | tf_op jit(solution)/shard_map/ppermute | solution.py:38
  168.3 1.9 collective-permute-start.11
  170.2 9.7 %collective-permute-done.22 = bf16[144,1792]{1,0:T(8,128)(2,1)S(1)} collective-permute-done((bf16[144,1792]{1,0:T(8,128)(2,1)S(1)}, bf16[144,1792]{1,0:T(8,128)(2,1)S(1)}, u32[]{:S(2)}, u32[]{:S(2)}) %collective-permute-start.22) | collective-permute-done | bytes 516128 | tf_op jit(solution)/shard_map/ppermute | solution.py:38
  179.9 5.8 %collective-permute-start.23 = (bf16[144,1792]{1,0:T(8,128)(2,1)S(1)}, bf16[144,1792]{1,0:T(8,128)(2,1)S(1)}, u32[]{:S(2)}, u32[]{:S(2)}) collective-permute-start(bf16[144,1792]{1,0:T(8,128)(2,1)S(1)} %collective-permute-done.22), channel_id=1, source_target_pairs={{0,12},{4,0},{8,4},{12,8},{1,13},{5,1},{9,5},{13,9},{2,14},{6,2},{... | collective-permute-start | bytes 1548296 | tf_op jit(solution)/shard_map/ppermute | solution.py:38
  186.5 4.5 %collective-permute-done.11 = bf16[144,1792]{1,0:T(8,128)(2,1)S(1)} collective-permute-done((bf16[144,1792]{1,0:T(8,128)(2,1)S(1)}, bf16[144,1792]{1,0:T(8,128)(2,1)S(1)}, u32[]{:S(2)}, u32[]{:S(2)}) %collective-permute-start.11) | collective-permute-done | bytes 516128 | tf_op jit(solution)/shard_map/ppermute | solution.py:38
  191.1 5.8 %collective-permute-start.12 = (bf16[144,1792]{1,0:T(8,128)(2,1)S(1)}, bf16[144,1792]{1,0:T(8,128)(2,1)S(1)}, u32[]{:S(2)}, u32[]{:S(2)}) collective-permute-start(bf16[144,1792]{1,0:T(8,128)(2,1)S(1)} %add.235), channel_id=1, source_target_pairs={{0,12},{4,0},{8,4},{12,8},{1,13},{5,1},{9,5},{13,9},{2,14},{6,2},{... | collective-permute-start | bytes 1548296 | tf_op jit(solution)/shard_map/ppermute | solution.py:38
  196.9 5.1 %collective-permute-done.23 = bf16[144,1792]{1,0:T(8,128)(2,1)S(1)} collective-permute-done((bf16[144,1792]{1,0:T(8,128)(2,1)S(1)}, bf16[144,1792]{1,0:T(8,128)(2,1)S(1)}, u32[]{:S(2)}, u32[]{:S(2)}) %collective-permute-start.23) | collective-permute-done | bytes 516128 | tf_op jit(solution)/shard_map/ppermute | solution.py:38
  202.5 1.9 collective-permute-start.24
  205.1 1.0 pad.4
  206.4 4.7 %collective-permute-done.12 = bf16[144,1792]{1,0:T(8,128)(2,1)S(1)} collective-permute-done((bf16[144,1792]{1,0:T(8,128)(2,1)S(1)}, bf16[144,1792]{1,0:T(8,128)(2,1)S(1)}, u32[]{:S(2)}, u32[]{:S(2)}) %collective-permute-start.12) | collective-permute-done | bytes 516128 | tf_op jit(solution)/shard_map/ppermute | solution.py:38
  211.2 6.1 %collective-permute-start.13 = (bf16[144,1792]{1,0:T(8,128)(2,1)S(1)}, bf16[144,1792]{1,0:T(8,128)(2,1)S(1)}, u32[]{:S(2)}, u32[]{:S(2)}) collective-permute-start(bf16[144,1792]{1,0:T(8,128)(2,1)S(1)} %add.236), channel_id=1, source_target_pairs={{0,12},{4,0},{8,4},{12,8},{1,13},{5,1},{9,5},{13,9},{2,14},{6,2},{... | collective-permute-start | bytes 1548296 | tf_op jit(solution)/shard_map/ppermute | solution.py:38
  217.4 4.9 %collective-permute-start.25 = (bf16[288,256]{1,0:T(8,128)(2,1)S(1)}, bf16[288,256]{1,0:T(8,128)(2,1)S(1)}, u32[]{:S(2)}, u32[]{:S(2)}) collective-permute-start(bf16[288,256]{1,0:T(8,128)(2,1)S(1)} %get-tuple-element.14), channel_id=1, source_target_pairs={{0,2},{2,0},{1,3},{3,1},{4,6},{6,4},{5,7},{7,5},{8,10},{10,8},{9,1... | collective-permute-start | bytes 442376 | tf_op jit(solution)/shard_map/ppermute | solution.py:20
  222.7 3.3 collective-permute-done.25
  226.2 1.9 collective-permute-start.26
  228.3 5.8 %collective-permute-start.15 = (bf16[2,24,1792]{2,1,0:T(8,128)(2,1)S(1)}, bf16[2,24,1792]{2,1,0:T(8,128)(2,1)S(1)}, u32[]{:S(2)}, u32[]{:S(2)}) collective-permute-start(bf16[2,24,1792]{2,1,0:T(8,128)(2,1)S(1)} %bitcast.234), channel_id=1, source_target_pairs={{0,16},{4,20},{8,24},{12,28},{16,32},{20,36},{24,40},{28,44},{32,0... | collective-permute-start | bytes 516104 | tf_op jit(solution)/shard_map/ppermute | solution.py:16
  234.1 3.9 %collective-permute-start.14 = (bf16[2,24,1792]{2,1,0:T(8,128)(2,1)S(1)}, bf16[2,24,1792]{2,1,0:T(8,128)(2,1)S(1)}, u32[]{:S(2)}, u32[]{:S(2)}) collective-permute-start(bf16[2,24,1792]{2,1,0:T(8,128)(2,1)S(1)} %bitcast.232), channel_id=1, source_target_pairs={{0,32},{4,36},{8,40},{12,44},{16,0},{20,4},{24,8},{28,12},{32,16},... | collective-permute-start | bytes 516104 | tf_op jit(solution)/shard_map/ppermute | solution.py:16
  239.6 1.9 collective-permute-start.27
  242.5 22.3 %collective-permute-done.27 = bf16[144,1792]{1,0:T(8,128)(2,1)S(1)} collective-permute-done((bf16[144,1792]{1,0:T(8,128)(2,1)S(1)}, bf16[144,1792]{1,0:T(8,128)(2,1)S(1)}, u32[]{:S(2)}, u32[]{:S(2)}) %collective-permute-start.27) | collective-permute-done | bytes 516128 | tf_op jit(solution)/shard_map/ppermute | solution.py:38
  264.9 2.1 collective-permute-start.28
  267.9 13.5 %collective-permute-done.28 = bf16[144,1792]{1,0:T(8,128)(2,1)S(1)} collective-permute-done((bf16[144,1792]{1,0:T(8,128)(2,1)S(1)}, bf16[144,1792]{1,0:T(8,128)(2,1)S(1)}, u32[]{:S(2)}, u32[]{:S(2)}) %collective-permute-start.28) | collective-permute-done | bytes 516128 | tf_op jit(solution)/shard_map/ppermute | solution.py:38
  281.5 1.9 collective-permute-start.29
  284.0 13.1 %collective-permute-done.29 = bf16[144,1792]{1,0:T(8,128)(2,1)S(1)} collective-permute-done((bf16[144,1792]{1,0:T(8,128)(2,1)S(1)}, bf16[144,1792]{1,0:T(8,128)(2,1)S(1)}, u32[]{:S(2)}, u32[]{:S(2)}) %collective-permute-start.29) | collective-permute-done | bytes 516128 | tf_op jit(solution)/shard_map/ppermute | solution.py:38
  297.3 2.6 collective-permute-start.31
  299.8 7.2 %collective-permute-start.30 = (bf16[2,24,1792]{2,1,0:T(8,128)(2,1)S(1)}, bf16[2,24,1792]{2,1,0:T(8,128)(2,1)S(1)}, u32[]{:S(2)}, u32[]{:S(2)}) collective-permute-start(bf16[2,24,1792]{2,1,0:T(8,128)(2,1)S(1)} %bitcast.238), channel_id=1, source_target_pairs={{0,32},{4,36},{8,40},{12,44},{16,0},{20,4},{24,8},{28,12},{32,16},... | collective-permute-start | bytes 516104 | tf_op jit(solution)/shard_map/ppermute | solution.py:16
  307.1 5.5 %collective-permute-start.17 = (bf16[3,24,1792]{2,1,0:T(8,128)(2,1)S(1)}, bf16[3,24,1792]{2,1,0:T(8,128)(2,1)S(1)}, u32[]{:S(2)}, u32[]{:S(2)}) collective-permute-start(bf16[3,24,1792]{2,1,0:T(8,128)(2,1)S(1)} %get-tuple-element.39), channel_id=1, source_target_pairs={{0,144},{48,96},{96,240},{144,192},{192,336},{240,288},{288,432},{... | collective-permute-start | bytes 774152 | tf_op jit(solution)/shard_map/ppermute | solution.py:176
  312.6 1.9 collective-permute-start.16
  314.6 2.0 collective-permute-done.30
  316.6 2.1 collective-permute-start.33
  319.8 2.2 collective-permute-start.32
  322.1 1.2 fusion.9
  323.2 6.5 %collective-permute-done.33 = bf16[3,24,1792]{2,1,0:T(8,128)(2,1)S(1)} collective-permute-done((bf16[3,24,1792]{2,1,0:T(8,128)(2,1)S(1)}, bf16[3,24,1792]{2,1,0:T(8,128)(2,1)S(1)}, u32[]{:S(2)}, u32[]{:S(2)}) %collective-permute-start.33) | collective-permute-done | bytes 258080 | tf_op jit(solution)/shard_map/ppermute | solution.py:176
  330.8 3.5 %collective-permute-done.32 = bf16[3,24,1792]{2,1,0:T(8,128)(2,1)S(1)} collective-permute-done((bf16[3,24,1792]{2,1,0:T(8,128)(2,1)S(1)}, bf16[3,24,1792]{2,1,0:T(8,128)(2,1)S(1)}, u32[]{:S(2)}, u32[]{:S(2)}) %collective-permute-start.32) | collective-permute-done | bytes 258080 | tf_op jit(solution)/shard_map/ppermute | solution.py:175
  334.3 1.2 fusion.10
  (140 shorter events, 25.6 us)
Async XLA Ops:
  0.6 149.2 %copy-start = (bf16[1,256,1792]{2,1,0:T(8,128)(2,1)S(1)}, bf16[1,256,1792]{2,1,0:T(8,128)(2,1)}, u32[]{:S(2)}) copy-start(bf16[1,256,1792]{2,1,0:T(8,128)(2,1)} %param.19) | copy-start | bytes 2752516
  0.8 1.1 copy-start.13
  0.8 0.7 copy-start.20
  3.4 3.7 %copy-start.11 = (bf16[1,528,2,256]{3,2,1,0:T(2,128)(2,1)S(1)}, bf16[1,528,2,256]{3,2,1,0:T(2,128)(2,1)}, u32[]{:S(2)}) copy-start(bf16[1,528,2,256]{3,2,1,0:T(2,128)(2,1)} %param.16) | copy-start | bytes 1622020
  3.5 10.0 %collective-permute-start = (bf16[3,24,1792]{2,1,0:T(8,128)(2,1)S(1)}, bf16[3,24,1792]{2,1,0:T(8,128)(2,1)S(1)}, u32[]{:S(2)}, u32[]{:S(2)}) collective-permute-start(bf16[3,24,1792]{2,1,0:T(8,128)(2,1)S(1)} %bitcast.230), channel_id=1, source_target_pairs={{0,48},{48,0},{1,49},{49,1},{2,50},{50,2},{3,51},{51,3},{4,52},{52... | collective-permute-start | bytes 774152 | tf_op jit(solution)/shard_map/ppermute | solution.py:20
  9.8 0.7 copy-start.24
  13.4 34.9 %copy-start.1 = (bf16[1,1792,256]{2,1,0:T(8,128)(2,1)S(1)}, bf16[1,1792,256]{2,1,0:T(8,128)(2,1)}, u32[]{:S(2)}) copy-start(bf16[1,1792,256]{2,1,0:T(8,128)(2,1)} %param.18) | copy-start | bytes 2752516
  13.5 16.6 %copy-start.21 = (s32[1,128,1]{1,2,0:T(1,128)S(1)}, s32[1,128,1]{1,2,0:T(1,128)}, u32[]{:S(2)}) copy-start(s32[1,128,1]{1,2,0:T(1,128)} %param.14) | copy-start | bytes 1540
  13.5 18.5 %collective-permute-start.2 = (bf16[48,1792]{1,0:T(8,128)(2,1)S(1)}, bf16[48,1792]{1,0:T(8,128)(2,1)S(1)}, u32[]{:S(2)}, u32[]{:S(2)}) collective-permute-start(bf16[48,1792]{1,0:T(8,128)(2,1)S(1)} %get-tuple-element.44), channel_id=1, source_target_pairs={{0,16},{4,20},{8,24},{12,28},{16,32},{20,36},{24,40},{28,44},{32,0... | collective-permute-start | bytes 516104 | tf_op jit(solution)/shard_map/ppermute | solution.py:16
  24.5 21.6 %collective-permute-start.1 = (bf16[48,1792]{1,0:T(8,128)(2,1)S(1)}, bf16[48,1792]{1,0:T(8,128)(2,1)S(1)}, u32[]{:S(2)}, u32[]{:S(2)}) collective-permute-start(bf16[48,1792]{1,0:T(8,128)(2,1)S(1)} %get-tuple-element.45), channel_id=1, source_target_pairs={{0,32},{4,36},{8,40},{12,44},{16,0},{20,4},{24,8},{28,12},{32,16},... | collective-permute-start | bytes 516104 | tf_op jit(solution)/shard_map/ppermute | solution.py:16
  46.2 2.4 copy-start.2
  46.2 17.8 %collective-permute-start.3 = (bf16[144,1792]{1,0:T(8,128)(2,1)S(1)}, bf16[144,1792]{1,0:T(8,128)(2,1)S(1)}, u32[]{:S(2)}, u32[]{:S(2)}) collective-permute-start(bf16[144,1792]{1,0:T(8,128)(2,1)S(1)} %bitcast.220), channel_id=1, source_target_pairs={{0,4},{4,8},{8,12},{12,0},{1,5},{5,9},{9,13},{13,1},{2,6},{6,10},{... | collective-permute-start | bytes 1548296 | tf_op jit(solution)/shard_map/ppermute | solution.py:38
  64.0 24.6 %collective-permute-start.6 = (f32[2,128]{1,0:T(2,128)S(1)}, f32[2,128]{1,0:T(2,128)S(1)}, u32[]{:S(2)}, u32[]{:S(2)}) collective-permute-start(f32[2,128]{1,0:T(2,128)S(1)} %pad_maximum_fusion.9), channel_id=1, source_target_pairs={{0,96},{96,192},{192,288},{288,384},{384,480},{480,576},{576,672},... | collective-permute-start | bytes 3080 | tf_op jit(solution)/shard_map/ppermute | solution.py:134
  68.7 19.8 %collective-permute-start.7 = (f32[128]{0:T(128)S(1)}, f32[128]{0:T(128)S(1)}, u32[]{:S(2)}, u32[]{:S(2)}) collective-permute-start(f32[128]{0:T(128)S(1)} %bitcast_convert_fusion), channel_id=1, source_target_pairs={{96,0},{192,96},{288,192},{384,288},{480,384},{576,480},{672,576},... | collective-permute-start | bytes 1544 | tf_op jit(solution)/shard_map/ppermute | solution.py:135
  70.6 15.4 %collective-permute-start.4 = (bf16[144,1792]{1,0:T(8,128)(2,1)S(1)}, bf16[144,1792]{1,0:T(8,128)(2,1)S(1)}, u32[]{:S(2)}, u32[]{:S(2)}) collective-permute-start(bf16[144,1792]{1,0:T(8,128)(2,1)S(1)} %collective-permute-done.3), channel_id=1, source_target_pairs={{0,4},{4,8},{8,12},{12,0},{1,5},{5,9},{9,13},{13,1},{2,6},{6,10},{... | collective-permute-start | bytes 1548296 | tf_op jit(solution)/shard_map/ppermute | solution.py:38
  86.0 14.4 %collective-permute-start.5 = (bf16[144,1792]{1,0:T(8,128)(2,1)S(1)}, bf16[144,1792]{1,0:T(8,128)(2,1)S(1)}, u32[]{:S(2)}, u32[]{:S(2)}) collective-permute-start(bf16[144,1792]{1,0:T(8,128)(2,1)S(1)} %collective-permute-done.4), channel_id=1, source_target_pairs={{0,4},{4,8},{8,12},{12,0},{1,5},{5,9},{9,13},{13,1},{2,6},{6,10},{... | collective-permute-start | bytes 1548296 | tf_op jit(solution)/shard_map/ppermute | solution.py:38
  88.5 12.5 %copy-start.3 = (f32[144,256]{1,0:T(8,128)}, f32[144,256]{1,0:T(8,128)S(1)}, u32[]{:S(2)}) copy-start(f32[144,256]{1,0:T(8,128)S(1)} %fusion.45) | copy-start | bytes 442372
  100.7 0.7 copy-start.5
  101.4 0.9 copy-start.7
  102.3 29.9 %collective-permute-start.8 = (f32[288,512]{1,0:T(8,128)}, f32[288,512]{1,0:T(8,128)}, u32[]{:S(2)}, u32[]{:S(2)}) collective-permute-start(f32[288,512]{1,0:T(8,128)} %fusion.55), channel_id=1, source_target_pairs={{0,1},{1,0},{2,3},{3,2},{4,5},{5,4},{6,7},{7,6},{8,9},{9,8},{10,11... | collective-permute-start | bytes 1769480 | tf_op jit(solution)/shard_map/ppermute | solution.py:20
  104.2 0.6 copy-start.22
  104.9 0.5 copy-start.17
  104.9 0.6 copy-start.14
  107.3 0.9 copy-start.12
  108.9 0.7 copy-start.18
  109.7 0.7 copy-start.23
  111.7 3.4 %copy-start.9 = (bf16[2,22,2,256]{3,1,0,2:T(8,128)(2,1)S(1)}, bf16[2,22,2,256]{3,1,0,2:T(8,128)(2,1)}, u32[]{:S(2)}) copy-start(bf16[2,22,2,256]{3,1,0,2:T(8,128)(2,1)} %get-tuple-element.69) | copy-start | bytes 135172
  111.8 10.5 %collective-permute-start.18 = (bf16[3,24,1792]{2,1,0:T(8,128)(2,1)S(1)}, bf16[3,24,1792]{2,1,0:T(8,128)(2,1)S(1)}, u32[]{:S(2)}, u32[]{:S(2)}) collective-permute-start(bf16[3,24,1792]{2,1,0:T(8,128)(2,1)S(1)} %bitcast.231), channel_id=1, source_target_pairs={{0,48},{48,0},{1,49},{49,1},{2,50},{50,2},{3,51},{51,3},{4,52},{52... | collective-permute-start | bytes 774152 | tf_op jit(solution)/shard_map/ppermute | solution.py:20
  115.2 0.8 copy-start.10
  122.3 10.0 %copy-start.4 = (f32[144,256]{1,0:T(8,128)S(1)}, f32[144,256]{1,0:T(8,128)}, u32[]{:S(2)}) copy-start(f32[144,256]{1,0:T(8,128)} %copy-done.3) | copy-start | bytes 442372
  122.3 10.0 %copy-start.6 = (f32[144,256]{1,0:T(8,128)S(1)}, f32[144,256]{1,0:T(8,128)}, u32[]{:S(2)}) copy-start(f32[144,256]{1,0:T(8,128)} %copy-done.5) | copy-start | bytes 442372
  122.3 10.0 %copy-start.8 = (f32[144,256]{1,0:T(8,128)S(1)}, f32[144,256]{1,0:T(8,128)}, u32[]{:S(2)}) copy-start(f32[144,256]{1,0:T(8,128)} %copy-done.7) | copy-start | bytes 442372
  122.4 21.2 %collective-permute-start.20 = (bf16[48,1792]{1,0:T(8,128)(2,1)S(1)}, bf16[48,1792]{1,0:T(8,128)(2,1)S(1)}, u32[]{:S(2)}, u32[]{:S(2)}) collective-permute-start(bf16[48,1792]{1,0:T(8,128)(2,1)S(1)} %get-tuple-element.34), channel_id=1, source_target_pairs={{0,16},{4,20},{8,24},{12,28},{16,32},{20,36},{24,40},{28,44},{32,0... | collective-permute-start | bytes 516104 | tf_op jit(solution)/shard_map/ppermute | solution.py:16
  126.0 21.8 %collective-permute-start.19 = (bf16[48,1792]{1,0:T(8,128)(2,1)S(1)}, bf16[48,1792]{1,0:T(8,128)(2,1)S(1)}, u32[]{:S(2)}, u32[]{:S(2)}) collective-permute-start(bf16[48,1792]{1,0:T(8,128)(2,1)S(1)} %get-tuple-element.35), channel_id=1, source_target_pairs={{0,32},{4,36},{8,40},{12,44},{16,0},{20,4},{24,8},{28,12},{32,16},... | collective-permute-start | bytes 516104 | tf_op jit(solution)/shard_map/ppermute | solution.py:16
  133.5 16.8 %collective-permute-start.9 = (bf16[288,512]{1,0:T(8,128)(2,1)S(1)}, bf16[288,512]{1,0:T(8,128)(2,1)S(1)}, u32[]{:S(2)}, u32[]{:S(2)}) collective-permute-start(bf16[288,512]{1,0:T(8,128)(2,1)S(1)} %get-tuple-element.16), channel_id=1, source_target_pairs={{0,2},{2,0},{1,3},{3,1},{4,6},{6,4},{5,7},{7,5},{8,10},{10,8},{9,1... | collective-permute-start | bytes 884744 | tf_op jit(solution)/shard_map/ppermute | solution.py:20
  147.9 15.5 %collective-permute-start.21 = (bf16[144,1792]{1,0:T(8,128)(2,1)S(1)}, bf16[144,1792]{1,0:T(8,128)(2,1)S(1)}, u32[]{:S(2)}, u32[]{:S(2)}) collective-permute-start(bf16[144,1792]{1,0:T(8,128)(2,1)S(1)} %bitcast.223), channel_id=1, source_target_pairs={{0,12},{4,0},{8,4},{12,8},{1,13},{5,1},{9,5},{13,9},{2,14},{6,2},{... | collective-permute-start | bytes 1548296 | tf_op jit(solution)/shard_map/ppermute | solution.py:38
  150.5 17.3 %collective-permute-start.10 = (bf16[288,256]{1,0:T(8,128)(2,1)S(1)}, bf16[288,256]{1,0:T(8,128)(2,1)S(1)}, u32[]{:S(2)}, u32[]{:S(2)}) collective-permute-start(bf16[288,256]{1,0:T(8,128)(2,1)S(1)} %fusion.64), channel_id=1, source_target_pairs={{0,1},{1,0},{2,3},{3,2},{4,5},{5,4},{6,7},{7,6},{8,9},{9,8},{10,11... | collective-permute-start | bytes 442376 | tf_op jit(solution)/shard_map/ppermute | solution.py:20
  163.3 16.6 %collective-permute-start.22 = (bf16[144,1792]{1,0:T(8,128)(2,1)S(1)}, bf16[144,1792]{1,0:T(8,128)(2,1)S(1)}, u32[]{:S(2)}, u32[]{:S(2)}) collective-permute-start(bf16[144,1792]{1,0:T(8,128)(2,1)S(1)} %collective-permute-done.21), channel_id=1, source_target_pairs={{0,12},{4,0},{8,4},{12,8},{1,13},{5,1},{9,5},{13,9},{2,14},{6,2},{... | collective-permute-start | bytes 1548296 | tf_op jit(solution)/shard_map/ppermute | solution.py:38
  168.3 22.7 %collective-permute-start.11 = (bf16[144,1792]{1,0:T(8,128)(2,1)S(1)}, bf16[144,1792]{1,0:T(8,128)(2,1)S(1)}, u32[]{:S(2)}, u32[]{:S(2)}) collective-permute-start(bf16[144,1792]{1,0:T(8,128)(2,1)S(1)} %convolution_convert_fusion.4), channel_id=1, source_target_pairs={{0,12},{4,0},{8,4},{12,8},{1,13},{5,1},{9,5},{13,9},{2,14},{6,2},{... | collective-permute-start | bytes 1548296 | tf_op jit(solution)/shard_map/ppermute | solution.py:38
  179.9 22.1 %collective-permute-start.23 = (bf16[144,1792]{1,0:T(8,128)(2,1)S(1)}, bf16[144,1792]{1,0:T(8,128)(2,1)S(1)}, u32[]{:S(2)}, u32[]{:S(2)}) collective-permute-start(bf16[144,1792]{1,0:T(8,128)(2,1)S(1)} %collective-permute-done.22), channel_id=1, source_target_pairs={{0,12},{4,0},{8,4},{12,8},{1,13},{5,1},{9,5},{13,9},{2,14},{6,2},{... | collective-permute-start | bytes 1548296 | tf_op jit(solution)/shard_map/ppermute | solution.py:38
  191.1 20.0 %collective-permute-start.12 = (bf16[144,1792]{1,0:T(8,128)(2,1)S(1)}, bf16[144,1792]{1,0:T(8,128)(2,1)S(1)}, u32[]{:S(2)}, u32[]{:S(2)}) collective-permute-start(bf16[144,1792]{1,0:T(8,128)(2,1)S(1)} %add.235), channel_id=1, source_target_pairs={{0,12},{4,0},{8,4},{12,8},{1,13},{5,1},{9,5},{13,9},{2,14},{6,2},{... | collective-permute-start | bytes 1548296 | tf_op jit(solution)/shard_map/ppermute | solution.py:38
  202.5 14.8 %collective-permute-start.24 = (f32[288,256]{1,0:T(8,128)S(1)}, f32[288,256]{1,0:T(8,128)S(1)}, u32[]{:S(2)}, u32[]{:S(2)}) collective-permute-start(f32[288,256]{1,0:T(8,128)S(1)} %fusion.66), channel_id=1, source_target_pairs={{0,1},{1,0},{2,3},{3,2},{4,5},{5,4},{6,7},{7,6},{8,9},{9,8},{10,11... | collective-permute-start | bytes 884744 | tf_op jit(solution)/shard_map/ppermute | solution.py:20
  211.2 16.9 %collective-permute-start.13 = (bf16[144,1792]{1,0:T(8,128)(2,1)S(1)}, bf16[144,1792]{1,0:T(8,128)(2,1)S(1)}, u32[]{:S(2)}, u32[]{:S(2)}) collective-permute-start(bf16[144,1792]{1,0:T(8,128)(2,1)S(1)} %add.236), channel_id=1, source_target_pairs={{0,12},{4,0},{8,4},{12,8},{1,13},{5,1},{9,5},{13,9},{2,14},{6,2},{... | collective-permute-start | bytes 1548296 | tf_op jit(solution)/shard_map/ppermute | solution.py:38
  217.4 8.5 %collective-permute-start.25 = (bf16[288,256]{1,0:T(8,128)(2,1)S(1)}, bf16[288,256]{1,0:T(8,128)(2,1)S(1)}, u32[]{:S(2)}, u32[]{:S(2)}) collective-permute-start(bf16[288,256]{1,0:T(8,128)(2,1)S(1)} %get-tuple-element.14), channel_id=1, source_target_pairs={{0,2},{2,0},{1,3},{3,1},{4,6},{6,4},{5,7},{7,5},{8,10},{10,8},{9,1... | collective-permute-start | bytes 442376 | tf_op jit(solution)/shard_map/ppermute | solution.py:20
  226.2 11.9 %collective-permute-start.26 = (bf16[288,512]{1,0:T(8,128)(2,1)S(1)}, bf16[288,512]{1,0:T(8,128)(2,1)S(1)}, u32[]{:S(2)}, u32[]{:S(2)}) collective-permute-start(bf16[288,512]{1,0:T(8,128)(2,1)S(1)} %pad_maximum_fusion.6), channel_id=1, source_target_pairs={{0,1},{1,0},{2,3},{3,2},{4,5},{5,4},{6,7},{7,6},{8,9},{9,8},{10,11... | collective-permute-start | bytes 884744 | tf_op jit(solution)/shard_map/ppermute | solution.py:20
  228.3 55.6 %collective-permute-start.15 = (bf16[2,24,1792]{2,1,0:T(8,128)(2,1)S(1)}, bf16[2,24,1792]{2,1,0:T(8,128)(2,1)S(1)}, u32[]{:S(2)}, u32[]{:S(2)}) collective-permute-start(bf16[2,24,1792]{2,1,0:T(8,128)(2,1)S(1)} %bitcast.234), channel_id=1, source_target_pairs={{0,16},{4,20},{8,24},{12,28},{16,32},{20,36},{24,40},{28,44},{32,0... | collective-permute-start | bytes 516104 | tf_op jit(solution)/shard_map/ppermute | solution.py:16
  234.1 49.8 %collective-permute-start.14 = (bf16[2,24,1792]{2,1,0:T(8,128)(2,1)S(1)}, bf16[2,24,1792]{2,1,0:T(8,128)(2,1)S(1)}, u32[]{:S(2)}, u32[]{:S(2)}) collective-permute-start(bf16[2,24,1792]{2,1,0:T(8,128)(2,1)S(1)} %bitcast.232), channel_id=1, source_target_pairs={{0,32},{4,36},{8,40},{12,44},{16,0},{20,4},{24,8},{28,12},{32,16},... | collective-permute-start | bytes 516104 | tf_op jit(solution)/shard_map/ppermute | solution.py:16
  239.6 25.1 %collective-permute-start.27 = (bf16[144,1792]{1,0:T(8,128)(2,1)S(1)}, bf16[144,1792]{1,0:T(8,128)(2,1)S(1)}, u32[]{:S(2)}, u32[]{:S(2)}) collective-permute-start(bf16[144,1792]{1,0:T(8,128)(2,1)S(1)} %fusion.3), channel_id=1, source_target_pairs={{0,4},{4,8},{8,12},{12,0},{1,5},{5,9},{9,13},{13,1},{2,6},{6,10},{... | collective-permute-start | bytes 1548296 | tf_op jit(solution)/shard_map/ppermute | solution.py:38
  264.9 16.5 %collective-permute-start.28 = (bf16[144,1792]{1,0:T(8,128)(2,1)S(1)}, bf16[144,1792]{1,0:T(8,128)(2,1)S(1)}, u32[]{:S(2)}, u32[]{:S(2)}) collective-permute-start(bf16[144,1792]{1,0:T(8,128)(2,1)S(1)} %add.253), channel_id=1, source_target_pairs={{0,4},{4,8},{8,12},{12,0},{1,5},{5,9},{9,13},{13,1},{2,6},{6,10},{... | collective-permute-start | bytes 1548296 | tf_op jit(solution)/shard_map/ppermute | solution.py:38
  281.5 15.6 %collective-permute-start.29 = (bf16[144,1792]{1,0:T(8,128)(2,1)S(1)}, bf16[144,1792]{1,0:T(8,128)(2,1)S(1)}, u32[]{:S(2)}, u32[]{:S(2)}) collective-permute-start(bf16[144,1792]{1,0:T(8,128)(2,1)S(1)} %add.255), channel_id=1, source_target_pairs={{0,4},{4,8},{8,12},{12,0},{1,5},{5,9},{9,13},{13,1},{2,6},{6,10},{... | collective-permute-start | bytes 1548296 | tf_op jit(solution)/shard_map/ppermute | solution.py:38
  297.3 17.3 %collective-permute-start.31 = (bf16[2,24,1792]{2,1,0:T(8,128)(2,1)S(1)}, bf16[2,24,1792]{2,1,0:T(8,128)(2,1)S(1)}, u32[]{:S(2)}, u32[]{:S(2)}) collective-permute-start(bf16[2,24,1792]{2,1,0:T(8,128)(2,1)S(1)} %bitcast.240), channel_id=1, source_target_pairs={{0,16},{4,20},{8,24},{12,28},{16,32},{20,36},{24,40},{28,44},{32,0... | collective-permute-start | bytes 516104 | tf_op jit(solution)/shard_map/ppermute | solution.py:16
  299.8 16.7 %collective-permute-start.30 = (bf16[2,24,1792]{2,1,0:T(8,128)(2,1)S(1)}, bf16[2,24,1792]{2,1,0:T(8,128)(2,1)S(1)}, u32[]{:S(2)}, u32[]{:S(2)}) collective-permute-start(bf16[2,24,1792]{2,1,0:T(8,128)(2,1)S(1)} %bitcast.238), channel_id=1, source_target_pairs={{0,32},{4,36},{8,40},{12,44},{16,0},{20,4},{24,8},{28,12},{32,16},... | collective-permute-start | bytes 516104 | tf_op jit(solution)/shard_map/ppermute | solution.py:16
  307.1 11.7 %collective-permute-start.17 = (bf16[3,24,1792]{2,1,0:T(8,128)(2,1)S(1)}, bf16[3,24,1792]{2,1,0:T(8,128)(2,1)S(1)}, u32[]{:S(2)}, u32[]{:S(2)}) collective-permute-start(bf16[3,24,1792]{2,1,0:T(8,128)(2,1)S(1)} %get-tuple-element.39), channel_id=1, source_target_pairs={{0,144},{48,96},{96,240},{144,192},{192,336},{240,288},{288,432},{... | collective-permute-start | bytes 774152 | tf_op jit(solution)/shard_map/ppermute | solution.py:176
  312.6 9.4 %collective-permute-start.16 = (bf16[3,24,1792]{2,1,0:T(8,128)(2,1)S(1)}, bf16[3,24,1792]{2,1,0:T(8,128)(2,1)S(1)}, u32[]{:S(2)}, u32[]{:S(2)}) collective-permute-start(bf16[3,24,1792]{2,1,0:T(8,128)(2,1)S(1)} %get-tuple-element.38), channel_id=1, source_target_pairs={{0,96},{96,192},{192,288},{288,384},{384,480},{480,576},{576,672},... | collective-permute-start | bytes 774152 | tf_op jit(solution)/shard_map/ppermute | solution.py:175
  316.6 13.1 %collective-permute-start.33 = (bf16[3,24,1792]{2,1,0:T(8,128)(2,1)S(1)}, bf16[3,24,1792]{2,1,0:T(8,128)(2,1)S(1)}, u32[]{:S(2)}, u32[]{:S(2)}) collective-permute-start(bf16[3,24,1792]{2,1,0:T(8,128)(2,1)S(1)} %get-tuple-element.29), channel_id=1, source_target_pairs={{96,48},{144,0},{192,144},{240,96},{288,240},{336,192},{384,336},{... | collective-permute-start | bytes 774152 | tf_op jit(solution)/shard_map/ppermute | solution.py:176
  318.8 0.7 copy-start.15
  319.8 2.2 copy-start.19
  319.8 14.4 %collective-permute-start.32 = (bf16[3,24,1792]{2,1,0:T(8,128)(2,1)S(1)}, bf16[3,24,1792]{2,1,0:T(8,128)(2,1)S(1)}, u32[]{:S(2)}, u32[]{:S(2)}) collective-permute-start(bf16[3,24,1792]{2,1,0:T(8,128)(2,1)S(1)} %get-tuple-element.28), channel_id=1, source_target_pairs={{96,0},{192,96},{288,192},{384,288},{480,384},{576,480},{672,576},... | collective-permute-start | bytes 774152 | tf_op jit(solution)/shard_map/ppermute | solution.py:175
  329.7 0.7 copy-start.16
